TPU v7x, 32 devices: a whole 2x2x4 slice. The times are simulated.
32 devices in a mesh: dp: 4 (over y, core), tensor: 8 (over z, x).
Axes of the slice: x: 2, y: 2, z: 4, core: 2. Of those that a mesh axis runs over, the one named last changes fastest.
Arguments:
- gate_pre: bfloat16 [28, 512, 4096], P(None, 'tensor', 'dp'), parts along dimension 2, may hold values from -6 to 6
- up_pre: bfloat16 [28, 512, 4096], P(None, 'tensor', 'dp'), parts along dimension 2, may hold values from -6 to 6
- down_weight: bfloat16 [28, 512, 4096], P(None, 'tensor'), may hold values from -0.0625 to 0.0625
Outputs:
- mixed: bfloat16 [4096, 4096], P('tensor', 'dp'), parts along dimension 1
There are 4 independent parts, one for each index of `dp`. A program takes and returns all parts, laid end to end along the dimension named above; an argument that names none is the same for every part. Nothing has to cross between parts.
All inputs are finite; a program needn't handle non-finite values.
Results may differ from a plain program's by a relative error of at most 0.024.
Values may be sent and summed in bfloat16 or wider, within the bound.
No kernel may reach another device: no remote copies, remote signals or barrier semaphores. Data moves between devices by JAX's collectives and lax.ppermute only.
A program may use at most 128 MiB of HBM per device.

v0:
```python
import math

import jax
import jax.numpy as jnp
import numpy as np
from jax import lax
from jax.sharding import PartitionSpec as P


def partner_2(value, axis, distance):
    mask = 2**distance
    pairs = [(source, source ^ mask) for source in range(lax.axis_size(axis))]
    return lax.ppermute(value, axis, pairs)


def character(value, prime_order):
    residue = value % prime_order
    if residue == 0:
        return 0
    squares_list = [index * index % prime_order for index in range(1, prime_order)]
    return 1 if residue in squares_list else -1


def paley_matrix():
    prime_order = 13
    conference = np.zeros((14, 14))
    conference[0, 1:] = 1.0
    conference[1:, 0] = 1.0
    for row_index in range(prime_order):
        for col_index in range(prime_order):
            conference[row_index + 1, col_index + 1] = character(col_index - row_index, prime_order)
    first = np.array([[1.0, 1.0], [1.0, -1.0]])
    second = np.array([[1.0, -1.0], [-1.0, -1.0]])
    return np.kron(conference, first) + np.kron(np.eye(14), second)


def sylvester(order):
    matrix = np.ones((1, 1))
    basic = np.array([[1.0, 1.0], [1.0, -1.0]])
    while matrix.shape[0] < order:
        matrix = np.kron(basic, matrix)
    return matrix


def both_factors(values, left_factor, right_factor):
    values = jnp.einsum(
        "ij,jbt->ibt", left_factor, values.astype(jnp.float32), precision=lax.Precision.DEFAULT
    )
    return jnp.einsum("bc,act->abt", right_factor, values, precision=lax.Precision.HIGH)


def body(gate_pre, up_pre, down_weight):
    hidden = (jax.nn.silu(gate_pre.astype(jnp.float32)) * up_pre.astype(jnp.float32)).astype(
        jnp.bfloat16
    )
    devices = lax.axis_size("tensor")
    left_factor = jnp.asarray(paley_matrix(), jnp.float32)
    local_width = hidden.shape[1]
    inner_factor = jnp.asarray(sylvester(local_width), jnp.float32)
    current = both_factors(hidden, left_factor, inner_factor)
    position = lax.axis_index("tensor")
    for bit_level in range(devices.bit_length() - 1):
        partner = partner_2(current.astype(jnp.bfloat16), "tensor", bit_level).astype(current.dtype)
        parity = position // 2**bit_level % 2
        flip_sign = (1 - 2 * parity).astype(jnp.float32)
        current = partner + flip_sign * current
    rotated = (current * (1.0 / math.sqrt(hidden.shape[0] * devices * local_width))).astype(
        jnp.bfloat16
    )
    return lax.psum_scatter(
        lax.dot_general(
            down_weight, rotated, (((0, 1), (0, 1)), ((), ())), preferred_element_type=jnp.float32
        ).astype(jnp.bfloat16),
        "tensor",
        scatter_dimension=0,
        tiled=True,
    )


def solution(mesh):
    in_specs = (P(None, "tensor", "dp"), P(None, "tensor", "dp"), P(None, "tensor", None))
    out_specs = P("tensor", "dp")
    return jax.shard_map(body, mesh=mesh, in_specs=in_specs, out_specs=out_specs, check_vma=False)
```

profile of v0, /device:TPU:0, one launch (start us, length us, event | category | flops | bytes accessed | tf_op | source)
XLA Modules:
  0.0 557.3 jit_solution(3754877688352205837)
XLA Ops:
  6.5 0.0 copy-start.2
  6.5 0.0 reduce-scatter.2.cloned.1.call-start
  6.5 4.4 fusion.6
  11.0 0.0 copy-done.2
  11.0 0.0 copy-start.1
  11.0 5.1 fusion.9
  16.1 0.0 copy-done.1
  16.1 9.0 %fusion.4 = f32[28,1024,64]{1,2,0:T(8,128)S(1)} fusion(f32[64,64,1]{1,0,2:T(8,128)S(1)} %copy-done.1, f32[28,64,1024]{2,0,1:T(8,128)S(1)} %fusion.9), kind=kOutput, calls=%fused_computation.8 | convolution fusion | flops 704643072 | bytes 14696448 | tf_op jit(solution)/shard_map/bc,act->abt/dot_general | solution.py:49
  25.2 0.0 copy-start
  25.2 3.0 copy-done
  28.1 2.4 convert_bitcast_fusion
  30.5 2.9 collective-permute-start
  33.4 79.7 %collective-permute-done = bf16[28,64,1024]{2,1,0:T(8,128)(2,1)} collective-permute-done((bf16[28,64,1024]{2,1,0:T(8,128)(2,1)}, bf16[28,64,1024]{2,1,0:T(8,128)(2,1)}, u32[]{:S(2)}, u32[]{:S(2)}) %collective-permute-start) | collective-permute-done | bytes 3670048 | tf_op jit(solution)/shard_map/ppermute | solution.py:13
  113.1 7.3 %fusion.14 = bf16[28,64,1024]{2,1,0:T(8,128)(2,1)} fusion(f32[28,1024,64]{1,2,0:T(8,128)} %copy-done, f32[]{:T(128)S(6)} %convert_element_type.55, bf16[28,64,1024]{2,1,0:T(8,128)(2,1)} %collective-permute-done), kind=kLoop, calls=%fused_computation.21 | loop fusion | flops 7340032 | bytes 14680068 | tf_op jit(solution)/shard_map/convert_element_type | solution.py:63
  120.4 1.8 collective-permute-start.1
  122.2 79.0 %collective-permute-done.1 = bf16[28,64,1024]{2,1,0:T(8,128)(2,1)} collective-permute-done((bf16[28,64,1024]{2,1,0:T(8,128)(2,1)}, bf16[28,64,1024]{2,1,0:T(8,128)(2,1)}, u32[]{:S(2)}, u32[]{:S(2)}) %collective-permute-start.1) | collective-permute-done | bytes 3670048 | tf_op jit(solution)/shard_map/ppermute | solution.py:13
  201.2 9.3 %fusion.8 = bf16[28,64,1024]{2,1,0:T(8,128)(2,1)} fusion(bf16[28,64,1024]{2,1,0:T(8,128)(2,1)} %collective-permute-done.1, f32[]{:T(128)S(6)} %convert_element_type.58, f32[28,1024,64]{1,2,0:T(8,128)} %copy-done, f32[]{:T(128)S(6)} %convert_element_type.55, bf16[28,64,1024]{2,1,0:T(8,128)(2,1)} %collective-permute-done), kind=kLoop, calls=%fused_computation.14 | loop fusion | flops 12845056 | bytes 18350088 | tf_op jit(solution)/shard_map/convert_element_type | solution.py:63
  210.5 2.5 collective-permute-start.2
  213.0 157.0 %collective-permute-done.2 = bf16[28,64,1024]{2,1,0:T(8,128)(2,1)} collective-permute-done((bf16[28,64,1024]{2,1,0:T(8,128)(2,1)}, bf16[28,64,1024]{2,1,0:T(8,128)(2,1)}, u32[]{:S(2)}, u32[]{:S(2)}) %collective-permute-start.2) | collective-permute-done | bytes 3670048 | tf_op jit(solution)/shard_map/ppermute | solution.py:13
  370.0 27.8 %fusion.7 = bf16[4096,1024]{0,1:T(8,128)(2,1)} fusion(bf16[28,64,4096]{2,1,0:T(8,128)(2,1)} %param.7, bf16[28,64,1024]{2,1,0:T(8,128)(2,1)} %collective-permute-done.2, bf16[28,64,1024]{2,1,0:T(8,128)(2,1)} %collective-permute-done.1, f32[]{:T(128)S(6)} %convert_element_type.61, f32[]{:T(128)S(6)} %convert_element_type.58, f32[28,1024,64]{1,2,0:T(8,128)} %copy-done, ...), kind=kOutput, calls=%fused_computation.13 | convolution fusion | flops 15056764928 | bytes 41418764 | tf_op jit(solution)/shard_map/dot_general | solution.py:71
  397.8 0.0 reduce-scatter.2.cloned.1.call-update
  397.8 150.3 %reduce-scatter.2.cloned.1.call-done = bf16[512,1024]{0,1:T(8,128)(2,1)} async-done(((bf16[4096,1024]{0,1:T(8,128)(2,1)}), bf16[512,1024]{0,1:T(8,128)(2,1)}) %reduce-scatter.2.cloned.1.call-update) | async-done | bytes 1048592 | tf_op jit(solution)/shard_map/reduce_scatter | solution.py:70
  548.2 2.3 copy.6
Async XLA Ops:
  6.5 4.4 copy-start.2
  6.5 541.6 %reduce-scatter.2.cloned.1.call-start = ((), (), s32[]{:S(2)}) async-start(), calls=%async_computation.1 | async-start | bytes 9437184 | tf_op jit(solution)/shard_map/reduce_scatter | solution.py:70
  11.0 5.1 copy-start.1
  25.2 3.0 copy-start
  30.5 82.6 %collective-permute-start = (bf16[28,64,1024]{2,1,0:T(8,128)(2,1)}, bf16[28,64,1024]{2,1,0:T(8,128)(2,1)}, u32[]{:S(2)}, u32[]{:S(2)}) collective-permute-start(bf16[28,64,1024]{2,1,0:T(8,128)(2,1)} %convert_bitcast_fusion), channel_id=1, source_target_pairs={{0,1},{1,0},{2,3},{3,2},{4,5},{5,4},{6,7},{7,6},{8,9},{9,8},{10,11... | collective-permute-start | bytes 11010056 | tf_op jit(solution)/shard_map/ppermute | solution.py:13
  120.4 80.8 %collective-permute-start.1 = (bf16[28,64,1024]{2,1,0:T(8,128)(2,1)}, bf16[28,64,1024]{2,1,0:T(8,128)(2,1)}, u32[]{:S(2)}, u32[]{:S(2)}) collective-permute-start(bf16[28,64,1024]{2,1,0:T(8,128)(2,1)} %fusion.14), channel_id=1, source_target_pairs={{0,2},{1,3},{2,0},{3,1},{4,6},{5,7},{6,4},{7,5},{8,10},{9,11},{10,... | collective-permute-start | bytes 11010056 | tf_op jit(solution)/shard_map/ppermute | solution.py:13
  210.5 159.5 %collective-permute-start.2 = (bf16[28,64,1024]{2,1,0:T(8,128)(2,1)}, bf16[28,64,1024]{2,1,0:T(8,128)(2,1)}, u32[]{:S(2)}, u32[]{:S(2)}) collective-permute-start(bf16[28,64,1024]{2,1,0:T(8,128)(2,1)} %fusion.8), channel_id=1, source_target_pairs={{0,4},{1,5},{2,6},{3,7},{4,0},{5,1},{6,2},{7,3},{8,12},{9,13},{10,... | collective-permute-start | bytes 11010056 | tf_op jit(solution)/shard_map/ppermute | solution.py:13
Sparse Core Ops, SparseCore 0:
  397.9 150.1 reduce-scatter.1
where the time goes:
time: 557 us
  waiting for transfers between devices  466 us (84%)
  matrix products  42 us (8%)
  other arithmetic  23.4 us (4%)
  between operations  13.4 us (2%)
  starting transfers between devices  7.26 us (1%)
    ppermute x3, waiting for transfers between devices, partner_2(): return lax.ppermute(value, axis, pairs)  316 us
    reduce_scatter x1, waiting for transfers between devices, body(): lax.psum_scatter(lax.dot_general(down_weight, rotated, (((0, 1), (0, 1)),...  150 us
    dot_general x1, matrix products, body(): lax.dot_general(down_weight, rotated, (((0, 1), (0, 1)), ((), ())), prefe...  27.8 us
    convert_element_type x3, other arithmetic, body(): current.astype(jnp.bfloat16)  18.9 us
  transfers between devices with their start and end apart: 4, of which 4 were waited for; matrix products, arithmetic and copies ran while one was open for 0% of the time, Pallas kernels for 0%

commit v1 on v0

v1 whole, which is shorter than its diff:
```python
import functools
import math

import jax
import jax.numpy as jnp
import numpy as np
from jax import lax
from jax.experimental import pallas as pl
from jax.experimental.pallas import tpu as pltpu
from jax.sharding import PartitionSpec as P

CHUNKS = 8
VMEM = 48 * 1024 * 1024
ORDER = (1, 2, 3, 4, 5, 6, 0)


def character(value, prime_order):
    residue = value % prime_order
    if residue == 0:
        return 0
    squares_list = [index * index % prime_order for index in range(1, prime_order)]
    return 1 if residue in squares_list else -1


def paley_matrix():
    prime_order = 13
    conference = np.zeros((14, 14))
    conference[0, 1:] = 1.0
    conference[1:, 0] = 1.0
    for row_index in range(prime_order):
        for col_index in range(prime_order):
            conference[row_index + 1, col_index + 1] = character(col_index - row_index, prime_order)
    first = np.array([[1.0, 1.0], [1.0, -1.0]])
    second = np.array([[1.0, -1.0], [-1.0, -1.0]])
    return np.kron(conference, first) + np.kron(np.eye(14), second)


def sylvester(order):
    matrix = np.ones((1, 1))
    basic = np.array([[1.0, 1.0], [1.0, -1.0]])
    while matrix.shape[0] < order:
        matrix = np.kron(basic, matrix)
    return matrix


def exchange(value, bit):
    pairs = [(source, source ^ (1 << bit)) for source in range(lax.axis_size("tensor"))]
    return lax.ppermute(value, "tensor", pairs)


def call(kernel, after, operands, specs, outs, out_specs, grid, flops, scratch=()):
    moved = sum(int(np.prod(x.shape)) * x.dtype.itemsize for x in (*operands, *outs))

    def run(_, *refs):
        kernel(*refs)

    return pl.pallas_call(
        run,
        out_shape=outs,
        grid=grid,
        in_specs=[pl.BlockSpec(memory_space=pl.ANY), *specs],
        out_specs=out_specs,
        scratch_shapes=list(scratch),
        compiler_params=pltpu.CompilerParams(vmem_limit_bytes=VMEM),
        cost_estimate=pl.CostEstimate(flops=flops, bytes_accessed=moved, transcendentals=0),
    )(after, *operands)


def bf16(*shape):
    return jax.ShapeDtypeStruct(shape, jnp.bfloat16)


def rows_spec(rows, step, offset=0):
    return pl.BlockSpec((rows, step), lambda i: (i + offset, 0))


SCALAR = pl.BlockSpec(memory_space=pltpu.SMEM)


def activate(after, gate, up, chunk, step):
    units = gate.shape[0]
    blocks = 4

    def kernel(gate_ref, up_ref, out_ref):
        g = gate_ref[...].astype(jnp.float32)
        u = up_ref[...].astype(jnp.float32)
        out_ref[...] = (g / (1.0 + jnp.exp(-g)) * u).astype(jnp.bfloat16)

    spec = pl.BlockSpec((units // blocks, step), lambda i: (i, chunk))
    return call(
        kernel, after, (gate, up), [spec, spec], [bf16(units, step)],
        [rows_spec(units // blocks, step)], (blocks,), 0,
    )[0]


def mix(after, partner, own, sign):
    units, step = own.shape
    blocks = 2

    def kernel(partner_ref, own_ref, sign_ref, out_ref):
        total = partner_ref[...].astype(jnp.float32) + sign_ref[0] * own_ref[...].astype(jnp.float32)
        out_ref[...] = total.astype(jnp.bfloat16)

    spec = rows_spec(units // blocks, step)
    return call(
        kernel, after, (partner, own, sign), [spec, spec, SCALAR], [bf16(units, step)],
        [spec], (blocks,), 0,
    )[0]


def fold_weight(after, weight, factor, block_of, scale, first, count, devices):
    units, features = weight.shape
    rows = features // devices

    def kernel(block_ref, _, weight_ref, factor_ref, out_ref):
        product = lax.dot_general(
            weight_ref[...], factor_ref[...], (((0,), (0,)), ((), ())),
            preferred_element_type=jnp.float32,
        )
        out_ref[...] = (product * scale).astype(jnp.bfloat16)

    return pl.pallas_call(
        kernel,
        out_shape=bf16(count * rows, units),
        grid_spec=pltpu.PrefetchScalarGridSpec(
            num_scalar_prefetch=1,
            grid=(count,),
            in_specs=[
                pl.BlockSpec(memory_space=pl.ANY),
                pl.BlockSpec((units, rows), lambda i, block: (0, block[first + i])),
                pl.BlockSpec((units, units), lambda i, block: (0, 0)),
            ],
            out_specs=pl.BlockSpec((rows, units), lambda i, block: (i, 0)),
        ),
        compiler_params=pltpu.CompilerParams(vmem_limit_bytes=VMEM),
        cost_estimate=pl.CostEstimate(
            flops=2 * count * rows * units * units,
            bytes_accessed=2 * units * (2 * count * rows + units),
            transcendentals=0,
        ),
    )(block_of, after, weight, factor)


def project(after, partner, own, sign, given_weight, kept_weight):
    units, step = own.shape
    half = given_weight.shape[0]
    blocks = 4
    rows = half // blocks

    def kernel(partner_ref, own_ref, sign_ref, given_w, kept_w, given_ref, kept_ref, mixed):
        index = pl.program_id(0)

        @pl.when(index == 0)
        def _():
            total = partner_ref[...].astype(jnp.float32) + sign_ref[0] * own_ref[...].astype(jnp.float32)
            mixed[...] = total.astype(jnp.bfloat16)

        @pl.when(index < blocks)
        def _():
            given_ref[...] = jnp.dot(
                given_w[...], mixed[...], preferred_element_type=jnp.float32
            ).astype(jnp.bfloat16)

        @pl.when(index >= blocks)
        def _():
            kept_ref[...] = jnp.dot(
                kept_w[...], mixed[...], preferred_element_type=jnp.float32
            ).astype(jnp.bfloat16)

    whole = pl.BlockSpec((units, step), lambda i: (0, 0))
    early = lambda i: (jnp.minimum(i, blocks - 1), 0)
    late = lambda i: (jnp.maximum(i - blocks, 0), 0)
    return call(
        kernel, after, (partner, own, sign, given_weight, kept_weight),
        [whole, whole, SCALAR, pl.BlockSpec((rows, units), early), pl.BlockSpec((rows, units), late)],
        [bf16(half, step), bf16(half, step)],
        [pl.BlockSpec((rows, step), early), pl.BlockSpec((rows, step), late)],
        (2 * blocks,), 4 * half * units * step, [pltpu.VMEM((units, step), jnp.bfloat16)],
    )


def add(after, taken, kept):
    rows, step = kept.shape

    def kernel(taken_ref, kept_ref, out_ref):
        total = taken_ref[...].astype(jnp.float32) + kept_ref[...].astype(jnp.float32)
        out_ref[...] = total.astype(jnp.bfloat16)

    spec = rows_spec(rows, step)
    return call(kernel, after, (taken, kept), [spec, spec], [bf16(rows, step)], [spec], (1,), 0)[0]


def add_split(after, taken, kept):
    rows, step = kept.shape
    half = rows // 2

    def kernel(taken_ref, kept_ref, given_ref, kept_out):
        total = taken_ref[...].astype(jnp.float32) + kept_ref[...].astype(jnp.float32)
        total = total.astype(jnp.bfloat16)
        kept_out[...] = total[:half]
        given_ref[...] = total[half:]

    spec = rows_spec(rows, step)
    out = rows_spec(half, step)
    return call(
        kernel, after, (taken, kept), [spec, spec], [bf16(half, step)] * 2, [out, out], (1,), 0
    )


def body(gate_pre, up_pre, down_weight):
    left, width, tokens = gate_pre.shape
    units = left * width
    features = down_weight.shape[-1]
    devices = lax.axis_size("tensor")
    levels = devices.bit_length() - 1
    position = lax.axis_index("tensor")
    signs = [
        (1 - 2 * ((position >> level) & 1)).astype(jnp.float32).reshape(1) for level in range(levels)
    ]
    scale = 1.0 / math.sqrt(units * devices)
    factor = jnp.asarray(np.kron(paley_matrix(), sylvester(width)), jnp.bfloat16)
    weight = down_weight.reshape(units, features)
    gate = gate_pre.reshape(units, tokens)
    up = up_pre.reshape(units, tokens)
    step = tokens // CHUNKS

    order = sorted(
        range(devices),
        key=lambda r: (1 - (r & 1), *[(r >> level) & 1 for level in range(1, levels)]),
    )
    block_of = jnp.asarray(order, jnp.int32) ^ position

    last = [gate]
    folded = []
    half = devices // 2

    def fold(part):
        parts = 4 if devices >= 8 else 2
        count = devices // parts
        made = fold_weight(
            last[0], weight, factor, block_of, scale, part * count, count, devices
        )
        last[0] = made
        folded.append(made)

    state = [None] * CHUNKS
    outs = [None] * CHUNKS
    stages = 2 * levels + 1

    def weights():
        if len(folded) != 2:
            both = [jnp.concatenate(folded[:2]), jnp.concatenate(folded[2:])]
            folded[:] = both
        return folded

    def run(stage, chunk):
        if stage == 0:
            made = activate(last[0], gate, up, chunk, step)
            last[0] = made
            state[chunk] = (exchange(made, 0), made)
            return
        partner, own = state[chunk]
        if stage < levels:
            made = mix(last[0], partner, own, signs[stage - 1])
            last[0] = made
            state[chunk] = (exchange(made, stage), made)
        elif stage == levels:
            given, kept = project(last[0], partner, own, signs[stage - 1], *weights())
            last[0] = kept
            state[chunk] = (exchange(given, 0), kept)
        elif stage < 2 * levels:
            given, kept = add_split(last[0], partner, own)
            last[0] = kept
            state[chunk] = (exchange(given, stage - levels), kept)
        else:
            outs[chunk] = last[0] = add(last[0], partner, own)

    run(0, 0)
    fold(0)
    run(0, 1)
    for turn in range(1, CHUNKS + stages):
        for stage in range(1, stages):
            chunk = turn - stage
            if 0 <= chunk < CHUNKS:
                run(stage, chunk)
        if turn + 1 < CHUNKS:
            run(0, turn + 1)
        if len(folded) < 4 and turn < levels:
            fold(len(folded))
            if turn == levels - 1:
                while len(folded) < 4:
                    fold(len(folded))
    return jnp.concatenate(outs, axis=1)


def solution(mesh):
    in_specs = (P(None, "tensor", "dp"), P(None, "tensor", "dp"), P(None, "tensor", None))
    out_specs = P("tensor", "dp")
    return jax.shard_map(body, mesh=mesh, in_specs=in_specs, out_specs=out_specs, check_vma=False)
```

time: 557 us -> 319 us (0.57)
  waiting for transfers between devices: 466 us -> 74.5 us
  Pallas kernels: 0 us -> 154 us
  starting transfers between devices: 7.26 us -> 60.6 us
  matrix products: 42 us -> 0 us
  between operations: 13.4 us -> 0.72 us
  other arithmetic: 23.4 us -> 13.4 us
  local copies, waits for them, and re-layouts: 5.25 us -> 14.1 us
    ppermute x3 -> x48, waiting for transfers between devices: 316 us -> 74.5 us  [exchange(): return lax.ppermute(value, 'tensor', pairs)]
    pallas_call x0 -> x60, Pallas kernels: none -> 154 us  [the longest x56 110 us: call(): pl.pallas_call(run, out_shape=outs, grid=grid, in_specs=[pl.BlockSpec(mem...]
    reduce_scatter x1 -> x0, waiting for transfers between devices: 150 us -> none  [body(): lax.psum_scatter(lax.dot_general(down_weight, rotated, (((0, 1), (0, 1)),...]
    ppermute x3 -> x48, starting transfers between devices: 7.26 us -> 60.6 us  [exchange(): return lax.ppermute(value, 'tensor', pairs)]
    dot_general x3 -> x0, matrix products: 42 us -> none  [the longest x1 27.8 us: body(): lax.dot_general(down_weight, rotated, (((0, 1), (0, 1)), ((), ())), prefe...]
    convert_element_type x4 -> x0, other arithmetic: 23.4 us -> none  [the longest x3 18.9 us: body(): current.astype(jnp.bfloat16)]
    concatenate x0 -> x2, other arithmetic: none -> 13.4 us  [weights(): both = [jnp.concatenate(folded[:2]), jnp.concatenate(folded[2:])]]
    unnamed x6 -> x29, local copies, waits for them, and re-layouts: 2.99 us -> 13.5 us
  transfers between devices with their start and end apart: 4 -> 48, of which waited for: 4 -> 15; matrix products, arithmetic and copies ran while one was open for 0% -> 4% of each run, Pallas kernels for 0% -> 48%
where the time goes in v1:
time: 319 us; the launch traced here: 317 us
  Pallas kernels  154 us (48%)
  waiting for transfers between devices  74.5 us (23%)
  starting transfers between devices  60.6 us (19%)
  local copies, waits for them, and re-layouts  14.1 us (4%)
  other arithmetic  13.4 us (4%)
    pallas_call x56, Pallas kernels, call(): pl.pallas_call(run, out_shape=outs, grid=grid, in_specs=[pl.BlockSpec(mem...  110 us
    ppermute x48, waiting for transfers between devices, exchange(): return lax.ppermute(value, 'tensor', pairs)  74.5 us
    ppermute x48, starting transfers between devices, exchange(): return lax.ppermute(value, 'tensor', pairs)  60.6 us
    pallas_call x4, Pallas kernels, fold_weight(): pl.pallas_call(kernel, out_shape=bf16(count * rows, units), grid_spec=plt...  44.4 us
    unnamed x29, local copies, waits for them, and re-layouts  13.5 us
    concatenate x2, other arithmetic, weights(): both = [jnp.concatenate(folded[:2]), jnp.concatenate(folded[2:])]  13.4 us
  transfers between devices with their start and end apart: 48, of which 15 were waited for; matrix products, arithmetic and copies ran while one was open for 4% of the time, Pallas kernels for 48%

profile of v1, /device:TPU:0, one launch (start us, length us, event | category | flops | bytes accessed | tf_op | source)
XLA Modules:
  0.0 317.2 jit_solution(6745703217211736717)
XLA Ops:
  4.3 3.0 collective-permute-start
  7.3 11.0 %shard_map.56._ = bf16[1024,1792]{1,0:T(8,128)(2,1)S(1)} custom-call(s32[8]{0:T(128)S(1)} %broadcast_xor_fusion.block_ref, bf16[1792,128]{1,0:T(8,128)(2,1)S(1)} %shard_map.55._.refs_1_, bf16[1792,4096]{1,0:T(8,128)(2,1)} %bitcast.15, bf16[1792,1792]{1,0:T(8,128)(2,1)} %constant.14.clone.factor_ref), custom_call_target="tpu_custom_call" | custom-call | flops 6576668672 | bytes 13762560 | tf_op jit(solution)/shard_map/pallas_call | solution.py:122
  30.5 11.0 %shard_map.60._ = bf16[1024,1792]{1,0:T(8,128)(2,1)S(1)} custom-call(s32[8]{0:T(128)S(1)} %broadcast_xor_fusion.block_ref, bf16[1792,128]{1,0:T(8,128)(2,1)S(1)} %shard_map.59._.refs_1_, bf16[1792,4096]{1,0:T(8,128)(2,1)} %bitcast.16, bf16[1792,1792]{1,0:T(8,128)(2,1)} %constant.14.clone.factor_ref), custom_call_target="tpu_custom_call" | custom-call | flops 6576668672 | bytes 13762560 | tf_op jit(solution)/shard_map/pallas_call | solution.py:122
  44.7 6.8 %pad_maximum_fusion.refs_3_ = bf16[2048,1792]{1,0:T(8,128)(2,1)} fusion(bf16[1024,1792]{1,0:T(8,128)(2,1)} %copy-done.5, bf16[1024,1792]{1,0:T(8,128)(2,1)} %copy-done.3), kind=kLoop, calls=%fused_computation | loop fusion | flops 14680064 | bytes 14680064 | tf_op jit(solution)/shard_map/concatenate | solution.py:252
  55.5 2.6 collective-permute-start.5
  58.2 11.1 %shard_map.64._ = bf16[1024,1792]{1,0:T(8,128)(2,1)S(1)} custom-call(s32[8]{0:T(128)S(1)} %broadcast_xor_fusion.block_ref, bf16[1792,128]{1,0:T(8,128)(2,1)S(1)} %shard_map.63._.refs_1_, bf16[1792,4096]{1,0:T(8,128)(2,1)} %bitcast.17, bf16[1792,1792]{1,0:T(8,128)(2,1)} %constant.14.clone.factor_ref), custom_call_target="tpu_custom_call" | custom-call | flops 6576668672 | bytes 13762560 | tf_op jit(solution)/shard_map/pallas_call | solution.py:122
  71.6 11.2 %shard_map.65._ = bf16[1024,1792]{1,0:T(8,128)(2,1)S(1)} custom-call(s32[8]{0:T(128)S(1)} %broadcast_xor_fusion.block_ref, bf16[1024,1792]{1,0:T(8,128)(2,1)} %copy-done.6, bf16[1792,4096]{1,0:T(8,128)(2,1)} %bitcast.18, bf16[1792,1792]{1,0:T(8,128)(2,1)} %constant.14.clone.factor_ref), custom_call_target="tpu_custom_call" | custom-call | flops 6576668672 | bytes 13762560 | tf_op jit(solution)/shard_map/pallas_call | solution.py:122
  89.8 6.6 %pad_maximum_fusion.1.refs_4_ = bf16[2048,1792]{1,0:T(8,128)(2,1)} fusion(bf16[1024,1792]{1,0:T(8,128)(2,1)} %copy-done.4, bf16[1024,1792]{1,0:T(8,128)(2,1)} %copy-done.6), kind=kLoop, calls=%fused_computation.1 | loop fusion | flops 14680064 | bytes 14680064 | tf_op jit(solution)/shard_map/concatenate | solution.py:252
  96.5 10.4 %shard_map.68 = (bf16[2048,128]{1,0:T(8,128)(2,1)S(1)}, bf16[2048,128]{1,0:T(8,128)(2,1)S(1)}) custom-call(bf16[1792,128]{1,0:T(8,128)(2,1)S(1)} %shard_map.67._.refs_1_, bf16[1792,128]{1,0:T(8,128)(2,1)} %collective-permute-done.5.refs_0_, bf16[1792,128]{1,0:T(8,128)(2,1)} %shard_map.62._.refs_1_, f32[1]{0:T(128)} %bitcast.5.refs_2_, ...), custom_call_target="tpu_custom_call" | custom-call | flops 1879048192 | bytes 16646148 | tf_op jit(solution)/shard_map/pallas_call | solution.py:57
  113.9 3.0 collective-permute-start.12
  116.9 10.3 %shard_map.72 = (bf16[2048,128]{1,0:T(8,128)(2,1)S(1)}, bf16[2048,128]{1,0:T(8,128)(2,1)S(1)}) custom-call(bf16[1792,128]{1,0:T(8,128)(2,1)S(1)} %shard_map.71._.refs_1_, bf16[1792,128]{1,0:T(8,128)(2,1)} %collective-permute-done.8.refs_0_, bf16[1792,128]{1,0:T(8,128)(2,1)S(1)} %shard_map.67._.refs_1_, f32[1]{0:T(128)} %bitcast.5.refs_2_, ...), custom_call_target="tpu_custom_call" | custom-call | flops 1879048192 | bytes 16646148 | tf_op jit(solution)/shard_map/pallas_call | solution.py:57
  134.1 2.6 collective-permute-start.17
  136.7 10.2 %shard_map.77 = (bf16[2048,128]{1,0:T(8,128)(2,1)S(1)}, bf16[2048,128]{1,0:T(8,128)(2,1)S(1)}) custom-call(bf16[1792,128]{1,0:T(8,128)(2,1)S(1)} %shard_map.76._.refs_1_, bf16[1792,128]{1,0:T(8,128)(2,1)S(1)} %collective-permute-done.12.refs_0_, bf16[1792,128]{1,0:T(8,128)(2,1)S(1)} %shard_map.71._.refs_1_, f32[1]{0:T(128)} %bitcast.5.refs_2_, ...), custom_call_target="tpu_custom_call" | custom-call | flops 1879048192 | bytes 16646148 | tf_op jit(solution)/shard_map/pallas_call | solution.py:57
  153.6 6.7 %collective-permute-done.16.refs_0_ = bf16[1792,128]{1,0:T(8,128)(2,1)S(1)} collective-permute-done((bf16[1792,128]{1,0:T(8,128)(2,1)S(1)}, bf16[1792,128]{1,0:T(8,128)(2,1)S(1)}, u32[]{:S(2)}, u32[]{:S(2)}) %collective-permute-start.16) | collective-permute-done | bytes 458784 | tf_op jit(solution)/shard_map/ppermute | solution.py:48
  160.5 8.0 %collective-permute-start.23 = (bf16[1792,128]{1,0:T(8,128)(2,1)S(1)}, bf16[1792,128]{1,0:T(8,128)(2,1)S(1)}, u32[]{:S(2)}, u32[]{:S(2)}) collective-permute-start(bf16[1792,128]{1,0:T(8,128)(2,1)S(1)} %shard_map.82._.refs_1_), channel_id=1, source_target_pairs={{0,4},{1,5},{2,6},{3,7},{4,0},{5,1},{6,2},{7,3},{8,12},{9,13},{10,... | collective-permute-start | bytes 1376264 | tf_op jit(solution)/shard_map/ppermute | solution.py:48
  168.6 10.2 %shard_map.83 = (bf16[2048,128]{1,0:T(8,128)(2,1)S(1)}, bf16[2048,128]{1,0:T(8,128)(2,1)S(1)}) custom-call(bf16[1792,128]{1,0:T(8,128)(2,1)S(1)} %shard_map.82._.refs_1_, bf16[1792,128]{1,0:T(8,128)(2,1)S(1)} %collective-permute-done.17.refs_0_, bf16[1792,128]{1,0:T(8,128)(2,1)S(1)} %shard_map.76._.refs_1_, f32[1]{0:T(128)} %bitcast.5.refs_2_, ...), custom_call_target="tpu_custom_call" | custom-call | flops 1879048192 | bytes 16646148 | tf_op jit(solution)/shard_map/pallas_call | solution.py:57
  180.5 9.7 %collective-permute-done.20.refs_0_ = bf16[512,128]{1,0:T(8,128)(2,1)S(1)} collective-permute-done((bf16[512,128]{1,0:T(8,128)(2,1)S(1)}, bf16[512,128]{1,0:T(8,128)(2,1)S(1)}, u32[]{:S(2)}, u32[]{:S(2)}) %collective-permute-start.20) | collective-permute-done | bytes 131104 | tf_op jit(solution)/shard_map/ppermute | solution.py:48
  192.5 2.5 collective-permute-start.27
  197.6 10.4 %shard_map.90 = (bf16[2048,128]{1,0:T(8,128)(2,1)S(1)}, bf16[2048,128]{1,0:T(8,128)(2,1)S(1)}) custom-call(bf16[1792,128]{1,0:T(8,128)(2,1)S(1)} %shard_map.89._.refs_1_, bf16[1792,128]{1,0:T(8,128)(2,1)S(1)} %collective-permute-done.23.refs_0_, bf16[1792,128]{1,0:T(8,128)(2,1)S(1)} %shard_map.82._.refs_1_, f32[1]{0:T(128)} %bitcast.5.refs_2_, ...), custom_call_target="tpu_custom_call" | custom-call | flops 1879048192 | bytes 16646148 | tf_op jit(solution)/shard_map/pallas_call | solution.py:57
  211.3 10.5 %collective-permute-done.26.refs_0_ = bf16[512,128]{1,0:T(8,128)(2,1)S(1)} collective-permute-done((bf16[512,128]{1,0:T(8,128)(2,1)S(1)}, bf16[512,128]{1,0:T(8,128)(2,1)S(1)}, u32[]{:S(2)}, u32[]{:S(2)}) %collective-permute-start.26) | collective-permute-done | bytes 131104 | tf_op jit(solution)/shard_map/ppermute | solution.py:48
  229.3 10.2 %shard_map.96 = (bf16[2048,128]{1,0:T(8,128)(2,1)S(1)}, bf16[2048,128]{1,0:T(8,128)(2,1)S(1)}) custom-call(bf16[1792,128]{1,0:T(8,128)(2,1)S(1)} %shard_map.95._.refs_1_, bf16[1792,128]{1,0:T(8,128)(2,1)S(1)} %collective-permute-done.29.refs_0_, bf16[1792,128]{1,0:T(8,128)(2,1)S(1)} %shard_map.89._.refs_1_, f32[1]{0:T(128)} %bitcast.5.refs_2_, ...), custom_call_target="tpu_custom_call" | custom-call | flops 1879048192 | bytes 16646148 | tf_op jit(solution)/shard_map/pallas_call | solution.py:57
  239.7 7.6 %collective-permute-done.31.refs_0_ = bf16[1024,128]{1,0:T(8,128)(2,1)S(1)} collective-permute-done((bf16[1024,128]{1,0:T(8,128)(2,1)S(1)}, bf16[1024,128]{1,0:T(8,128)(2,1)S(1)}, u32[]{:S(2)}, u32[]{:S(2)}) %collective-permute-start.31) | collective-permute-done | bytes 262176 | tf_op jit(solution)/shard_map/ppermute | solution.py:48
  247.8 2.8 collective-permute-start.37
  250.7 10.2 %shard_map.101 = (bf16[2048,128]{1,0:T(8,128)(2,1)S(1)}, bf16[2048,128]{1,0:T(8,128)(2,1)S(1)}) custom-call(bf16[1792,128]{1,0:T(8,128)(2,1)S(1)} %shard_map.100._.refs_1_, bf16[1792,128]{1,0:T(8,128)(2,1)S(1)} %collective-permute-done.34.refs_0_, bf16[1792,128]{1,0:T(8,128)(2,1)S(1)} %shard_map.95._.refs_1_, f32[1]{0:T(128)} %bitcast.5.refs_2_, ...), custom_call_target="tpu_custom_call" | custom-call | flops 1879048192 | bytes 16646148 | tf_op jit(solution)/shard_map/pallas_call | solution.py:57
  261.2 9.1 %collective-permute-done.37.refs_0_ = bf16[512,128]{1,0:T(8,128)(2,1)S(1)} collective-permute-done((bf16[512,128]{1,0:T(8,128)(2,1)S(1)}, bf16[512,128]{1,0:T(8,128)(2,1)S(1)}, u32[]{:S(2)}, u32[]{:S(2)}) %collective-permute-start.37) | collective-permute-done | bytes 131104 | tf_op jit(solution)/shard_map/ppermute | solution.py:48
  270.3 10.2 %shard_map.105 = (bf16[2048,128]{1,0:T(8,128)(2,1)S(1)}, bf16[2048,128]{1,0:T(8,128)(2,1)S(1)}) custom-call(bf16[512,128]{1,0:T(8,128)(2,1)S(1)} %shard_map.104._, bf16[1792,128]{1,0:T(8,128)(2,1)S(1)} %collective-permute-done.38.refs_0_, bf16[1792,128]{1,0:T(8,128)(2,1)S(1)} %shard_map.100._.refs_1_, f32[1]{0:T(128)} %bitcast.5.refs_2_, ...), custom_call_target="tpu_custom_call" | custom-call | flops 1879048192 | bytes 16646148 | tf_op jit(solution)/shard_map/pallas_call | solution.py:57
  281.7 2.8 collective-permute-start.41
  284.9 8.2 %collective-permute-done.40.refs_0_ = bf16[1024,128]{1,0:T(8,128)(2,1)S(1)} collective-permute-done((bf16[1024,128]{1,0:T(8,128)(2,1)S(1)}, bf16[1024,128]{1,0:T(8,128)(2,1)S(1)}, u32[]{:S(2)}, u32[]{:S(2)}) %collective-permute-start.40) | collective-permute-done | bytes 262176 | tf_op jit(solution)/shard_map/ppermute | solution.py:48
  294.9 2.5 collective-permute-start.44
  297.4 4.1 %collective-permute-done.43.refs_0_ = bf16[1024,128]{1,0:T(8,128)(2,1)S(1)} collective-permute-done((bf16[1024,128]{1,0:T(8,128)(2,1)S(1)}, bf16[1024,128]{1,0:T(8,128)(2,1)S(1)}, u32[]{:S(2)}, u32[]{:S(2)}) %collective-permute-start.43) | collective-permute-done | bytes 262176 | tf_op jit(solution)/shard_map/ppermute | solution.py:48
  302.1 3.2 %collective-permute-done.44.refs_0_ = bf16[512,128]{1,0:T(8,128)(2,1)S(1)} collective-permute-done((bf16[512,128]{1,0:T(8,128)(2,1)S(1)}, bf16[512,128]{1,0:T(8,128)(2,1)S(1)}, u32[]{:S(2)}, u32[]{:S(2)}) %collective-permute-start.44) | collective-permute-done | bytes 131104 | tf_op jit(solution)/shard_map/ppermute | solution.py:48
  309.0 5.6 %collective-permute-done.46.refs_0_ = bf16[512,128]{1,0:T(8,128)(2,1)S(1)} collective-permute-done((bf16[512,128]{1,0:T(8,128)(2,1)S(1)}, bf16[512,128]{1,0:T(8,128)(2,1)S(1)}, u32[]{:S(2)}, u32[]{:S(2)}) %collective-permute-start.46) | collective-permute-done | bytes 131104 | tf_op jit(solution)/shard_map/ppermute | solution.py:48
  (157 shorter events, 82.1 us)
Async XLA Ops:
  26.9 24.6 %collective-permute-start.2 = (bf16[1792,128]{1,0:T(8,128)(2,1)S(1)}, bf16[1792,128]{1,0:T(8,128)(2,1)}, u32[]{:S(2)}, u32[]{:S(2)}) collective-permute-start(bf16[1792,128]{1,0:T(8,128)(2,1)S(1)} %shard_map.58._.refs_1_), channel_id=1, source_target_pairs={{0,2},{1,3},{2,0},{3,1},{4,6},{5,7},{6,4},{7,5},{8,10},{9,11},{10,... | collective-permute-start | bytes 1376264 | tf_op jit(solution)/shard_map/ppermute | solution.py:48
  29.0 53.8 %collective-permute-start.3 = (bf16[1792,128]{1,0:T(8,128)(2,1)S(1)}, bf16[1792,128]{1,0:T(8,128)(2,1)S(1)}, u32[]{:S(2)}, u32[]{:S(2)}) collective-permute-start(bf16[1792,128]{1,0:T(8,128)(2,1)S(1)} %shard_map.59._.refs_1_), channel_id=1, source_target_pairs={{0,1},{1,0},{2,3},{3,2},{4,5},{5,4},{6,7},{7,6},{8,9},{9,8},{10,11... | collective-permute-start | bytes 1376264 | tf_op jit(solution)/shard_map/ppermute | solution.py:48
  44.3 43.8 %collective-permute-start.4 = (bf16[1792,128]{1,0:T(8,128)(2,1)}, bf16[1792,128]{1,0:T(8,128)(2,1)}, u32[]{:S(2)}, u32[]{:S(2)}) collective-permute-start(bf16[1792,128]{1,0:T(8,128)(2,1)} %shard_map.61._.refs_1_), channel_id=1, source_target_pairs={{0,2},{1,3},{2,0},{3,1},{4,6},{5,7},{6,4},{7,5},{8,10},{9,11},{10,... | collective-permute-start | bytes 1376264 | tf_op jit(solution)/shard_map/ppermute | solution.py:48
  55.5 40.9 %collective-permute-start.5 = (bf16[1792,128]{1,0:T(8,128)(2,1)}, bf16[1792,128]{1,0:T(8,128)(2,1)}, u32[]{:S(2)}, u32[]{:S(2)}) collective-permute-start(bf16[1792,128]{1,0:T(8,128)(2,1)} %shard_map.62._.refs_1_), channel_id=1, source_target_pairs={{0,4},{1,5},{2,6},{3,7},{4,0},{5,1},{6,2},{7,3},{8,12},{9,13},{10,... | collective-permute-start | bytes 1376264 | tf_op jit(solution)/shard_map/ppermute | solution.py:48
  71.0 40.2 %collective-permute-start.6 = (bf16[1792,128]{1,0:T(8,128)(2,1)S(1)}, bf16[1792,128]{1,0:T(8,128)(2,1)}, u32[]{:S(2)}, u32[]{:S(2)}) collective-permute-start(bf16[1792,128]{1,0:T(8,128)(2,1)S(1)} %shard_map.63._.refs_1_), channel_id=1, source_target_pairs={{0,1},{1,0},{2,3},{3,2},{4,5},{5,4},{6,7},{7,6},{8,9},{9,8},{10,11... | collective-permute-start | bytes 1376264 | tf_op jit(solution)/shard_map/ppermute | solution.py:48
  86.7 26.1 %collective-permute-start.7 = (bf16[1792,128]{1,0:T(8,128)(2,1)S(1)}, bf16[1792,128]{1,0:T(8,128)(2,1)}, u32[]{:S(2)}, u32[]{:S(2)}) collective-permute-start(bf16[1792,128]{1,0:T(8,128)(2,1)S(1)} %shard_map.66._.refs_1_), channel_id=1, source_target_pairs={{0,2},{1,3},{2,0},{3,1},{4,6},{5,7},{6,4},{7,5},{8,10},{9,11},{10,... | collective-permute-start | bytes 1376264 | tf_op jit(solution)/shard_map/ppermute | solution.py:48
  89.4 27.5 %collective-permute-start.8 = (bf16[1792,128]{1,0:T(8,128)(2,1)S(1)}, bf16[1792,128]{1,0:T(8,128)(2,1)}, u32[]{:S(2)}, u32[]{:S(2)}) collective-permute-start(bf16[1792,128]{1,0:T(8,128)(2,1)S(1)} %shard_map.67._.refs_1_), channel_id=1, source_target_pairs={{0,4},{1,5},{2,6},{3,7},{4,0},{5,1},{6,2},{7,3},{8,12},{9,13},{10,... | collective-permute-start | bytes 1376264 | tf_op jit(solution)/shard_map/ppermute | solution.py:48
  106.9 21.9 %collective-permute-start.9 = (bf16[2048,128]{1,0:T(8,128)(2,1)S(1)}, bf16[2048,128]{1,0:T(8,128)(2,1)S(1)}, u32[]{:S(2)}, u32[]{:S(2)}) collective-permute-start(bf16[2048,128]{1,0:T(8,128)(2,1)S(1)} %get-tuple-element.55), channel_id=1, source_target_pairs={{0,1},{1,0},{2,3},{3,2},{4,5},{5,4},{6,7},{7,6},{8,9},{9,8},{10,11... | collective-permute-start | bytes 1572872 | tf_op jit(solution)/shard_map/ppermute | solution.py:48
  110.6 21.1 %collective-permute-start.10 = (bf16[1792,128]{1,0:T(8,128)(2,1)S(1)}, bf16[1792,128]{1,0:T(8,128)(2,1)S(1)}, u32[]{:S(2)}, u32[]{:S(2)}) collective-permute-start(bf16[1792,128]{1,0:T(8,128)(2,1)S(1)} %shard_map.69._.refs_1_), channel_id=1, source_target_pairs={{0,1},{1,0},{2,3},{3,2},{4,5},{5,4},{6,7},{7,6},{8,9},{9,8},{10,11... | collective-permute-start | bytes 1376264 | tf_op jit(solution)/shard_map/ppermute | solution.py:48
  112.4 20.8 %collective-permute-start.11 = (bf16[1792,128]{1,0:T(8,128)(2,1)S(1)}, bf16[1792,128]{1,0:T(8,128)(2,1)S(1)}, u32[]{:S(2)}, u32[]{:S(2)}) collective-permute-start(bf16[1792,128]{1,0:T(8,128)(2,1)S(1)} %shard_map.70._.refs_1_), channel_id=1, source_target_pairs={{0,2},{1,3},{2,0},{3,1},{4,6},{5,7},{6,4},{7,5},{8,10},{9,11},{10,... | collective-permute-start | bytes 1376264 | tf_op jit(solution)/shard_map/ppermute | solution.py:48
  113.9 20.2 %collective-permute-start.12 = (bf16[1792,128]{1,0:T(8,128)(2,1)S(1)}, bf16[1792,128]{1,0:T(8,128)(2,1)S(1)}, u32[]{:S(2)}, u32[]{:S(2)}) collective-permute-start(bf16[1792,128]{1,0:T(8,128)(2,1)S(1)} %shard_map.71._.refs_1_), channel_id=1, source_target_pairs={{0,4},{1,5},{2,6},{3,7},{4,0},{5,1},{6,2},{7,3},{8,12},{9,13},{10,... | collective-permute-start | bytes 1376264 | tf_op jit(solution)/shard_map/ppermute | solution.py:48
  131.1 21.3 %collective-permute-start.15 = (bf16[1792,128]{1,0:T(8,128)(2,1)S(1)}, bf16[1792,128]{1,0:T(8,128)(2,1)S(1)}, u32[]{:S(2)}, u32[]{:S(2)}) collective-permute-start(bf16[1792,128]{1,0:T(8,128)(2,1)S(1)} %shard_map.74._.refs_1_), channel_id=1, source_target_pairs={{0,1},{1,0},{2,3},{3,2},{4,5},{5,4},{6,7},{7,6},{8,9},{9,8},{10,11... | collective-permute-start | bytes 1376264 | tf_op jit(solution)/shard_map/ppermute | solution.py:48
  133.2 27.1 %collective-permute-start.16 = (bf16[1792,128]{1,0:T(8,128)(2,1)S(1)}, bf16[1792,128]{1,0:T(8,128)(2,1)S(1)}, u32[]{:S(2)}, u32[]{:S(2)}) collective-permute-start(bf16[1792,128]{1,0:T(8,128)(2,1)S(1)} %shard_map.75._.refs_1_), channel_id=1, source_target_pairs={{0,2},{1,3},{2,0},{3,1},{4,6},{5,7},{6,4},{7,5},{8,10},{9,11},{10,... | collective-permute-start | bytes 1376264 | tf_op jit(solution)/shard_map/ppermute | solution.py:48
  134.1 26.4 %collective-permute-start.17 = (bf16[1792,128]{1,0:T(8,128)(2,1)S(1)}, bf16[1792,128]{1,0:T(8,128)(2,1)S(1)}, u32[]{:S(2)}, u32[]{:S(2)}) collective-permute-start(bf16[1792,128]{1,0:T(8,128)(2,1)S(1)} %shard_map.76._.refs_1_), channel_id=1, source_target_pairs={{0,4},{1,5},{2,6},{3,7},{4,0},{5,1},{6,2},{7,3},{8,12},{9,13},{10,... | collective-permute-start | bytes 1376264 | tf_op jit(solution)/shard_map/ppermute | solution.py:48
  146.9 33.4 %collective-permute-start.18 = (bf16[2048,128]{1,0:T(8,128)(2,1)S(1)}, bf16[2048,128]{1,0:T(8,128)(2,1)S(1)}, u32[]{:S(2)}, u32[]{:S(2)}) collective-permute-start(bf16[2048,128]{1,0:T(8,128)(2,1)S(1)} %get-tuple-element.63), channel_id=1, source_target_pairs={{0,1},{1,0},{2,3},{3,2},{4,5},{5,4},{6,7},{7,6},{8,9},{9,8},{10,11... | collective-permute-start | bytes 1572872 | tf_op jit(solution)/shard_map/ppermute | solution.py:48
  149.5 29.2 %collective-permute-start.19 = (bf16[1024,128]{1,0:T(8,128)(2,1)S(1)}, bf16[1024,128]{1,0:T(8,128)(2,1)S(1)}, u32[]{:S(2)}, u32[]{:S(2)}) collective-permute-start(bf16[1024,128]{1,0:T(8,128)(2,1)S(1)} %get-tuple-element.65), channel_id=1, source_target_pairs={{0,2},{1,3},{2,0},{3,1},{4,6},{5,7},{6,4},{7,5},{8,10},{9,11},{10,... | collective-permute-start | bytes 786440 | tf_op jit(solution)/shard_map/ppermute | solution.py:48
  152.4 42.6 %collective-permute-start.21 = (bf16[1792,128]{1,0:T(8,128)(2,1)S(1)}, bf16[1792,128]{1,0:T(8,128)(2,1)S(1)}, u32[]{:S(2)}, u32[]{:S(2)}) collective-permute-start(bf16[1792,128]{1,0:T(8,128)(2,1)S(1)} %shard_map.80._.refs_1_), channel_id=1, source_target_pairs={{0,1},{1,0},{2,3},{3,2},{4,5},{5,4},{6,7},{7,6},{8,9},{9,8},{10,11... | collective-permute-start | bytes 1376264 | tf_op jit(solution)/shard_map/ppermute | solution.py:48
  160.3 34.9 %collective-permute-start.22 = (bf16[1792,128]{1,0:T(8,128)(2,1)S(1)}, bf16[1792,128]{1,0:T(8,128)(2,1)S(1)}, u32[]{:S(2)}, u32[]{:S(2)}) collective-permute-start(bf16[1792,128]{1,0:T(8,128)(2,1)S(1)} %shard_map.81._.refs_1_), channel_id=1, source_target_pairs={{0,2},{1,3},{2,0},{3,1},{4,6},{5,7},{6,4},{7,5},{8,10},{9,11},{10,... | collective-permute-start | bytes 1376264 | tf_op jit(solution)/shard_map/ppermute | solution.py:48
  160.5 37.0 %collective-permute-start.23 = (bf16[1792,128]{1,0:T(8,128)(2,1)S(1)}, bf16[1792,128]{1,0:T(8,128)(2,1)S(1)}, u32[]{:S(2)}, u32[]{:S(2)}) collective-permute-start(bf16[1792,128]{1,0:T(8,128)(2,1)S(1)} %shard_map.82._.refs_1_), channel_id=1, source_target_pairs={{0,4},{1,5},{2,6},{3,7},{4,0},{5,1},{6,2},{7,3},{8,12},{9,13},{10,... | collective-permute-start | bytes 1376264 | tf_op jit(solution)/shard_map/ppermute | solution.py:48
  178.7 31.7 %collective-permute-start.24 = (bf16[2048,128]{1,0:T(8,128)(2,1)S(1)}, bf16[2048,128]{1,0:T(8,128)(2,1)S(1)}, u32[]{:S(2)}, u32[]{:S(2)}) collective-permute-start(bf16[2048,128]{1,0:T(8,128)(2,1)S(1)} %get-tuple-element.69), channel_id=1, source_target_pairs={{0,1},{1,0},{2,3},{3,2},{4,5},{5,4},{6,7},{7,6},{8,9},{9,8},{10,11... | collective-permute-start | bytes 1572872 | tf_op jit(solution)/shard_map/ppermute | solution.py:48
  192.5 29.2 %collective-permute-start.27 = (bf16[1792,128]{1,0:T(8,128)(2,1)S(1)}, bf16[1792,128]{1,0:T(8,128)(2,1)S(1)}, u32[]{:S(2)}, u32[]{:S(2)}) collective-permute-start(bf16[1792,128]{1,0:T(8,128)(2,1)S(1)} %shard_map.87._.refs_1_), channel_id=1, source_target_pairs={{0,1},{1,0},{2,3},{3,2},{4,5},{5,4},{6,7},{7,6},{8,9},{9,8},{10,11... | collective-permute-start | bytes 1376264 | tf_op jit(solution)/shard_map/ppermute | solution.py:48
  195.2 30.9 %collective-permute-start.28 = (bf16[1792,128]{1,0:T(8,128)(2,1)S(1)}, bf16[1792,128]{1,0:T(8,128)(2,1)S(1)}, u32[]{:S(2)}, u32[]{:S(2)}) collective-permute-start(bf16[1792,128]{1,0:T(8,128)(2,1)S(1)} %shard_map.88._.refs_1_), channel_id=1, source_target_pairs={{0,2},{1,3},{2,0},{3,1},{4,6},{5,7},{6,4},{7,5},{8,10},{9,11},{10,... | collective-permute-start | bytes 1376264 | tf_op jit(solution)/shard_map/ppermute | solution.py:48
  197.5 30.1 %collective-permute-start.29 = (bf16[1792,128]{1,0:T(8,128)(2,1)S(1)}, bf16[1792,128]{1,0:T(8,128)(2,1)S(1)}, u32[]{:S(2)}, u32[]{:S(2)}) collective-permute-start(bf16[1792,128]{1,0:T(8,128)(2,1)S(1)} %shard_map.89._.refs_1_), channel_id=1, source_target_pairs={{0,4},{1,5},{2,6},{3,7},{4,0},{5,1},{6,2},{7,3},{8,12},{9,13},{10,... | collective-permute-start | bytes 1376264 | tf_op jit(solution)/shard_map/ppermute | solution.py:48
  210.4 29.1 %collective-permute-start.30 = (bf16[2048,128]{1,0:T(8,128)(2,1)S(1)}, bf16[2048,128]{1,0:T(8,128)(2,1)S(1)}, u32[]{:S(2)}, u32[]{:S(2)}) collective-permute-start(bf16[2048,128]{1,0:T(8,128)(2,1)S(1)} %get-tuple-element.75), channel_id=1, source_target_pairs={{0,1},{1,0},{2,3},{3,2},{4,5},{5,4},{6,7},{7,6},{8,9},{9,8},{10,11... | collective-permute-start | bytes 1572872 | tf_op jit(solution)/shard_map/ppermute | solution.py:48
  222.0 25.5 %collective-permute-start.33 = (bf16[1792,128]{1,0:T(8,128)(2,1)S(1)}, bf16[1792,128]{1,0:T(8,128)(2,1)S(1)}, u32[]{:S(2)}, u32[]{:S(2)}) collective-permute-start(bf16[1792,128]{1,0:T(8,128)(2,1)S(1)} %shard_map.94._.refs_1_), channel_id=1, source_target_pairs={{0,2},{1,3},{2,0},{3,1},{4,6},{5,7},{6,4},{7,5},{8,10},{9,11},{10,... | collective-permute-start | bytes 1376264 | tf_op jit(solution)/shard_map/ppermute | solution.py:48
  222.0 25.3 %collective-permute-start.31 = (bf16[1024,128]{1,0:T(8,128)(2,1)S(1)}, bf16[1024,128]{1,0:T(8,128)(2,1)S(1)}, u32[]{:S(2)}, u32[]{:S(2)}) collective-permute-start(bf16[1024,128]{1,0:T(8,128)(2,1)S(1)} %get-tuple-element.77), channel_id=1, source_target_pairs={{0,2},{1,3},{2,0},{3,1},{4,6},{5,7},{6,4},{7,5},{8,10},{9,11},{10,... | collective-permute-start | bytes 786440 | tf_op jit(solution)/shard_map/ppermute | solution.py:48
  226.2 21.3 %collective-permute-start.32 = (bf16[512,128]{1,0:T(8,128)(2,1)S(1)}, bf16[512,128]{1,0:T(8,128)(2,1)S(1)}, u32[]{:S(2)}, u32[]{:S(2)}) collective-permute-start(bf16[512,128]{1,0:T(8,128)(2,1)S(1)} %get-tuple-element.79), channel_id=1, source_target_pairs={{0,4},{1,5},{2,6},{3,7},{4,0},{5,1},{6,2},{7,3},{8,12},{9,13},{10,... | collective-permute-start | bytes 393224 | tf_op jit(solution)/shard_map/ppermute | solution.py:48
  227.6 23.1 %collective-permute-start.34 = (bf16[1792,128]{1,0:T(8,128)(2,1)S(1)}, bf16[1792,128]{1,0:T(8,128)(2,1)S(1)}, u32[]{:S(2)}, u32[]{:S(2)}) collective-permute-start(bf16[1792,128]{1,0:T(8,128)(2,1)S(1)} %shard_map.95._.refs_1_), channel_id=1, source_target_pairs={{0,4},{1,5},{2,6},{3,7},{4,0},{5,1},{6,2},{7,3},{8,12},{9,13},{10,... | collective-permute-start | bytes 1376264 | tf_op jit(solution)/shard_map/ppermute | solution.py:48
  239.5 21.4 %collective-permute-start.35 = (bf16[2048,128]{1,0:T(8,128)(2,1)S(1)}, bf16[2048,128]{1,0:T(8,128)(2,1)S(1)}, u32[]{:S(2)}, u32[]{:S(2)}) collective-permute-start(bf16[2048,128]{1,0:T(8,128)(2,1)S(1)} %get-tuple-element.81), channel_id=1, source_target_pairs={{0,1},{1,0},{2,3},{3,2},{4,5},{5,4},{6,7},{7,6},{8,9},{9,8},{10,11... | collective-permute-start | bytes 1572872 | tf_op jit(solution)/shard_map/ppermute | solution.py:48
  247.7 22.6 %collective-permute-start.38 = (bf16[1792,128]{1,0:T(8,128)(2,1)S(1)}, bf16[1792,128]{1,0:T(8,128)(2,1)S(1)}, u32[]{:S(2)}, u32[]{:S(2)}) collective-permute-start(bf16[1792,128]{1,0:T(8,128)(2,1)S(1)} %shard_map.100._.refs_1_), channel_id=1, source_target_pairs={{0,4},{1,5},{2,6},{3,7},{4,0},{5,1},{6,2},{7,3},{8,12},{9,13},{10,... | collective-permute-start | bytes 1376264 | tf_op jit(solution)/shard_map/ppermute | solution.py:48
  247.8 22.4 %collective-permute-start.37 = (bf16[512,128]{1,0:T(8,128)(2,1)S(1)}, bf16[512,128]{1,0:T(8,128)(2,1)S(1)}, u32[]{:S(2)}, u32[]{:S(2)}) collective-permute-start(bf16[512,128]{1,0:T(8,128)(2,1)S(1)} %get-tuple-element.85), channel_id=1, source_target_pairs={{0,4},{1,5},{2,6},{3,7},{4,0},{5,1},{6,2},{7,3},{8,12},{9,13},{10,... | collective-permute-start | bytes 393224 | tf_op jit(solution)/shard_map/ppermute | solution.py:48
  260.9 23.7 %collective-permute-start.39 = (bf16[2048,128]{1,0:T(8,128)(2,1)S(1)}, bf16[2048,128]{1,0:T(8,128)(2,1)S(1)}, u32[]{:S(2)}, u32[]{:S(2)}) collective-permute-start(bf16[2048,128]{1,0:T(8,128)(2,1)S(1)} %get-tuple-element.87), channel_id=1, source_target_pairs={{0,1},{1,0},{2,3},{3,2},{4,5},{5,4},{6,7},{7,6},{8,9},{9,8},{10,11... | collective-permute-start | bytes 1572872 | tf_op jit(solution)/shard_map/ppermute | solution.py:48
  (27 other events, 255.0 us)

commit v2 on v0

v2 whole, which is shorter than its diff:
```python
import math

import jax
import jax.numpy as jnp
import numpy as np
from jax import lax
from jax.experimental import pallas as pl
from jax.experimental.pallas import tpu as pltpu
from jax.sharding import PartitionSpec as P

SIZES = (1, 1, 1, 1, 1, 1, 1, 1)
EXCHANGE = (
    (2, 0, 1), (1, 0, 2), (0, 1, 2), (1, 0, 2), (0, 1, 2), (0, 1, 2), (1, 0, 2), (2, 1, 0),
)
REDUCE = (
    (0, 1, 2), (0, 1, 2), (0, 1, 2), (0, 1, 2), (0, 1, 2), (0, 1, 2), (0, 2, 1), (0, 1, 2),
)
EVENTS = (
    3, 7, 4, 1, 3, 6, 2, 7, 0, 4, 5, 1, 3, 0, 5, 6, 1, 2, 3, 7, 0, 6, 4, 1,
    7, 3, 5, 4, 1, 2, 6, 7, 4, 0, 2, 3, 6, 1, 5, 4, 6, 0, 4, 7, 3, 5, 0, 7,
    2, 5, 0, 2, 5, 1, 6, 2,
)
COSTS = (
    1, 1, 1, 1, 1, 1, 1, 1,
    1, 1, 1, 1, 1, 1, 1, 1,
    1, 1, 1, 1, 1, 1, 1, 1,
    1, 1, 1, 1, 1, 1, 1, 1,
    1, 1, 1, 1, 1, 1, 1, 1,
    1, 1, 1, 1, 1, 1, 1, 1,
    1, 1, 1, 1, 1, 1, 1, 1,
)
VMEM = 48 * 1024 * 1024


def character(value, prime_order):
    residue = value % prime_order
    if residue == 0:
        return 0
    squares_list = [index * index % prime_order for index in range(1, prime_order)]
    return 1 if residue in squares_list else -1


def paley_matrix():
    prime_order = 13
    conference = np.zeros((14, 14))
    conference[0, 1:] = 1.0
    conference[1:, 0] = 1.0
    for row_index in range(prime_order):
        for col_index in range(prime_order):
            conference[row_index + 1, col_index + 1] = character(col_index - row_index, prime_order)
    first = np.array([[1.0, 1.0], [1.0, -1.0]])
    second = np.array([[1.0, -1.0], [-1.0, -1.0]])
    return np.kron(conference, first) + np.kron(np.eye(14), second)


def sylvester(order):
    matrix = np.ones((1, 1))
    basic = np.array([[1.0, 1.0], [1.0, -1.0]])
    while matrix.shape[0] < order:
        matrix = np.kron(basic, matrix)
    return matrix


def plan(levels):
    if levels == len(EXCHANGE[0]):
        return SIZES, EXCHANGE, REDUCE, zip(EVENTS, COSTS)
    plain = (tuple(range(levels)),) * 8
    stages = 2 * levels + 1
    turns = [turn - stage for turn in range(8 + stages) for stage in (*range(1, stages), 0)]
    turns = [chunk for chunk in turns if 0 <= chunk < 8]
    return (1,) * 8, plain, plain, [(chunk, 1) for chunk in turns]


def exchange(value, bit):
    pairs = [(source, source ^ (1 << bit)) for source in range(lax.axis_size("tensor"))]
    return lax.ppermute(value, "tensor", pairs)


def call(kernel, after, cost, operands, specs, outs, out_specs, grid, scratch=()):
    def run(_, *refs):
        kernel(*refs)

    return pl.pallas_call(
        run,
        out_shape=outs,
        grid=grid,
        in_specs=[pl.BlockSpec(memory_space=pl.ANY), *specs],
        out_specs=out_specs,
        scratch_shapes=list(scratch),
        compiler_params=pltpu.CompilerParams(vmem_limit_bytes=VMEM),
        cost_estimate=pl.CostEstimate(flops=cost, bytes_accessed=1, transcendentals=0),
    )(after, *operands)


def bf16(*shape):
    return jax.ShapeDtypeStruct(shape, jnp.bfloat16)


def rows_spec(rows, step, offset=0):
    return pl.BlockSpec((rows, step), lambda i: (i + offset, 0))


SCALAR = pl.BlockSpec(memory_space=pltpu.SMEM)


def activate(after, cost, gate, up, first, step):
    units = gate.shape[0]
    blocks = 4
    size = math.gcd(first, step)

    def kernel(gate_ref, up_ref, out_ref):
        g = gate_ref[...].astype(jnp.float32)
        u = up_ref[...].astype(jnp.float32)
        out_ref[...] = (0.5 * g * (1.0 + jnp.tanh(0.5 * g)) * u).astype(jnp.bfloat16)

    spec = pl.BlockSpec((units // blocks, size), lambda i, j: (i, first // size + j))
    return call(
        kernel, after, cost, (gate, up), [spec, spec], [bf16(units, step)],
        [pl.BlockSpec((units // blocks, size), lambda i, j: (i, j))], (blocks, step // size),
    )[0]


def mix(after, cost, partner, own, sign):
    units, step = own.shape
    blocks = 2

    def kernel(partner_ref, own_ref, sign_ref, out_ref):
        total = partner_ref[...].astype(jnp.float32) + sign_ref[0] * own_ref[...].astype(jnp.float32)
        out_ref[...] = total.astype(jnp.bfloat16)

    spec = rows_spec(units // blocks, step)
    return call(
        kernel, after, cost, (partner, own, sign), [spec, spec, SCALAR], [bf16(units, step)],
        [spec], (blocks,),
    )[0]


def project(after, cost, partner, own, sign, factor, weight, block_of, scale):
    units, step = own.shape
    features = weight.shape[1]
    blocks = block_of.shape[0] // 2
    rows = features // (2 * blocks)
    side = factor.shape[0]
    groups = units // side
    inner = side // 28

    def rotate(partner_ref, own_ref, sign_ref, factor_ref, rotated):
        total = partner_ref[...].astype(jnp.float32) + sign_ref[0] * own_ref[...].astype(jnp.float32)
        total = total.astype(jnp.bfloat16).reshape(28, groups, inner, step)
        parts = [
            jnp.dot(
                factor_ref[...], total[:, group].reshape(side, step), preferred_element_type=jnp.float32
            )
            for group in range(groups)
        ]
        distance = 1
        while distance < groups:
            parts = [
                parts[index] + parts[index ^ distance]
                if not index & distance
                else parts[index ^ distance] - parts[index]
                for index in range(groups)
            ]
            distance *= 2
        parts = [(part * scale).astype(jnp.bfloat16).reshape(28, 1, inner, step) for part in parts]
        rotated[...] = jnp.concatenate(parts, axis=1).reshape(units, step)

    def kernel(block_ref, _, partner_ref, own_ref, sign_ref, factor_ref, given_w, kept_w, given_ref, kept_ref, rotated):
        @pl.when(pl.program_id(0) == 0)
        def _():
            rotate(partner_ref, own_ref, sign_ref, factor_ref, rotated)

        for w_ref, out_ref in ((given_w, given_ref), (kept_w, kept_ref)):
            out_ref[...] = lax.dot_general(
                w_ref[...], rotated[...], (((0,), (0,)), ((), ())), preferred_element_type=jnp.float32
            ).astype(jnp.bfloat16)

    whole = pl.BlockSpec((units, step), lambda i, block: (0, 0))
    out = pl.BlockSpec((rows, step), lambda i, block: (i, 0))
    return pl.pallas_call(
        kernel,
        out_shape=[bf16(features // 2, step)] * 2,
        grid_spec=pltpu.PrefetchScalarGridSpec(
            num_scalar_prefetch=1,
            grid=(blocks,),
            in_specs=[
                pl.BlockSpec(memory_space=pl.ANY),
                whole,
                whole,
                SCALAR,
                pl.BlockSpec((side, side), lambda i, block: (0, 0)),
                pl.BlockSpec((units, rows), lambda i, block: (0, block[i])),
                pl.BlockSpec((units, rows), lambda i, block: (0, block[blocks + i])),
            ],
            out_specs=[out, out],
            scratch_shapes=[pltpu.VMEM((units, step), jnp.bfloat16)],
        ),
        compiler_params=pltpu.CompilerParams(vmem_limit_bytes=VMEM),
        cost_estimate=pl.CostEstimate(flops=cost, bytes_accessed=1, transcendentals=0),
    )(block_of, after, partner, own, sign, factor, weight, weight)


def add(after, cost, taken, kept):
    rows, step = kept.shape

    def kernel(taken_ref, kept_ref, out_ref):
        total = taken_ref[...].astype(jnp.float32) + kept_ref[...].astype(jnp.float32)
        out_ref[...] = total.astype(jnp.bfloat16)

    spec = rows_spec(rows, step)
    return call(kernel, after, cost, (taken, kept), [spec, spec], [bf16(rows, step)], [spec], (1,))[0]


def add_split(after, cost, taken, kept):
    rows, step = kept.shape
    half = rows // 2

    def kernel(taken_ref, kept_ref, given_ref, kept_out):
        total = taken_ref[...].astype(jnp.float32) + kept_ref[...].astype(jnp.float32)
        total = total.astype(jnp.bfloat16)
        kept_out[...] = total[:half]
        given_ref[...] = total[half:]

    spec = rows_spec(rows, step)
    out = rows_spec(half, step)
    return call(
        kernel, after, cost, (taken, kept), [spec, spec], [bf16(half, step)] * 2, [out, out], (1,)
    )


def body(gate_pre, up_pre, down_weight):
    left, width, tokens = gate_pre.shape
    units = left * width
    features = down_weight.shape[-1]
    devices = lax.axis_size("tensor")
    levels = devices.bit_length() - 1
    position = lax.axis_index("tensor")
    signs = [
        (1 - 2 * ((position >> level) & 1)).astype(jnp.float32).reshape(1) for level in range(levels)
    ]
    scale = 1.0 / math.sqrt(units * devices)
    inner = min(width, 16)
    factor = jnp.asarray(np.kron(paley_matrix(), sylvester(inner)), jnp.bfloat16)
    weight = down_weight.reshape(units, features)
    gate = gate_pre.reshape(units, tokens)
    up = up_pre.reshape(units, tokens)

    def blocks_of(reduction):
        order = sorted(
            range(devices),
            key=lambda r: (1 - (r >> reduction[0] & 1), *[r >> level & 1 for level in reduction[1:]]),
        )
        return jnp.asarray(order, jnp.int32) ^ position

    sizes, exchanges, reductions, turns = plan(levels)
    places = {reduction: blocks_of(reduction) for reduction in sorted(set(reductions))}
    stages = [0] * len(sizes)
    state = [None] * len(sizes)
    outs = [None] * len(sizes)
    last = gate
    for chunk, cost in turns:
        stage = stages[chunk]
        stages[chunk] += 1
        turn, reduction = exchanges[chunk], reductions[chunk]
        if stage == 0:
            step = tokens // sum(sizes)
            first = sum(sizes[:chunk])
            last = activate(last, cost, gate, up, first * step, sizes[chunk] * step)
            state[chunk] = (exchange(last, turn[0]), last)
            continue
        partner, own = state[chunk]
        if stage < levels:
            last = mix(last, cost, partner, own, signs[turn[stage - 1]])
            state[chunk] = (exchange(last, turn[stage]), last)
        elif stage == levels:
            given, last = project(
                last, cost, partner, own, signs[turn[-1]], factor, weight, places[reduction], scale
            )
            state[chunk] = (exchange(given, reduction[0]), last)
        elif stage < 2 * levels:
            given, last = add_split(last, cost, partner, own)
            state[chunk] = (exchange(given, reduction[stage - levels]), last)
        else:
            outs[chunk] = last = add(last, cost, partner, own)
    return jnp.concatenate(outs, axis=1)


def solution(mesh):
    in_specs = (P(None, "tensor", "dp"), P(None, "tensor", "dp"), P(None, "tensor", None))
    out_specs = P("tensor", "dp")
    return jax.shard_map(body, mesh=mesh, in_specs=in_specs, out_specs=out_specs, check_vma=False)
```

time: 557 us -> 249 us (0.45)
  waiting for transfers between devices: 466 us -> 80.1 us
  Pallas kernels: 0 us -> 99.7 us
  starting transfers between devices: 7.26 us -> 57.3 us
  matrix products: 42 us -> 0 us
  other arithmetic: 23.4 us -> 0.01 us
  between operations: 13.4 us -> 0.69 us
    ppermute x3 -> x48, waiting for transfers between devices: 316 us -> 80.1 us  [exchange(): return lax.ppermute(value, 'tensor', pairs)]
    reduce_scatter x1 -> x0, waiting for transfers between devices: 150 us -> none  [body(): lax.psum_scatter(lax.dot_general(down_weight, rotated, (((0, 1), (0, 1)),...]
    pallas_call x0 -> x56, Pallas kernels: none -> 99.7 us  [the longest x8 72.8 us: project(): pl.pallas_call(kernel, out_shape=[bf16(features // 2, step)] * 2, grid_sp...]
    ppermute x3 -> x48, starting transfers between devices: 7.26 us -> 57.3 us  [exchange(): return lax.ppermute(value, 'tensor', pairs)]
    dot_general x3 -> x0, matrix products: 42 us -> none  [the longest x1 27.8 us: body(): lax.dot_general(down_weight, rotated, (((0, 1), (0, 1)), ((), ())), prefe...]
    convert_element_type x4 -> x0, other arithmetic: 23.4 us -> none  [the longest x3 18.9 us: body(): current.astype(jnp.bfloat16)]
    unnamed x6 -> x25, local copies, waits for them, and re-layouts: 2.99 us -> 9.39 us
  transfers between devices with their start and end apart: 4 -> 48, of which waited for: 4 -> 18; matrix products, arithmetic and copies ran while one was open for 0% -> 0% of each run, Pallas kernels for 0% -> 39%
where the time goes in v2:
time: 249 us; the launch traced here: 248 us
  Pallas kernels  99.7 us (40%)
  waiting for transfers between devices  80.1 us (32%)
  starting transfers between devices  57.3 us (23%)
  local copies, waits for them, and re-layouts  10.1 us (4%)
    ppermute x48, waiting for transfers between devices, exchange(): return lax.ppermute(value, 'tensor', pairs)  80.1 us
    pallas_call x8, Pallas kernels, project(): pl.pallas_call(kernel, out_shape=[bf16(features // 2, step)] * 2, grid_sp...  72.8 us
    ppermute x48, starting transfers between devices, exchange(): return lax.ppermute(value, 'tensor', pairs)  57.3 us
    pallas_call x48, Pallas kernels, call(): pl.pallas_call(run, out_shape=outs, grid=grid, in_specs=[pl.BlockSpec(mem...  26.9 us
    unnamed x25, local copies, waits for them, and re-layouts  9.39 us
  transfers between devices with their start and end apart: 48, of which 18 were waited for; matrix products, arithmetic and copies ran while one was open for 0% of the time, Pallas kernels for 39%

profile of v2, /device:TPU:0, one launch (start us, length us, event | category | flops | bytes accessed | tf_op | source)
XLA Modules:
  0.0 247.8 jit_solution(570236629685076612)
XLA Ops:
  4.2 3.1 %collective-permute-start = (bf16[1792,128]{1,0:T(8,128)(2,1)S(1)}, bf16[1792,128]{1,0:T(8,128)(2,1)S(1)}, u32[]{:S(2)}, u32[]{:S(2)}) collective-permute-start(bf16[1792,128]{1,0:T(8,128)(2,1)S(1)} %shard_map.64._.refs_1_), channel_id=1, source_target_pairs={{0,2},{1,3},{2,0},{3,1},{4,6},{5,7},{6,4},{7,5},{8,10},{9,11},{10,... | collective-permute-start | bytes 1376264 | tf_op jit(solution)/shard_map/ppermute | solution.py:76
  9.4 2.7 %collective-permute-start.1 = (bf16[1792,128]{1,0:T(8,128)(2,1)S(1)}, bf16[1792,128]{1,0:T(8,128)(2,1)}, u32[]{:S(2)}, u32[]{:S(2)}) collective-permute-start(bf16[1792,128]{1,0:T(8,128)(2,1)S(1)} %shard_map.65._.refs_1_), channel_id=1, source_target_pairs={{0,4},{1,5},{2,6},{3,7},{4,0},{5,1},{6,2},{7,3},{8,12},{9,13},{10,... | collective-permute-start | bytes 1376264 | tf_op jit(solution)/shard_map/ppermute | solution.py:76
  18.5 7.7 %collective-permute-done.refs_0_ = bf16[1792,128]{1,0:T(8,128)(2,1)S(1)} collective-permute-done((bf16[1792,128]{1,0:T(8,128)(2,1)S(1)}, bf16[1792,128]{1,0:T(8,128)(2,1)S(1)}, u32[]{:S(2)}, u32[]{:S(2)}) %collective-permute-start) | collective-permute-done | bytes 458784 | tf_op jit(solution)/shard_map/ppermute | solution.py:76
  46.8 2.5 %collective-permute-start.7 = (bf16[1792,128]{1,0:T(8,128)(2,1)S(1)}, bf16[1792,128]{1,0:T(8,128)(2,1)S(1)}, u32[]{:S(2)}, u32[]{:S(2)}) collective-permute-start(bf16[1792,128]{1,0:T(8,128)(2,1)S(1)} %shard_map.69._.refs_1_), channel_id=1, source_target_pairs={{0,2},{1,3},{2,0},{3,1},{4,6},{5,7},{6,4},{7,5},{8,10},{9,11},{10,... | collective-permute-start | bytes 1376264 | tf_op jit(solution)/shard_map/ppermute | solution.py:76
  52.5 8.6 %collective-permute-done.5.refs_0_ = bf16[1792,128]{1,0:T(8,128)(2,1)} collective-permute-done((bf16[1792,128]{1,0:T(8,128)(2,1)S(1)}, bf16[1792,128]{1,0:T(8,128)(2,1)}, u32[]{:S(2)}, u32[]{:S(2)}) %collective-permute-start.5) | collective-permute-done | bytes 458784 | tf_op jit(solution)/shard_map/ppermute | solution.py:76
  65.6 11.2 %collective-permute-done.7.refs_0_ = bf16[1792,128]{1,0:T(8,128)(2,1)S(1)} collective-permute-done((bf16[1792,128]{1,0:T(8,128)(2,1)S(1)}, bf16[1792,128]{1,0:T(8,128)(2,1)S(1)}, u32[]{:S(2)}, u32[]{:S(2)}) %collective-permute-start.7) | collective-permute-done | bytes 458784 | tf_op jit(solution)/shard_map/ppermute | solution.py:76
  79.4 2.5 %collective-permute-start.14 = (bf16[1792,128]{1,0:T(8,128)(2,1)S(1)}, bf16[1792,128]{1,0:T(8,128)(2,1)S(1)}, u32[]{:S(2)}, u32[]{:S(2)}) collective-permute-start(bf16[1792,128]{1,0:T(8,128)(2,1)S(1)} %shard_map.73._.refs_1_), channel_id=1, source_target_pairs={{0,2},{1,3},{2,0},{3,1},{4,6},{5,7},{6,4},{7,5},{8,10},{9,11},{10,... | collective-permute-start | bytes 1376264 | tf_op jit(solution)/shard_map/ppermute | solution.py:76
  82.0 11.9 %collective-permute-done.11.refs_0_ = bf16[1792,128]{1,0:T(8,128)(2,1)S(1)} collective-permute-done((bf16[1792,128]{1,0:T(8,128)(2,1)S(1)}, bf16[1792,128]{1,0:T(8,128)(2,1)S(1)}, u32[]{:S(2)}, u32[]{:S(2)}) %collective-permute-start.11) | collective-permute-done | bytes 458784 | tf_op jit(solution)/shard_map/ppermute | solution.py:76
  93.9 2.5 collective-permute-start.18
  96.6 9.1 %shard_map.82 = (bf16[2048,128]{1,0:T(8,128)(2,1)S(1)}, bf16[2048,128]{1,0:T(8,128)(2,1)S(1)}) custom-call(s32[8]{0:T(128)S(1)} %broadcast_xor_fusion.1.block_ref, bf16[1792,128]{1,0:T(8,128)(2,1)S(1)} %shard_map.81._.refs_1_, bf16[1792,128]{1,0:T(8,128)(2,1)S(1)} %collective-permute-done.10.partner_ref, bf16[1792,128]{1,0:T(8,128)(2,1)S(1)} %shard_map.76._.own_ref, ...), custom_call_target="tpu_custom_call" | custom-call | flops 1 | bytes 1 | tf_op jit(solution)/shard_map/pallas_call | solution.py:180
  110.2 2.5 %collective-permute-done.15.partner_ref = bf16[1792,128]{1,0:T(8,128)(2,1)S(1)} collective-permute-done((bf16[1792,128]{1,0:T(8,128)(2,1)S(1)}, bf16[1792,128]{1,0:T(8,128)(2,1)S(1)}, u32[]{:S(2)}, u32[]{:S(2)}) %collective-permute-start.15) | collective-permute-done | bytes 458784 | tf_op jit(solution)/shard_map/ppermute | solution.py:76
  112.7 9.1 %shard_map.87 = (bf16[2048,128]{1,0:T(8,128)(2,1)S(1)}, bf16[2048,128]{1,0:T(8,128)(2,1)S(1)}) custom-call(s32[8]{0:T(128)S(1)} %broadcast_xor_fusion.1.block_ref, bf16[1792,128]{1,0:T(8,128)(2,1)S(1)} %shard_map.86._.own_ref, bf16[1792,128]{1,0:T(8,128)(2,1)S(1)} %collective-permute-done.15.partner_ref, bf16[1792,128]{1,0:T(8,128)(2,1)S(1)} %shard_map.80._.own_ref, ...), custom_call_target="tpu_custom_call" | custom-call | flops 1 | bytes 1 | tf_op jit(solution)/shard_map/pallas_call | solution.py:180
  121.8 2.9 %collective-permute-start.20 = (bf16[2048,128]{1,0:T(8,128)(2,1)S(1)}, bf16[2048,128]{1,0:T(8,128)(2,1)S(1)}, u32[]{:S(2)}, u32[]{:S(2)}) collective-permute-start(bf16[2048,128]{1,0:T(8,128)(2,1)S(1)} %get-tuple-element.59), channel_id=1, source_target_pairs={{0,1},{1,0},{2,3},{3,2},{4,5},{5,4},{6,7},{7,6},{8,9},{9,8},{10,11... | collective-permute-start | bytes 1572872 | tf_op jit(solution)/shard_map/ppermute | solution.py:76
  125.5 2.4 collective-permute-start.22
  127.9 9.1 %shard_map.88 = (bf16[2048,128]{1,0:T(8,128)(2,1)S(1)}, bf16[2048,128]{1,0:T(8,128)(2,1)S(1)}) custom-call(s32[8]{0:T(128)S(1)} %broadcast_xor_fusion.1.block_ref, bf16[2048,128]{1,0:T(8,128)(2,1)S(1)} %get-tuple-element.54._.refs_1_, bf16[1792,128]{1,0:T(8,128)(2,1)S(1)} %collective-permute-done.16.partner_ref, bf16[1792,128]{1,0:T(8,128)(2,1)S(1)} %shard_map.83._.own_ref, ...), custom_call_target="tpu_custom_call" | custom-call | flops 1 | bytes 1 | tf_op jit(solution)/shard_map/pallas_call | solution.py:180
  138.9 9.1 %shard_map.91 = (bf16[2048,128]{1,0:T(8,128)(2,1)S(1)}, bf16[2048,128]{1,0:T(8,128)(2,1)S(1)}) custom-call(s32[8]{0:T(128)S(1)} %broadcast_xor_fusion.1.block_ref, bf16[1792,128]{1,0:T(8,128)(2,1)S(1)} %shard_map.90._.own_ref, bf16[1792,128]{1,0:T(8,128)(2,1)S(1)} %collective-permute-done.19.partner_ref, bf16[1792,128]{1,0:T(8,128)(2,1)S(1)} %shard_map.86._.own_ref, ...), custom_call_target="tpu_custom_call" | custom-call | flops 1 | bytes 1 | tf_op jit(solution)/shard_map/pallas_call | solution.py:180
  151.1 9.1 %shard_map.94 = (bf16[2048,128]{1,0:T(8,128)(2,1)S(1)}, bf16[2048,128]{1,0:T(8,128)(2,1)S(1)}) custom-call(s32[8]{0:T(128)S(1)} %broadcast_xor_fusion.block_ref, bf16[1792,128]{1,0:T(8,128)(2,1)S(1)} %shard_map.93._.own_ref, bf16[1792,128]{1,0:T(8,128)(2,1)S(1)} %collective-permute-done.22.partner_ref, bf16[1792,128]{1,0:T(8,128)(2,1)S(1)} %shard_map.85._.own_ref, ...), custom_call_target="tpu_custom_call" | custom-call | flops 1 | bytes 1 | tf_op jit(solution)/shard_map/pallas_call | solution.py:180
  166.3 9.1 %shard_map.97 = (bf16[2048,128]{1,0:T(8,128)(2,1)S(1)}, bf16[2048,128]{1,0:T(8,128)(2,1)S(1)}) custom-call(s32[8]{0:T(128)S(1)} %broadcast_xor_fusion.1.block_ref, bf16[1024,128]{1,0:T(8,128)(2,1)S(1)} %get-tuple-element.65._.refs_1_, bf16[1792,128]{1,0:T(8,128)(2,1)S(1)} %collective-permute-done.25.partner_ref, bf16[1792,128]{1,0:T(8,128)(2,1)S(1)} %shard_map.84._.own_ref, ...), custom_call_target="tpu_custom_call" | custom-call | flops 1 | bytes 1 | tf_op jit(solution)/shard_map/pallas_call | solution.py:180
  175.4 3.6 %collective-permute-done.27.refs_0_ = bf16[1024,128]{1,0:T(8,128)(2,1)S(1)} collective-permute-done((bf16[1024,128]{1,0:T(8,128)(2,1)S(1)}, bf16[1024,128]{1,0:T(8,128)(2,1)S(1)}, u32[]{:S(2)}, u32[]{:S(2)}) %collective-permute-start.27) | collective-permute-done | bytes 262176 | tf_op jit(solution)/shard_map/ppermute | solution.py:76
  179.0 9.1 %shard_map.98 = (bf16[2048,128]{1,0:T(8,128)(2,1)S(1)}, bf16[2048,128]{1,0:T(8,128)(2,1)S(1)}) custom-call(s32[8]{0:T(128)S(1)} %broadcast_xor_fusion.1.block_ref, bf16[2048,128]{1,0:T(8,128)(2,1)S(1)} %get-tuple-element.66._.refs_1_, bf16[1792,128]{1,0:T(8,128)(2,1)S(1)} %collective-permute-done.26.partner_ref, bf16[1792,128]{1,0:T(8,128)(2,1)S(1)} %shard_map.93._.own_ref, ...), custom_call_target="tpu_custom_call" | custom-call | flops 1 | bytes 1 | tf_op jit(solution)/shard_map/pallas_call | solution.py:180
  188.9 3.1 %collective-permute-done.30.partner_ref = bf16[1792,128]{1,0:T(8,128)(2,1)S(1)} collective-permute-done((bf16[1792,128]{1,0:T(8,128)(2,1)S(1)}, bf16[1792,128]{1,0:T(8,128)(2,1)S(1)}, u32[]{:S(2)}, u32[]{:S(2)}) %collective-permute-start.30) | collective-permute-done | bytes 458784 | tf_op jit(solution)/shard_map/ppermute | solution.py:76
  192.0 9.1 %shard_map.102 = (bf16[2048,128]{1,0:T(8,128)(2,1)S(1)}, bf16[2048,128]{1,0:T(8,128)(2,1)S(1)}) custom-call(s32[8]{0:T(128)S(1)} %broadcast_xor_fusion.1.block_ref, bf16[512,128]{1,0:T(8,128)(2,1)S(1)} %get-tuple-element.73._.refs_1_, bf16[1792,128]{1,0:T(8,128)(2,1)S(1)} %collective-permute-done.30.partner_ref, bf16[1792,128]{1,0:T(8,128)(2,1)S(1)} %shard_map.90._.own_ref, ...), custom_call_target="tpu_custom_call" | custom-call | flops 1 | bytes 1 | tf_op jit(solution)/shard_map/pallas_call | solution.py:180
  203.3 3.0 %collective-permute-start.34 = (bf16[512,128]{1,0:T(8,128)(2,1)S(1)}, bf16[512,128]{1,0:T(8,128)(2,1)S(1)}, u32[]{:S(2)}, u32[]{:S(2)}) collective-permute-start(bf16[512,128]{1,0:T(8,128)(2,1)S(1)} %get-tuple-element.81), channel_id=1, source_target_pairs={{0,4},{1,5},{2,6},{3,7},{4,0},{5,1},{6,2},{7,3},{8,12},{9,13},{10,... | collective-permute-start | bytes 393224 | tf_op jit(solution)/shard_map/ppermute | solution.py:76
  206.5 5.8 %collective-permute-done.34.refs_0_ = bf16[512,128]{1,0:T(8,128)(2,1)S(1)} collective-permute-done((bf16[512,128]{1,0:T(8,128)(2,1)S(1)}, bf16[512,128]{1,0:T(8,128)(2,1)S(1)}, u32[]{:S(2)}, u32[]{:S(2)}) %collective-permute-start.34) | collective-permute-done | bytes 131104 | tf_op jit(solution)/shard_map/ppermute | solution.py:76
  212.3 3.4 %collective-permute-start.36 = (bf16[512,128]{1,0:T(8,128)(2,1)S(1)}, bf16[512,128]{1,0:T(8,128)(2,1)S(1)}, u32[]{:S(2)}, u32[]{:S(2)}) collective-permute-start(bf16[512,128]{1,0:T(8,128)(2,1)S(1)} %get-tuple-element.84), channel_id=1, source_target_pairs={{0,4},{1,5},{2,6},{3,7},{4,0},{5,1},{6,2},{7,3},{8,12},{9,13},{10,... | collective-permute-start | bytes 393224 | tf_op jit(solution)/shard_map/ppermute | solution.py:76
  215.8 4.8 %collective-permute-done.36.refs_0_ = bf16[512,128]{1,0:T(8,128)(2,1)S(1)} collective-permute-done((bf16[512,128]{1,0:T(8,128)(2,1)S(1)}, bf16[512,128]{1,0:T(8,128)(2,1)S(1)}, u32[]{:S(2)}, u32[]{:S(2)}) %collective-permute-start.36) | collective-permute-done | bytes 131104 | tf_op jit(solution)/shard_map/ppermute | solution.py:76
  220.9 2.4 collective-permute-start.41
  223.3 5.7 %collective-permute-done.39.refs_0_ = bf16[512,128]{1,0:T(8,128)(2,1)S(1)} collective-permute-done((bf16[512,128]{1,0:T(8,128)(2,1)S(1)}, bf16[512,128]{1,0:T(8,128)(2,1)S(1)}, u32[]{:S(2)}, u32[]{:S(2)}) %collective-permute-start.39) | collective-permute-done | bytes 131104 | tf_op jit(solution)/shard_map/ppermute | solution.py:76
  229.3 3.8 %collective-permute-done.41.refs_0_ = bf16[1024,128]{1,0:T(8,128)(2,1)S(1)} collective-permute-done((bf16[1024,128]{1,0:T(8,128)(2,1)S(1)}, bf16[1024,128]{1,0:T(8,128)(2,1)S(1)}, u32[]{:S(2)}, u32[]{:S(2)}) %collective-permute-start.41) | collective-permute-done | bytes 262176 | tf_op jit(solution)/shard_map/ppermute | solution.py:76
  233.9 2.3 collective-permute-start.45
  240.4 2.7 %collective-permute-done.45.refs_0_ = bf16[512,128]{1,0:T(8,128)(2,1)S(1)} collective-permute-done((bf16[512,128]{1,0:T(8,128)(2,1)S(1)}, bf16[512,128]{1,0:T(8,128)(2,1)S(1)}, u32[]{:S(2)}, u32[]{:S(2)}) %collective-permute-start.45) | collective-permute-done | bytes 131104 | tf_op jit(solution)/shard_map/ppermute | solution.py:76
  243.2 2.7 %collective-permute-done.47.refs_0_ = bf16[512,128]{1,0:T(8,128)(2,1)S(1)} collective-permute-done((bf16[512,128]{1,0:T(8,128)(2,1)S(1)}, bf16[512,128]{1,0:T(8,128)(2,1)S(1)}, u32[]{:S(2)}, u32[]{:S(2)}) %collective-permute-start.47) | collective-permute-done | bytes 131104 | tf_op jit(solution)/shard_map/ppermute | solution.py:76
  (148 shorter events, 70.7 us)
Async XLA Ops:
  4.2 21.9 %collective-permute-start = (bf16[1792,128]{1,0:T(8,128)(2,1)S(1)}, bf16[1792,128]{1,0:T(8,128)(2,1)S(1)}, u32[]{:S(2)}, u32[]{:S(2)}) collective-permute-start(bf16[1792,128]{1,0:T(8,128)(2,1)S(1)} %shard_map.64._.refs_1_), channel_id=1, source_target_pairs={{0,2},{1,3},{2,0},{3,1},{4,6},{5,7},{6,4},{7,5},{8,10},{9,11},{10,... | collective-permute-start | bytes 1376264 | tf_op jit(solution)/shard_map/ppermute | solution.py:76
  9.4 27.5 %collective-permute-start.1 = (bf16[1792,128]{1,0:T(8,128)(2,1)S(1)}, bf16[1792,128]{1,0:T(8,128)(2,1)}, u32[]{:S(2)}, u32[]{:S(2)}) collective-permute-start(bf16[1792,128]{1,0:T(8,128)(2,1)S(1)} %shard_map.65._.refs_1_), channel_id=1, source_target_pairs={{0,4},{1,5},{2,6},{3,7},{4,0},{5,1},{6,2},{7,3},{8,12},{9,13},{10,... | collective-permute-start | bytes 1376264 | tf_op jit(solution)/shard_map/ppermute | solution.py:76
  14.2 26.6 %collective-permute-start.2 = (bf16[1792,128]{1,0:T(8,128)(2,1)S(1)}, bf16[1792,128]{1,0:T(8,128)(2,1)}, u32[]{:S(2)}, u32[]{:S(2)}) collective-permute-start(bf16[1792,128]{1,0:T(8,128)(2,1)S(1)} %shard_map.66._.refs_1_), channel_id=1, source_target_pairs={{0,1},{1,0},{2,3},{3,2},{4,5},{5,4},{6,7},{7,6},{8,9},{9,8},{10,11... | collective-permute-start | bytes 1376264 | tf_op jit(solution)/shard_map/ppermute | solution.py:76
  17.9 31.3 %collective-permute-start.3 = (bf16[1792,128]{1,0:T(8,128)(2,1)S(1)}, bf16[1792,128]{1,0:T(8,128)(2,1)}, u32[]{:S(2)}, u32[]{:S(2)}) collective-permute-start(bf16[1792,128]{1,0:T(8,128)(2,1)S(1)} %shard_map.67._.refs_1_), channel_id=1, source_target_pairs={{0,2},{1,3},{2,0},{3,1},{4,6},{5,7},{6,4},{7,5},{8,10},{9,11},{10,... | collective-permute-start | bytes 1376264 | tf_op jit(solution)/shard_map/ppermute | solution.py:76
  26.3 25.7 %collective-permute-start.4 = (bf16[1792,128]{1,0:T(8,128)(2,1)S(1)}, bf16[1792,128]{1,0:T(8,128)(2,1)}, u32[]{:S(2)}, u32[]{:S(2)}) collective-permute-start(bf16[1792,128]{1,0:T(8,128)(2,1)S(1)} %shard_map.68._.refs_1_), channel_id=1, source_target_pairs={{0,1},{1,0},{2,3},{3,2},{4,5},{5,4},{6,7},{7,6},{8,9},{9,8},{10,11... | collective-permute-start | bytes 1376264 | tf_op jit(solution)/shard_map/ppermute | solution.py:76
  40.2 20.9 %collective-permute-start.5 = (bf16[1792,128]{1,0:T(8,128)(2,1)S(1)}, bf16[1792,128]{1,0:T(8,128)(2,1)}, u32[]{:S(2)}, u32[]{:S(2)}) collective-permute-start(bf16[1792,128]{1,0:T(8,128)(2,1)S(1)} %shard_map.72._.refs_1_), channel_id=1, source_target_pairs={{0,4},{1,5},{2,6},{3,7},{4,0},{5,1},{6,2},{7,3},{8,12},{9,13},{10,... | collective-permute-start | bytes 1376264 | tf_op jit(solution)/shard_map/ppermute | solution.py:76
  46.8 30.1 %collective-permute-start.7 = (bf16[1792,128]{1,0:T(8,128)(2,1)S(1)}, bf16[1792,128]{1,0:T(8,128)(2,1)S(1)}, u32[]{:S(2)}, u32[]{:S(2)}) collective-permute-start(bf16[1792,128]{1,0:T(8,128)(2,1)S(1)} %shard_map.69._.refs_1_), channel_id=1, source_target_pairs={{0,2},{1,3},{2,0},{3,1},{4,6},{5,7},{6,4},{7,5},{8,10},{9,11},{10,... | collective-permute-start | bytes 1376264 | tf_op jit(solution)/shard_map/ppermute | solution.py:76
  50.4 28.2 %collective-permute-start.8 = (bf16[1792,128]{1,0:T(8,128)(2,1)S(1)}, bf16[1792,128]{1,0:T(8,128)(2,1)S(1)}, u32[]{:S(2)}, u32[]{:S(2)}) collective-permute-start(bf16[1792,128]{1,0:T(8,128)(2,1)S(1)} %shard_map.75._.refs_1_), channel_id=1, source_target_pairs={{0,1},{1,0},{2,3},{3,2},{4,5},{5,4},{6,7},{7,6},{8,9},{9,8},{10,11... | collective-permute-start | bytes 1376264 | tf_op jit(solution)/shard_map/ppermute | solution.py:76
  52.0 27.4 %collective-permute-start.9 = (bf16[1792,128]{1,0:T(8,128)(2,1)S(1)}, bf16[1792,128]{1,0:T(8,128)(2,1)S(1)}, u32[]{:S(2)}, u32[]{:S(2)}) collective-permute-start(bf16[1792,128]{1,0:T(8,128)(2,1)S(1)} %shard_map.70._.refs_1_), channel_id=1, source_target_pairs={{0,1},{1,0},{2,3},{3,2},{4,5},{5,4},{6,7},{7,6},{8,9},{9,8},{10,11... | collective-permute-start | bytes 1376264 | tf_op jit(solution)/shard_map/ppermute | solution.py:76
  61.1 32.8 %collective-permute-start.11 = (bf16[1792,128]{1,0:T(8,128)(2,1)S(1)}, bf16[1792,128]{1,0:T(8,128)(2,1)S(1)}, u32[]{:S(2)}, u32[]{:S(2)}) collective-permute-start(bf16[1792,128]{1,0:T(8,128)(2,1)S(1)} %shard_map.71._.refs_1_), channel_id=1, source_target_pairs={{0,2},{1,3},{2,0},{3,1},{4,6},{5,7},{6,4},{7,5},{8,10},{9,11},{10,... | collective-permute-start | bytes 1376264 | tf_op jit(solution)/shard_map/ppermute | solution.py:76
  62.3 31.6 %collective-permute-start.10 = (bf16[1792,128]{1,0:T(8,128)(2,1)S(1)}, bf16[1792,128]{1,0:T(8,128)(2,1)S(1)}, u32[]{:S(2)}, u32[]{:S(2)}) collective-permute-start(bf16[1792,128]{1,0:T(8,128)(2,1)S(1)} %shard_map.76._.own_ref), channel_id=1, source_target_pairs={{0,4},{1,5},{2,6},{3,7},{4,0},{5,1},{6,2},{7,3},{8,12},{9,13},{10,... | collective-permute-start | bytes 1376264 | tf_op jit(solution)/shard_map/ppermute | solution.py:76
  76.8 28.8 %collective-permute-start.12 = (bf16[1792,128]{1,0:T(8,128)(2,1)S(1)}, bf16[1792,128]{1,0:T(8,128)(2,1)S(1)}, u32[]{:S(2)}, u32[]{:S(2)}) collective-permute-start(bf16[1792,128]{1,0:T(8,128)(2,1)S(1)} %shard_map.77._.refs_1_), channel_id=1, source_target_pairs={{0,1},{1,0},{2,3},{3,2},{4,5},{5,4},{6,7},{7,6},{8,9},{9,8},{10,11... | collective-permute-start | bytes 1376264 | tf_op jit(solution)/shard_map/ppermute | solution.py:76
  78.6 28.8 %collective-permute-start.13 = (bf16[1792,128]{1,0:T(8,128)(2,1)S(1)}, bf16[1792,128]{1,0:T(8,128)(2,1)S(1)}, u32[]{:S(2)}, u32[]{:S(2)}) collective-permute-start(bf16[1792,128]{1,0:T(8,128)(2,1)S(1)} %shard_map.79._.refs_1_), channel_id=1, source_target_pairs={{0,1},{1,0},{2,3},{3,2},{4,5},{5,4},{6,7},{7,6},{8,9},{9,8},{10,11... | collective-permute-start | bytes 1376264 | tf_op jit(solution)/shard_map/ppermute | solution.py:76
  79.4 30.6 %collective-permute-start.14 = (bf16[1792,128]{1,0:T(8,128)(2,1)S(1)}, bf16[1792,128]{1,0:T(8,128)(2,1)S(1)}, u32[]{:S(2)}, u32[]{:S(2)}) collective-permute-start(bf16[1792,128]{1,0:T(8,128)(2,1)S(1)} %shard_map.73._.refs_1_), channel_id=1, source_target_pairs={{0,2},{1,3},{2,0},{3,1},{4,6},{5,7},{6,4},{7,5},{8,10},{9,11},{10,... | collective-permute-start | bytes 1376264 | tf_op jit(solution)/shard_map/ppermute | solution.py:76
  93.9 18.8 %collective-permute-start.15 = (bf16[1792,128]{1,0:T(8,128)(2,1)S(1)}, bf16[1792,128]{1,0:T(8,128)(2,1)S(1)}, u32[]{:S(2)}, u32[]{:S(2)}) collective-permute-start(bf16[1792,128]{1,0:T(8,128)(2,1)S(1)} %shard_map.80._.own_ref), channel_id=1, source_target_pairs={{0,4},{1,5},{2,6},{3,7},{4,0},{5,1},{6,2},{7,3},{8,12},{9,13},{10,... | collective-permute-start | bytes 1376264 | tf_op jit(solution)/shard_map/ppermute | solution.py:76
  93.9 30.9 %collective-permute-start.18 = (bf16[1792,128]{1,0:T(8,128)(2,1)S(1)}, bf16[1792,128]{1,0:T(8,128)(2,1)S(1)}, u32[]{:S(2)}, u32[]{:S(2)}) collective-permute-start(bf16[1792,128]{1,0:T(8,128)(2,1)S(1)} %shard_map.78._.refs_1_), channel_id=1, source_target_pairs={{0,2},{1,3},{2,0},{3,1},{4,6},{5,7},{6,4},{7,5},{8,10},{9,11},{10,... | collective-permute-start | bytes 1376264 | tf_op jit(solution)/shard_map/ppermute | solution.py:76
  105.7 31.7 %collective-permute-start.17 = (bf16[2048,128]{1,0:T(8,128)(2,1)S(1)}, bf16[2048,128]{1,0:T(8,128)(2,1)S(1)}, u32[]{:S(2)}, u32[]{:S(2)}) collective-permute-start(bf16[2048,128]{1,0:T(8,128)(2,1)S(1)} %get-tuple-element.56), channel_id=1, source_target_pairs={{0,1},{1,0},{2,3},{3,2},{4,5},{5,4},{6,7},{7,6},{8,9},{9,8},{10,11... | collective-permute-start | bytes 1572872 | tf_op jit(solution)/shard_map/ppermute | solution.py:76
  107.4 18.0 %collective-permute-start.16 = (bf16[1792,128]{1,0:T(8,128)(2,1)S(1)}, bf16[1792,128]{1,0:T(8,128)(2,1)S(1)}, u32[]{:S(2)}, u32[]{:S(2)}) collective-permute-start(bf16[1792,128]{1,0:T(8,128)(2,1)S(1)} %shard_map.83._.own_ref), channel_id=1, source_target_pairs={{0,1},{1,0},{2,3},{3,2},{4,5},{5,4},{6,7},{7,6},{8,9},{9,8},{10,11... | collective-permute-start | bytes 1376264 | tf_op jit(solution)/shard_map/ppermute | solution.py:76
  110.2 26.8 %collective-permute-start.19 = (bf16[1792,128]{1,0:T(8,128)(2,1)S(1)}, bf16[1792,128]{1,0:T(8,128)(2,1)S(1)}, u32[]{:S(2)}, u32[]{:S(2)}) collective-permute-start(bf16[1792,128]{1,0:T(8,128)(2,1)S(1)} %shard_map.86._.own_ref), channel_id=1, source_target_pairs={{0,4},{1,5},{2,6},{3,7},{4,0},{5,1},{6,2},{7,3},{8,12},{9,13},{10,... | collective-permute-start | bytes 1376264 | tf_op jit(solution)/shard_map/ppermute | solution.py:76
  121.8 26.2 %collective-permute-start.20 = (bf16[2048,128]{1,0:T(8,128)(2,1)S(1)}, bf16[2048,128]{1,0:T(8,128)(2,1)S(1)}, u32[]{:S(2)}, u32[]{:S(2)}) collective-permute-start(bf16[2048,128]{1,0:T(8,128)(2,1)S(1)} %get-tuple-element.59), channel_id=1, source_target_pairs={{0,1},{1,0},{2,3},{3,2},{4,5},{5,4},{6,7},{7,6},{8,9},{9,8},{10,11... | collective-permute-start | bytes 1572872 | tf_op jit(solution)/shard_map/ppermute | solution.py:76
  124.8 24.0 %collective-permute-start.21 = (bf16[1792,128]{1,0:T(8,128)(2,1)S(1)}, bf16[1792,128]{1,0:T(8,128)(2,1)S(1)}, u32[]{:S(2)}, u32[]{:S(2)}) collective-permute-start(bf16[1792,128]{1,0:T(8,128)(2,1)S(1)} %shard_map.81._.refs_1_), channel_id=1, source_target_pairs={{0,2},{1,3},{2,0},{3,1},{4,6},{5,7},{6,4},{7,5},{8,10},{9,11},{10,... | collective-permute-start | bytes 1376264 | tf_op jit(solution)/shard_map/ppermute | solution.py:76
  125.5 25.6 %collective-permute-start.22 = (bf16[1792,128]{1,0:T(8,128)(2,1)S(1)}, bf16[1792,128]{1,0:T(8,128)(2,1)S(1)}, u32[]{:S(2)}, u32[]{:S(2)}) collective-permute-start(bf16[1792,128]{1,0:T(8,128)(2,1)S(1)} %shard_map.85._.own_ref), channel_id=1, source_target_pairs={{0,4},{1,5},{2,6},{3,7},{4,0},{5,1},{6,2},{7,3},{8,12},{9,13},{10,... | collective-permute-start | bytes 1376264 | tf_op jit(solution)/shard_map/ppermute | solution.py:76
  137.0 26.9 %collective-permute-start.23 = (bf16[2048,128]{1,0:T(8,128)(2,1)S(1)}, bf16[2048,128]{1,0:T(8,128)(2,1)S(1)}, u32[]{:S(2)}, u32[]{:S(2)}) collective-permute-start(bf16[2048,128]{1,0:T(8,128)(2,1)S(1)} %get-tuple-element.62), channel_id=1, source_target_pairs={{0,1},{1,0},{2,3},{3,2},{4,5},{5,4},{6,7},{7,6},{8,9},{9,8},{10,11... | collective-permute-start | bytes 1572872 | tf_op jit(solution)/shard_map/ppermute | solution.py:76
  137.4 26.5 %collective-permute-start.25 = (bf16[1792,128]{1,0:T(8,128)(2,1)S(1)}, bf16[1792,128]{1,0:T(8,128)(2,1)S(1)}, u32[]{:S(2)}, u32[]{:S(2)}) collective-permute-start(bf16[1792,128]{1,0:T(8,128)(2,1)S(1)} %shard_map.84._.own_ref), channel_id=1, source_target_pairs={{0,2},{1,3},{2,0},{3,1},{4,6},{5,7},{6,4},{7,5},{8,10},{9,11},{10,... | collective-permute-start | bytes 1376264 | tf_op jit(solution)/shard_map/ppermute | solution.py:76
  149.2 29.8 %collective-permute-start.26 = (bf16[1792,128]{1,0:T(8,128)(2,1)S(1)}, bf16[1792,128]{1,0:T(8,128)(2,1)S(1)}, u32[]{:S(2)}, u32[]{:S(2)}) collective-permute-start(bf16[1792,128]{1,0:T(8,128)(2,1)S(1)} %shard_map.93._.own_ref), channel_id=1, source_target_pairs={{0,4},{1,5},{2,6},{3,7},{4,0},{5,1},{6,2},{7,3},{8,12},{9,13},{10,... | collective-permute-start | bytes 1376264 | tf_op jit(solution)/shard_map/ppermute | solution.py:76
  160.2 28.0 %collective-permute-start.28 = (bf16[2048,128]{1,0:T(8,128)(2,1)S(1)}, bf16[2048,128]{1,0:T(8,128)(2,1)S(1)}, u32[]{:S(2)}, u32[]{:S(2)}) collective-permute-start(bf16[2048,128]{1,0:T(8,128)(2,1)S(1)} %get-tuple-element.70), channel_id=1, source_target_pairs={{0,1},{1,0},{2,3},{3,2},{4,5},{5,4},{6,7},{7,6},{8,9},{9,8},{10,11... | collective-permute-start | bytes 1572872 | tf_op jit(solution)/shard_map/ppermute | solution.py:76
  164.0 28.0 %collective-permute-start.30 = (bf16[1792,128]{1,0:T(8,128)(2,1)S(1)}, bf16[1792,128]{1,0:T(8,128)(2,1)S(1)}, u32[]{:S(2)}, u32[]{:S(2)}) collective-permute-start(bf16[1792,128]{1,0:T(8,128)(2,1)S(1)} %shard_map.90._.own_ref), channel_id=1, source_target_pairs={{0,4},{1,5},{2,6},{3,7},{4,0},{5,1},{6,2},{7,3},{8,12},{9,13},{10,... | collective-permute-start | bytes 1376264 | tf_op jit(solution)/shard_map/ppermute | solution.py:76
  165.8 23.0 %collective-permute-start.29 = (bf16[1024,128]{1,0:T(8,128)(2,1)S(1)}, bf16[1024,128]{1,0:T(8,128)(2,1)S(1)}, u32[]{:S(2)}, u32[]{:S(2)}) collective-permute-start(bf16[1024,128]{1,0:T(8,128)(2,1)S(1)} %get-tuple-element.72), channel_id=1, source_target_pairs={{0,2},{1,3},{2,0},{3,1},{4,6},{5,7},{6,4},{7,5},{8,10},{9,11},{10,... | collective-permute-start | bytes 786440 | tf_op jit(solution)/shard_map/ppermute | solution.py:76
  179.0 27.3 %collective-permute-start.33 = (bf16[2048,128]{1,0:T(8,128)(2,1)S(1)}, bf16[2048,128]{1,0:T(8,128)(2,1)S(1)}, u32[]{:S(2)}, u32[]{:S(2)}) collective-permute-start(bf16[2048,128]{1,0:T(8,128)(2,1)S(1)} %get-tuple-element.79), channel_id=1, source_target_pairs={{0,1},{1,0},{2,3},{3,2},{4,5},{5,4},{6,7},{7,6},{8,9},{9,8},{10,11... | collective-permute-start | bytes 1572872 | tf_op jit(solution)/shard_map/ppermute | solution.py:76
  179.0 24.2 %collective-permute-start.31 = (bf16[1024,128]{1,0:T(8,128)(2,1)S(1)}, bf16[1024,128]{1,0:T(8,128)(2,1)S(1)}, u32[]{:S(2)}, u32[]{:S(2)}) collective-permute-start(bf16[1024,128]{1,0:T(8,128)(2,1)S(1)} %get-tuple-element.75), channel_id=1, source_target_pairs={{0,2},{1,3},{2,0},{3,1},{4,6},{5,7},{6,4},{7,5},{8,10},{9,11},{10,... | collective-permute-start | bytes 786440 | tf_op jit(solution)/shard_map/ppermute | solution.py:76
  201.1 19.6 %collective-permute-start.37 = (bf16[2048,128]{1,0:T(8,128)(2,1)S(1)}, bf16[2048,128]{1,0:T(8,128)(2,1)S(1)}, u32[]{:S(2)}, u32[]{:S(2)}) collective-permute-start(bf16[2048,128]{1,0:T(8,128)(2,1)S(1)} %get-tuple-element.85), channel_id=1, source_target_pairs={{0,1},{1,0},{2,3},{3,2},{4,5},{5,4},{6,7},{7,6},{8,9},{9,8},{10,11... | collective-permute-start | bytes 1572872 | tf_op jit(solution)/shard_map/ppermute | solution.py:76
  202.4 26.7 %collective-permute-start.40 = (bf16[2048,128]{1,0:T(8,128)(2,1)S(1)}, bf16[2048,128]{1,0:T(8,128)(2,1)S(1)}, u32[]{:S(2)}, u32[]{:S(2)}) collective-permute-start(bf16[2048,128]{1,0:T(8,128)(2,1)S(1)} %get-tuple-element.90), channel_id=1, source_target_pairs={{0,1},{1,0},{2,3},{3,2},{4,5},{5,4},{6,7},{7,6},{8,9},{9,8},{10,11... | collective-permute-start | bytes 1572872 | tf_op jit(solution)/shard_map/ppermute | solution.py:76
  (25 other events, 273.4 us)

commit v3 on v2

v3 whole, which is shorter than its diff:
```python
import math

import jax
import jax.numpy as jnp
import numpy as np
from jax import lax
from jax.experimental import pallas as pl
from jax.experimental.pallas import tpu as pltpu
from jax.sharding import PartitionSpec as P

SIZES = (1, 1, 1, 1, 1, 1, 1, 1)
EXCHANGE = (
    (100, 101, 102, 0), (1, 0, 2), (0, 100, 101, 102), (0, 1, 2), (0, 2, 1), (100, 101, 102, 0), (2, 0, 1), (0, 1, 2),
)
REDUCE = (
    (0, 1, 2), (0, 1, 2), (0, 1, 2), (1, 0, 2), (0, 1, 2), (0, 2, 1), (0, 1, 2), (0, 1, 2),
)
EVENTS = (
    5, 7, 6, 2, 0, 5, 6, 7, 2, 0, 1, 4, 6, 3, 7, 5, 1, 3, 7, 2, 5, 3, 1, 0,
    7, 6, 3, 4, 0, 6, 7, 2, 3, 0, 6, 5, 3, 4, 2, 5, 0, 1, 4, 2, 6, 0, 5, 4,
    2, 3, 7, 1, 4, 0, 4, 1, 2, 5, 1,
)
COSTS = (
    1, 1, 1, 1, 1, 1048421339, 1, 1,
    1, 1, 1048421339, 2096842679, 1, 1, 1048421339, 1,
    1, 1, 1, 2096842679, 1048421339, 4193685358, 1, 1,
    1048421339, 1, 2096842679, 1, 4193685358, 1048421339, 4193685358, 1048421339,
    1048421339, 1048421339, 1048421339, 1, 1, 1, 1, 1048421339,
    1, 1, 1, 1, 1048421339, 1048421339, 2096842679, 1,
    1048421339, 2096842679, 1, 1, 1, 1048421339, 1048421339, 1,
    1048421339, 1, 1,
)
VMEM = 16 * 1024 * 1024


def character(value, prime_order):
    residue = value % prime_order
    if residue == 0:
        return 0
    squares_list = [index * index % prime_order for index in range(1, prime_order)]
    return 1 if residue in squares_list else -1


def paley_matrix():
    prime_order = 13
    conference = np.zeros((14, 14))
    conference[0, 1:] = 1.0
    conference[1:, 0] = 1.0
    for row_index in range(prime_order):
        for col_index in range(prime_order):
            conference[row_index + 1, col_index + 1] = character(col_index - row_index, prime_order)
    first = np.array([[1.0, 1.0], [1.0, -1.0]])
    second = np.array([[1.0, -1.0], [-1.0, -1.0]])
    return np.kron(conference, first) + np.kron(np.eye(14), second)


def sylvester(order):
    matrix = np.ones((1, 1))
    basic = np.array([[1.0, 1.0], [1.0, -1.0]])
    while matrix.shape[0] < order:
        matrix = np.kron(basic, matrix)
    return matrix


def plan(levels):
    if levels == len(REDUCE[0]):
        return SIZES, EXCHANGE, REDUCE, zip(EVENTS, COSTS)
    plain = (tuple(range(levels)),) * 8
    stages = 2 * levels + 1
    turns = [turn - stage for turn in range(8 + stages) for stage in (*range(1, stages), 0)]
    turns = [chunk for chunk in turns if 0 <= chunk < 8]
    return (1,) * 8, plain, plain, [(chunk, 1) for chunk in turns]


RELAY = 100


def exchange(value, step):
    size = lax.axis_size("tensor")
    if step < RELAY:
        pairs = [(source, source ^ (1 << step)) for source in range(size)]
    else:
        ends = [(near, near ^ 2) for near in range(size) if (near >> 1 & 1) == (near >> 2 & 1)]
        middle = [(near, near ^ 6) for near in range(size) if (near >> 1 & 1) != (near >> 2 & 1)]
        pairs = (ends, middle, [(to, end) for end, to in ends])[step - RELAY]
    return lax.ppermute(value, "tensor", pairs)


HELD = pl.BlockSpec(memory_space=pltpu.VMEM)
AWAY = pl.BlockSpec(memory_space=pltpu.HBM)


def call(kernel, after, cost, operands, specs, outs, scratch=()):
    def run(_, *refs):
        kernel(*refs)

    return pl.pallas_call(
        run,
        out_shape=[jax.ShapeDtypeStruct(shape, jnp.bfloat16) for shape in outs],
        in_specs=[pl.BlockSpec(memory_space=pl.ANY), *specs],
        out_specs=[HELD] * len(outs),
        scratch_shapes=list(scratch),
        compiler_params=pltpu.CompilerParams(vmem_limit_bytes=VMEM),
        cost_estimate=pl.CostEstimate(flops=cost, bytes_accessed=1, transcendentals=0),
    )(after, *operands)


def wide(ref):
    return ref[...].astype(jnp.float32)


def activate(after, cost, gate, up, first, step):
    units = gate.shape[0]
    blocks = 2
    rows = units // blocks

    def kernel(gate_ref, up_ref, out_ref, gates, ups, arrived):
        copies = [
            [
                pltpu.make_async_copy(
                    ref.at[pl.ds(block * rows, rows), pl.ds(first, step)],
                    held.at[block],
                    arrived.at[which, block],
                )
                for which, (ref, held) in enumerate(((gate_ref, gates), (up_ref, ups)))
            ]
            for block in range(blocks)
        ]
        for pair in copies:
            for copy in pair:
                copy.start()
        for block, pair in enumerate(copies):
            for copy in pair:
                copy.wait()
            g = gates[block].astype(jnp.float32)
            u = ups[block].astype(jnp.float32)
            out_ref[pl.ds(block * rows, rows), :] = (
                0.5 * g * (1.0 + jnp.tanh(0.5 * g)) * u
            ).astype(jnp.bfloat16)

    held = pltpu.VMEM((blocks, rows, step), jnp.bfloat16)
    return call(
        kernel, after, cost, (gate, up), [AWAY, AWAY], [(units, step)],
        [held, held, pltpu.SemaphoreType.DMA((2, blocks))],
    )[0]


def bit_of(level):
    return lax.axis_index("tensor") >> level & 1


def sign_of(level):
    return (1 - 2 * bit_of(level)).astype(jnp.float32)


def joined(partner_ref, own_ref, before):
    if before < RELAY:
        total = wide(partner_ref) + sign_of(before) * wide(own_ref)
    else:
        middle = bit_of(1) != bit_of(2)
        total = jnp.where(middle, wide(own_ref), wide(partner_ref))
    return total.astype(jnp.bfloat16)


def rows_of(units):
    size = math.gcd(units, 256)
    return [pl.ds(first, size) for first in range(0, units, size)]


def mix(after, cost, partner, own, before):
    def kernel(partner_ref, own_ref, out_ref):
        for rows in rows_of(own.shape[0]):
            out_ref[rows] = joined(partner_ref.at[rows], own_ref.at[rows], before)

    return call(kernel, after, cost, (partner, own), [HELD, HELD], [own.shape])[0]


def relay_sums(after, cost, partner, own):
    units, step = own.shape

    def kernel(partner_ref, own_ref, out_ref):
        sign = -sign_of(2)
        for rows in rows_of(units):
            there, here = wide(partner_ref.at[rows]), wide(own_ref.at[rows])
            out_ref[rows] = (here + there).astype(jnp.bfloat16)
            below = pl.ds(units + rows.start, rows.size)
            out_ref[below] = (sign * (here - there)).astype(jnp.bfloat16)

    return call(kernel, after, cost, (partner, own), [HELD, HELD], [(2 * units, step)])[0]


def relay_results(after, cost, partner, own):
    units, step = own.shape[0] // 2, own.shape[1]

    def kernel(partner_ref, own_ref, away_ref, kept_ref):
        lower, sign = bit_of(2) == 0, sign_of(2)
        for rows in rows_of(units):
            below = pl.ds(units + rows.start, rows.size)
            first, second = [
                (wide(partner_ref.at[part]) + sign * wide(own_ref.at[part])).astype(jnp.bfloat16)
                for part in (rows, below)
            ]
            away_ref[rows] = jnp.where(lower, first, second)
            kept_ref[rows] = jnp.where(lower, second, first)

    return call(kernel, after, cost, (partner, own), [HELD, HELD], [(units, step)] * 2)


def project(after, cost, partner, own, before, factor, weight, order, scale):
    units, step = own.shape
    features = weight.shape[1]
    count = len(order)
    rows = features // count
    side = factor.shape[0]
    groups = units // side
    inner = side // 28

    def kernel(partner_ref, own_ref, factor_ref, weight_ref, given_ref, kept_ref):
        position = lax.axis_index("tensor")
        total = joined(partner_ref, own_ref, before).reshape(28, groups, inner, step)
        parts = [
            jnp.dot(
                factor_ref[...], total[:, group].reshape(side, step), preferred_element_type=jnp.float32
            )
            for group in range(groups)
        ]
        distance = 1
        while distance < groups:
            parts = [
                parts[index] + parts[index ^ distance]
                if not index & distance
                else parts[index ^ distance] - parts[index]
                for index in range(groups)
            ]
            distance *= 2
        parts = [(part * scale).astype(jnp.bfloat16).reshape(28, 1, inner, step) for part in parts]
        rotated = jnp.concatenate(parts, axis=1).reshape(units, step).T
        for index, relative in enumerate(order):
            first = pl.multiple_of((position ^ relative) * rows, rows)
            product = jnp.dot(
                rotated, weight_ref[:, pl.ds(first, rows)], preferred_element_type=jnp.float32
            ).astype(jnp.bfloat16)
            out_ref = given_ref if index < count // 2 else kept_ref
            out_ref[:, index % (count // 2) * rows : (index % (count // 2) + 1) * rows] = product

    return call(
        kernel, after, cost, (partner, own, factor, weight),
        [HELD, HELD, HELD, HELD], [(step, features // 2)] * 2,
    )


def add(after, cost, taken, kept):
    step, rows = kept.shape

    def kernel(taken_ref, kept_ref, out_ref):
        out_ref[...] = (wide(taken_ref) + wide(kept_ref)).astype(jnp.bfloat16).T

    return call(kernel, after, cost, (taken, kept), [HELD, HELD], [(rows, step)])[0]


def add_split(after, cost, taken, kept):
    step, half = kept.shape[0], kept.shape[1] // 2

    def kernel(taken_ref, kept_ref, given_ref, kept_out):
        total = (wide(taken_ref) + wide(kept_ref)).astype(jnp.bfloat16)
        kept_out[...] = total[:, :half]
        given_ref[...] = total[:, half:]

    return call(kernel, after, cost, (taken, kept), [HELD, HELD], [(step, half)] * 2)


def body(gate_pre, up_pre, down_weight):
    left, width, tokens = gate_pre.shape
    units = left * width
    features = down_weight.shape[-1]
    devices = lax.axis_size("tensor")
    levels = devices.bit_length() - 1
    scale = 1.0 / math.sqrt(units * devices)
    inner = min(width, 16)
    factor = jnp.asarray(np.kron(paley_matrix(), sylvester(inner)), jnp.bfloat16)
    weight = down_weight.reshape(units, features)
    gate = gate_pre.reshape(units, tokens)
    up = up_pre.reshape(units, tokens)

    def order_of(reduction):
        return sorted(
            range(devices),
            key=lambda r: (1 - (r >> reduction[0] & 1), *[r >> level & 1 for level in reduction[1:]]),
        )

    sizes, exchanges, reductions, turns = plan(levels)
    stages = [0] * len(sizes)
    state = [None] * len(sizes)
    outs = [None] * len(sizes)
    last = gate
    for chunk, cost in turns:
        stage = stages[chunk]
        stages[chunk] += 1
        steps, reduction = exchanges[chunk], reductions[chunk]
        if stage == 0:
            step = tokens // sum(sizes)
            first = sum(sizes[:chunk])
            last = activate(last, cost, gate, up, first * step, sizes[chunk] * step)
            state[chunk] = (exchange(last, steps[0]), last)
            continue
        partner, own = state[chunk]
        before = steps[min(stage, len(steps)) - 1]
        if stage < len(steps):
            if before == RELAY:
                away = last = relay_sums(last, cost, partner, own)
            elif before == RELAY + 1:
                away, last = relay_results(last, cost, partner, own)
            else:
                away = last = mix(last, cost, partner, own, before)
            state[chunk] = (exchange(away, steps[stage]), last)
        elif stage == len(steps):
            given, last = project(
                last, cost, partner, own, before, factor, weight, order_of(reduction), scale
            )
            state[chunk] = (exchange(given, reduction[0]), last)
        elif stage < len(steps) + levels:
            given, last = add_split(last, cost, partner, own)
            state[chunk] = (exchange(given, reduction[stage - len(steps)]), last)
        else:
            outs[chunk] = last = add(last, cost, partner, own)
    return jnp.concatenate(outs, axis=1)


def solution(mesh):
    in_specs = (P(None, "tensor", "dp"), P(None, "tensor", "dp"), P(None, "tensor", None))
    out_specs = P("tensor", "dp")
    return jax.shard_map(body, mesh=mesh, in_specs=in_specs, out_specs=out_specs, check_vma=False)
```

time: 249 us -> 239 us (0.960)
  Pallas kernels: 99.7 us -> 31.7 us
  waiting for transfers between devices: 80.1 us -> 136 us
  starting transfers between devices: 57.3 us -> 64 us
  local copies, waits for them, and re-layouts: 10.1 us -> 6 us
    pallas_call x56 -> x59, Pallas kernels: 99.7 us -> 31.7 us  [call(): pl.pallas_call(run, out_shape=[jax.ShapeDtypeStruct(shape, jnp.bfloat16)...]
    ppermute x48 -> x51, waiting for transfers between devices: 80.1 us -> 136 us  [exchange(): return lax.ppermute(value, 'tensor', pairs)]
    ppermute x48 -> x51, starting transfers between devices: 57.3 us -> 64 us  [exchange(): return lax.ppermute(value, 'tensor', pairs)]
    unnamed x25, local copies, waits for them, and re-layouts: 9.39 us -> 5.34 us
  transfers between devices with their start and end apart: 48 -> 51, of which waited for: 18 -> 23; matrix products, arithmetic and copies ran while one was open for 0% -> 0% of each run, Pallas kernels for 39% -> 13%
where the time goes in v3:
time: 239 us; the launch traced here: 238 us
  waiting for transfers between devices  136 us (57%)
  starting transfers between devices  64 us (27%)
  Pallas kernels  31.7 us (13%)
  local copies, waits for them, and re-layouts  6 us (3%)
    ppermute x51, waiting for transfers between devices, exchange(): return lax.ppermute(value, 'tensor', pairs)  136 us
    ppermute x51, starting transfers between devices, exchange(): return lax.ppermute(value, 'tensor', pairs)  64 us
    pallas_call x59, Pallas kernels, call(): pl.pallas_call(run, out_shape=[jax.ShapeDtypeStruct(shape, jnp.bfloat16)...  31.7 us
    unnamed x25, local copies, waits for them, and re-layouts  5.34 us
  transfers between devices with their start and end apart: 51, of which 23 were waited for; matrix products, arithmetic and copies ran while one was open for 0% of the time, Pallas kernels for 13%

profile of v3, /device:TPU:0, one launch (start us, length us, event | category | flops | bytes accessed | tf_op | source)
XLA Modules:
  0.0 238.3 jit_solution(3694185493140133732)
XLA Ops:
  4.6 5.0 %collective-permute-start = (bf16[1792,128]{1,0:T(8,128)(2,1)S(1)}, bf16[1792,128]{1,0:T(8,128)(2,1)S(1)}, u32[]{:S(2)}, u32[]{:S(2)}) collective-permute-start(bf16[1792,128]{1,0:T(8,128)(2,1)S(1)} %shard_map.46._.refs_1_), channel_id=1, source_target_pairs={{0,2},{1,3},{6,4},{7,5},{8,10},{9,11},{14,12},{15,13},{16,18},{17,... | collective-permute-start | bytes 1376264 | tf_op jit(solution)/shard_map/ppermute | solution.py:86
  14.2 4.6 %collective-permute-start.4 = (bf16[1792,128]{1,0:T(8,128)(2,1)S(1)}, bf16[1792,128]{1,0:T(8,128)(2,1)S(1)}, u32[]{:S(2)}, u32[]{:S(2)}) collective-permute-start(bf16[1792,128]{1,0:T(8,128)(2,1)S(1)} %shard_map.50._.refs_1_), channel_id=1, source_target_pairs={{0,2},{1,3},{6,4},{7,5},{8,10},{9,11},{14,12},{15,13},{16,18},{17,... | collective-permute-start | bytes 1376264 | tf_op jit(solution)/shard_map/ppermute | solution.py:86
  21.5 13.0 %collective-permute-done.1.refs_0_ = bf16[1792,128]{1,0:T(8,128)(2,1)S(1)} collective-permute-done((bf16[1792,128]{1,0:T(8,128)(2,1)S(1)}, bf16[1792,128]{1,0:T(8,128)(2,1)S(1)}, u32[]{:S(2)}, u32[]{:S(2)}) %collective-permute-start.1) | collective-permute-done | bytes 458784 | tf_op jit(solution)/shard_map/ppermute | solution.py:86
  36.7 3.5 %collective-permute-done.4.refs_0_ = bf16[1792,128]{1,0:T(8,128)(2,1)S(1)} collective-permute-done((bf16[1792,128]{1,0:T(8,128)(2,1)S(1)}, bf16[1792,128]{1,0:T(8,128)(2,1)S(1)}, u32[]{:S(2)}, u32[]{:S(2)}) %collective-permute-start.4) | collective-permute-done | bytes 458784 | tf_op jit(solution)/shard_map/ppermute | solution.py:86
  46.3 3.7 %collective-permute-done.6.refs_0_ = bf16[1792,128]{1,0:T(8,128)(2,1)S(1)} collective-permute-done((bf16[1792,128]{1,0:T(8,128)(2,1)S(1)}, bf16[1792,128]{1,0:T(8,128)(2,1)S(1)}, u32[]{:S(2)}, u32[]{:S(2)}) %collective-permute-start.6) | collective-permute-done | bytes 458784 | tf_op jit(solution)/shard_map/ppermute | solution.py:86
  50.1 3.6 %collective-permute-start.10 = (bf16[1792,128]{1,0:T(8,128)(2,1)S(1)}, bf16[1792,128]{1,0:T(8,128)(2,1)S(1)}, u32[]{:S(2)}, u32[]{:S(2)}) collective-permute-start(bf16[1792,128]{1,0:T(8,128)(2,1)S(1)} %shard_map.60._.refs_1_), channel_id=1, source_target_pairs={{0,4},{1,5},{2,6},{3,7},{4,0},{5,1},{6,2},{7,3},{8,12},{9,13},{10,... | collective-permute-start | bytes 1376264 | tf_op jit(solution)/shard_map/ppermute | solution.py:86
  56.9 8.1 %collective-permute-done.8.refs_0_ = bf16[1792,128]{1,0:T(8,128)(2,1)S(1)} collective-permute-done((bf16[1792,128]{1,0:T(8,128)(2,1)S(1)}, bf16[1792,128]{1,0:T(8,128)(2,1)S(1)}, u32[]{:S(2)}, u32[]{:S(2)}) %collective-permute-start.8) | collective-permute-done | bytes 458784 | tf_op jit(solution)/shard_map/ppermute | solution.py:86
  66.1 7.9 %collective-permute-done.10.refs_0_ = bf16[1792,128]{1,0:T(8,128)(2,1)S(1)} collective-permute-done((bf16[1792,128]{1,0:T(8,128)(2,1)S(1)}, bf16[1792,128]{1,0:T(8,128)(2,1)S(1)}, u32[]{:S(2)}, u32[]{:S(2)}) %collective-permute-start.10) | collective-permute-done | bytes 458784 | tf_op jit(solution)/shard_map/ppermute | solution.py:86
  74.1 2.7 %shard_map.64 = (bf16[128,2048]{1,0:T(8,128)(2,1)S(1)}, bf16[128,2048]{1,0:T(8,128)(2,1)S(1)}) custom-call(bf16[1792,128]{1,0:T(8,128)(2,1)S(1)} %shard_map.63._.refs_1_, bf16[1792,128]{1,0:T(8,128)(2,1)S(1)} %collective-permute-done.10.refs_0_, bf16[1792,128]{1,0:T(8,128)(2,1)S(1)} %shard_map.60._.refs_1_, bf16[448,448]{1,0:T(8,128)(2,1)S(1)} %copy-done.3, ...), custom_call_target="tpu_custom_call" | custom-call | flops 1 | bytes 1 | tf_op jit(solution)/shard_map/pallas_call | solution.py:97
  82.0 7.4 %collective-permute-done.13.refs_0_ = bf16[1792,128]{1,0:T(8,128)(2,1)S(1)} collective-permute-done((bf16[1792,128]{1,0:T(8,128)(2,1)S(1)}, bf16[1792,128]{1,0:T(8,128)(2,1)S(1)}, u32[]{:S(2)}, u32[]{:S(2)}) %collective-permute-start.13) | collective-permute-done | bytes 458784 | tf_op jit(solution)/shard_map/ppermute | solution.py:86
  89.5 3.6 %collective-permute-start.18 = (bf16[1792,128]{1,0:T(8,128)(2,1)S(1)}, bf16[1792,128]{1,0:T(8,128)(2,1)S(1)}, u32[]{:S(2)}, u32[]{:S(2)}) collective-permute-start(bf16[1792,128]{1,0:T(8,128)(2,1)S(1)} %shard_map.67._.refs_1_), channel_id=1, source_target_pairs={{0,4},{1,5},{2,6},{3,7},{4,0},{5,1},{6,2},{7,3},{8,12},{9,13},{10,... | collective-permute-start | bytes 1376264 | tf_op jit(solution)/shard_map/ppermute | solution.py:86
  96.4 7.8 %collective-permute-done.16.refs_0_ = bf16[128,2048]{1,0:T(8,128)(2,1)S(1)} collective-permute-done((bf16[128,2048]{1,0:T(8,128)(2,1)S(1)}, bf16[128,2048]{1,0:T(8,128)(2,1)S(1)}, u32[]{:S(2)}, u32[]{:S(2)}) %collective-permute-start.16) | collective-permute-done | bytes 524320 | tf_op jit(solution)/shard_map/ppermute | solution.py:86
  106.8 2.7 %shard_map.71 = (bf16[128,2048]{1,0:T(8,128)(2,1)S(1)}, bf16[128,2048]{1,0:T(8,128)(2,1)S(1)}) custom-call(bf16[128,1024]{1,0:T(8,128)(2,1)S(1)} %get-tuple-element.64._.refs_1_, bf16[1792,128]{1,0:T(8,128)(2,1)S(1)} %collective-permute-done.17.refs_0_, bf16[1792,128]{1,0:T(8,128)(2,1)S(1)} %shard_map.58._.refs_1_, bf16[448,448]{1,0:T(8,128)(2,1)S(1)} %copy-done.3, ...), custom_call_target="tpu_custom_call" | custom-call | flops 1 | bytes 1 | tf_op jit(solution)/shard_map/pallas_call | solution.py:97
  109.5 3.8 %collective-permute-done.18.refs_0_ = bf16[1792,128]{1,0:T(8,128)(2,1)S(1)} collective-permute-done((bf16[1792,128]{1,0:T(8,128)(2,1)S(1)}, bf16[1792,128]{1,0:T(8,128)(2,1)S(1)}, u32[]{:S(2)}, u32[]{:S(2)}) %collective-permute-start.18) | collective-permute-done | bytes 458784 | tf_op jit(solution)/shard_map/ppermute | solution.py:86
  114.8 2.7 %shard_map.72 = (bf16[128,2048]{1,0:T(8,128)(2,1)S(1)}, bf16[128,2048]{1,0:T(8,128)(2,1)S(1)}) custom-call(bf16[128,2048]{1,0:T(8,128)(2,1)S(1)} %get-tuple-element.65._.refs_1_, bf16[1792,128]{1,0:T(8,128)(2,1)S(1)} %collective-permute-done.18.refs_0_, bf16[1792,128]{1,0:T(8,128)(2,1)S(1)} %shard_map.67._.refs_1_, bf16[448,448]{1,0:T(8,128)(2,1)S(1)} %copy-done.3, ...), custom_call_target="tpu_custom_call" | custom-call | flops 2096842624 | bytes 1 | tf_op jit(solution)/shard_map/pallas_call | solution.py:97
  119.9 12.4 %collective-permute-done.21.refs_0_ = bf16[128,2048]{1,0:T(8,128)(2,1)S(1)} collective-permute-done((bf16[128,2048]{1,0:T(8,128)(2,1)S(1)}, bf16[128,2048]{1,0:T(8,128)(2,1)S(1)}, u32[]{:S(2)}, u32[]{:S(2)}) %collective-permute-start.21) | collective-permute-done | bytes 524320 | tf_op jit(solution)/shard_map/ppermute | solution.py:86
  134.0 3.6 %collective-permute-start.29 = (bf16[1792,128]{1,0:T(8,128)(2,1)S(1)}, bf16[1792,128]{1,0:T(8,128)(2,1)S(1)}, u32[]{:S(2)}, u32[]{:S(2)}) collective-permute-start(bf16[1792,128]{1,0:T(8,128)(2,1)S(1)} %shard_map.73._.refs_1_), channel_id=1, source_target_pairs={{0,4},{1,5},{2,6},{3,7},{4,0},{5,1},{6,2},{7,3},{8,12},{9,13},{10,... | collective-permute-start | bytes 1376264 | tf_op jit(solution)/shard_map/ppermute | solution.py:86
  139.5 3.5 %collective-permute-done.25.refs_0_ = bf16[1792,128]{1,0:T(8,128)(2,1)S(1)} collective-permute-done((bf16[1792,128]{1,0:T(8,128)(2,1)S(1)}, bf16[1792,128]{1,0:T(8,128)(2,1)S(1)}, u32[]{:S(2)}, u32[]{:S(2)}) %collective-permute-start.25) | collective-permute-done | bytes 458784 | tf_op jit(solution)/shard_map/ppermute | solution.py:86
  144.5 2.7 %shard_map.79 = (bf16[128,2048]{1,0:T(8,128)(2,1)S(1)}, bf16[128,2048]{1,0:T(8,128)(2,1)S(1)}) custom-call(bf16[128,1024]{1,0:T(8,128)(2,1)S(1)} %get-tuple-element.74._.refs_1_, bf16[1792,128]{1,0:T(8,128)(2,1)S(1)} %collective-permute-done.25.refs_0_, bf16[1792,128]{1,0:T(8,128)(2,1)S(1)} %shard_map.74._.refs_1_, bf16[448,448]{1,0:T(8,128)(2,1)S(1)} %copy-done.3, ...), custom_call_target="tpu_custom_call" | custom-call | flops 1048421312 | bytes 1 | tf_op jit(solution)/shard_map/pallas_call | solution.py:97
  147.2 8.3 %collective-permute-done.26.refs_0_ = bf16[128,1024]{1,0:T(8,128)(2,1)S(1)} collective-permute-done((bf16[128,1024]{1,0:T(8,128)(2,1)S(1)}, bf16[128,1024]{1,0:T(8,128)(2,1)S(1)}, u32[]{:S(2)}, u32[]{:S(2)}) %collective-permute-start.26) | collective-permute-done | bytes 262176 | tf_op jit(solution)/shard_map/ppermute | solution.py:86
  155.6 2.7 %shard_map.81 = (bf16[128,2048]{1,0:T(8,128)(2,1)S(1)}, bf16[128,2048]{1,0:T(8,128)(2,1)S(1)}) custom-call(bf16[128,512]{1,0:T(8,128)(2,1)S(1)} %get-tuple-element.77._.refs_1_, bf16[1792,128]{1,0:T(8,128)(2,1)S(1)} %collective-permute-done.27.refs_0_, bf16[1792,128]{1,0:T(8,128)(2,1)S(1)} %shard_map.66._.refs_1_, bf16[448,448]{1,0:T(8,128)(2,1)S(1)} %copy-done.3, ...), custom_call_target="tpu_custom_call" | custom-call | flops 1 | bytes 1 | tf_op jit(solution)/shard_map/pallas_call | solution.py:97
  161.7 14.2 %collective-permute-done.30.refs_0_ = bf16[1792,128]{1,0:T(8,128)(2,1)S(1)} collective-permute-done((bf16[1792,128]{1,0:T(8,128)(2,1)S(1)}, bf16[1792,128]{1,0:T(8,128)(2,1)S(1)}, u32[]{:S(2)}, u32[]{:S(2)}) %collective-permute-start.30) | collective-permute-done | bytes 458784 | tf_op jit(solution)/shard_map/ppermute | solution.py:86
  180.9 2.7 %shard_map.87 = (bf16[128,2048]{1,0:T(8,128)(2,1)S(1)}, bf16[128,2048]{1,0:T(8,128)(2,1)S(1)}) custom-call(bf16[128,1024]{1,0:T(8,128)(2,1)S(1)} %get-tuple-element.86._.refs_1_, bf16[1792,128]{1,0:T(8,128)(2,1)S(1)} %collective-permute-done.33.refs_0_, bf16[1792,128]{1,0:T(8,128)(2,1)S(1)} %shard_map.68._.refs_1_, bf16[448,448]{1,0:T(8,128)(2,1)S(1)} %copy-done.3, ...), custom_call_target="tpu_custom_call" | custom-call | flops 1 | bytes 1 | tf_op jit(solution)/shard_map/pallas_call | solution.py:97
  184.5 2.9 %shard_map.88 = (bf16[128,2048]{1,0:T(8,128)(2,1)S(1)}, bf16[128,2048]{1,0:T(8,128)(2,1)S(1)}) custom-call(bf16[128,2048]{1,0:T(8,128)(2,1)S(1)} %get-tuple-element.87._.refs_1_, bf16[1792,128]{1,0:T(8,128)(2,1)S(1)} %collective-permute-done.34.refs_0_, bf16[1792,128]{1,0:T(8,128)(2,1)S(1)} %shard_map.83._.refs_1_, bf16[448,448]{1,0:T(8,128)(2,1)S(1)} %copy-done.3, ...), custom_call_target="tpu_custom_call" | custom-call | flops 1 | bytes 1 | tf_op jit(solution)/shard_map/pallas_call | solution.py:97
  190.3 2.8 %collective-permute-done.35.refs_0_ = bf16[128,2048]{1,0:T(8,128)(2,1)S(1)} collective-permute-done((bf16[128,2048]{1,0:T(8,128)(2,1)S(1)}, bf16[128,2048]{1,0:T(8,128)(2,1)S(1)}, u32[]{:S(2)}, u32[]{:S(2)}) %collective-permute-start.35) | collective-permute-done | bytes 524320 | tf_op jit(solution)/shard_map/ppermute | solution.py:86
  194.2 11.1 %collective-permute-done.38.refs_0_ = bf16[128,1024]{1,0:T(8,128)(2,1)S(1)} collective-permute-done((bf16[128,1024]{1,0:T(8,128)(2,1)S(1)}, bf16[128,1024]{1,0:T(8,128)(2,1)S(1)}, u32[]{:S(2)}, u32[]{:S(2)}) %collective-permute-start.38) | collective-permute-done | bytes 262176 | tf_op jit(solution)/shard_map/ppermute | solution.py:86
  205.3 3.0 %collective-permute-start.45 = (bf16[128,512]{1,0:T(8,128)(2,1)S(1)}, bf16[128,512]{1,0:T(8,128)(2,1)S(1)}, u32[]{:S(2)}, u32[]{:S(2)}) collective-permute-start(bf16[128,512]{1,0:T(8,128)(2,1)S(1)} %get-tuple-element.106), channel_id=1, source_target_pairs={{0,4},{1,5},{2,6},{3,7},{4,0},{5,1},{6,2},{7,3},{8,12},{9,13},{10,... | collective-permute-start | bytes 393224 | tf_op jit(solution)/shard_map/ppermute | solution.py:86
  209.8 2.8 %collective-permute-done.41.refs_0_ = bf16[128,512]{1,0:T(8,128)(2,1)S(1)} collective-permute-done((bf16[128,512]{1,0:T(8,128)(2,1)S(1)}, bf16[128,512]{1,0:T(8,128)(2,1)S(1)}, u32[]{:S(2)}, u32[]{:S(2)}) %collective-permute-start.41) | collective-permute-done | bytes 131104 | tf_op jit(solution)/shard_map/ppermute | solution.py:86
  213.4 9.2 %collective-permute-done.44.refs_0_ = bf16[128,1024]{1,0:T(8,128)(2,1)S(1)} collective-permute-done((bf16[128,1024]{1,0:T(8,128)(2,1)S(1)}, bf16[128,1024]{1,0:T(8,128)(2,1)S(1)}, u32[]{:S(2)}, u32[]{:S(2)}) %collective-permute-start.44) | collective-permute-done | bytes 262176 | tf_op jit(solution)/shard_map/ppermute | solution.py:86
  226.1 3.7 %collective-permute-done.46.refs_0_ = bf16[128,512]{1,0:T(8,128)(2,1)S(1)} collective-permute-done((bf16[128,512]{1,0:T(8,128)(2,1)S(1)}, bf16[128,512]{1,0:T(8,128)(2,1)S(1)}, u32[]{:S(2)}, u32[]{:S(2)}) %collective-permute-start.46) | collective-permute-done | bytes 131104 | tf_op jit(solution)/shard_map/ppermute | solution.py:86
  230.1 2.7 %collective-permute-done.48.refs_0_ = bf16[128,512]{1,0:T(8,128)(2,1)S(1)} collective-permute-done((bf16[128,512]{1,0:T(8,128)(2,1)S(1)}, bf16[128,512]{1,0:T(8,128)(2,1)S(1)}, u32[]{:S(2)}, u32[]{:S(2)}) %collective-permute-start.48) | collective-permute-done | bytes 131104 | tf_op jit(solution)/shard_map/ppermute | solution.py:86
  233.0 3.3 %collective-permute-done.50.refs_0_ = bf16[128,512]{1,0:T(8,128)(2,1)S(1)} collective-permute-done((bf16[128,512]{1,0:T(8,128)(2,1)S(1)}, bf16[128,512]{1,0:T(8,128)(2,1)S(1)}, u32[]{:S(2)}, u32[]{:S(2)}) %collective-permute-start.50) | collective-permute-done | bytes 131104 | tf_op jit(solution)/shard_map/ppermute | solution.py:86
  (156 shorter events, 65.9 us)
Async XLA Ops:
  10.6 23.9 %collective-permute-start.1 = (bf16[1792,128]{1,0:T(8,128)(2,1)S(1)}, bf16[1792,128]{1,0:T(8,128)(2,1)S(1)}, u32[]{:S(2)}, u32[]{:S(2)}) collective-permute-start(bf16[1792,128]{1,0:T(8,128)(2,1)S(1)} %shard_map.48._.refs_1_), channel_id=1, source_target_pairs={{0,4},{1,5},{2,6},{3,7},{4,0},{5,1},{6,2},{7,3},{8,12},{9,13},{10,... | collective-permute-start | bytes 1376264 | tf_op jit(solution)/shard_map/ppermute | solution.py:86
  11.0 25.2 %collective-permute-start.2 = (bf16[1792,128]{1,0:T(8,128)(2,1)S(1)}, bf16[1792,128]{1,0:T(8,128)(2,1)S(1)}, u32[]{:S(2)}, u32[]{:S(2)}) collective-permute-start(bf16[1792,128]{1,0:T(8,128)(2,1)S(1)} %shard_map.47._.refs_1_), channel_id=1, source_target_pairs={{0,1},{1,0},{2,3},{3,2},{4,5},{5,4},{6,7},{7,6},{8,9},{9,8},{10,11... | collective-permute-start | bytes 1376264 | tf_op jit(solution)/shard_map/ppermute | solution.py:86
  13.1 23.4 %collective-permute-start.3 = (bf16[1792,128]{1,0:T(8,128)(2,1)S(1)}, bf16[1792,128]{1,0:T(8,128)(2,1)S(1)}, u32[]{:S(2)}, u32[]{:S(2)}) collective-permute-start(bf16[1792,128]{1,0:T(8,128)(2,1)S(1)} %shard_map.49._.refs_1_), channel_id=1, source_target_pairs={{0,1},{1,0},{2,3},{3,2},{4,5},{5,4},{6,7},{7,6},{8,9},{9,8},{10,11... | collective-permute-start | bytes 1376264 | tf_op jit(solution)/shard_map/ppermute | solution.py:86
  14.2 26.0 %collective-permute-start.4 = (bf16[1792,128]{1,0:T(8,128)(2,1)S(1)}, bf16[1792,128]{1,0:T(8,128)(2,1)S(1)}, u32[]{:S(2)}, u32[]{:S(2)}) collective-permute-start(bf16[1792,128]{1,0:T(8,128)(2,1)S(1)} %shard_map.50._.refs_1_), channel_id=1, source_target_pairs={{0,2},{1,3},{6,4},{7,5},{8,10},{9,11},{14,12},{15,13},{16,18},{17,... | collective-permute-start | bytes 1376264 | tf_op jit(solution)/shard_map/ppermute | solution.py:86
  20.7 34.5 %collective-permute-start.7 = (bf16[3584,128]{1,0:T(8,128)(2,1)S(1)}, bf16[3584,128]{1,0:T(8,128)(2,1)S(1)}, u32[]{:S(2)}, u32[]{:S(2)}) collective-permute-start(bf16[3584,128]{1,0:T(8,128)(2,1)S(1)} %shard_map.51._.refs_1_), channel_id=1, source_target_pairs={{2,4},{3,5},{4,2},{5,3},{10,12},{11,13},{12,10},{13,11},{18,20},{1... | collective-permute-start | bytes 2752520 | tf_op jit(solution)/shard_map/ppermute | solution.py:86
  40.9 24.0 %collective-permute-start.8 = (bf16[1792,128]{1,0:T(8,128)(2,1)S(1)}, bf16[1792,128]{1,0:T(8,128)(2,1)S(1)}, u32[]{:S(2)}, u32[]{:S(2)}) collective-permute-start(bf16[1792,128]{1,0:T(8,128)(2,1)S(1)} %shard_map.56._.refs_1_), channel_id=1, source_target_pairs={{0,2},{1,3},{2,0},{3,1},{4,6},{5,7},{6,4},{7,5},{8,10},{9,11},{10,... | collective-permute-start | bytes 1376264 | tf_op jit(solution)/shard_map/ppermute | solution.py:86
  44.7 20.4 %collective-permute-start.9 = (bf16[1792,128]{1,0:T(8,128)(2,1)S(1)}, bf16[1792,128]{1,0:T(8,128)(2,1)S(1)}, u32[]{:S(2)}, u32[]{:S(2)}) collective-permute-start(bf16[1792,128]{1,0:T(8,128)(2,1)S(1)} %shard_map.59._.refs_1_), channel_id=1, source_target_pairs={{0,1},{1,0},{2,3},{3,2},{4,5},{5,4},{6,7},{7,6},{8,9},{9,8},{10,11... | collective-permute-start | bytes 1376264 | tf_op jit(solution)/shard_map/ppermute | solution.py:86
  50.1 23.8 %collective-permute-start.10 = (bf16[1792,128]{1,0:T(8,128)(2,1)S(1)}, bf16[1792,128]{1,0:T(8,128)(2,1)S(1)}, u32[]{:S(2)}, u32[]{:S(2)}) collective-permute-start(bf16[1792,128]{1,0:T(8,128)(2,1)S(1)} %shard_map.60._.refs_1_), channel_id=1, source_target_pairs={{0,4},{1,5},{2,6},{3,7},{4,0},{5,1},{6,2},{7,3},{8,12},{9,13},{10,... | collective-permute-start | bytes 1376264 | tf_op jit(solution)/shard_map/ppermute | solution.py:86
  53.7 25.8 %collective-permute-start.11 = (bf16[1792,128]{1,0:T(8,128)(2,1)S(1)}, bf16[1792,128]{1,0:T(8,128)(2,1)S(1)}, u32[]{:S(2)}, u32[]{:S(2)}) collective-permute-start(bf16[1792,128]{1,0:T(8,128)(2,1)S(1)} %shard_map.54._.refs_1_), channel_id=1, source_target_pairs={{0,2},{1,3},{6,4},{7,5},{8,10},{9,11},{14,12},{15,13},{16,18},{17,... | collective-permute-start | bytes 1376264 | tf_op jit(solution)/shard_map/ppermute | solution.py:86
  55.6 25.7 %collective-permute-start.12 = (bf16[1792,128]{1,0:T(8,128)(2,1)S(1)}, bf16[1792,128]{1,0:T(8,128)(2,1)S(1)}, u32[]{:S(2)}, u32[]{:S(2)}) collective-permute-start(bf16[1792,128]{1,0:T(8,128)(2,1)S(1)} %get-tuple-element.61), channel_id=1, source_target_pairs={{2,0},{3,1},{4,6},{5,7},{10,8},{11,9},{12,14},{13,15},{18,16},{19,... | collective-permute-start | bytes 1376264 | tf_op jit(solution)/shard_map/ppermute | solution.py:86
  65.3 24.1 %collective-permute-start.13 = (bf16[1792,128]{1,0:T(8,128)(2,1)S(1)}, bf16[1792,128]{1,0:T(8,128)(2,1)S(1)}, u32[]{:S(2)}, u32[]{:S(2)}) collective-permute-start(bf16[1792,128]{1,0:T(8,128)(2,1)S(1)} %shard_map.63._.refs_1_), channel_id=1, source_target_pairs={{0,2},{1,3},{2,0},{3,1},{4,6},{5,7},{6,4},{7,5},{8,10},{9,11},{10,... | collective-permute-start | bytes 1376264 | tf_op jit(solution)/shard_map/ppermute | solution.py:86
  65.3 29.4 %collective-permute-start.15 = (bf16[3584,128]{1,0:T(8,128)(2,1)S(1)}, bf16[3584,128]{1,0:T(8,128)(2,1)S(1)}, u32[]{:S(2)}, u32[]{:S(2)}) collective-permute-start(bf16[3584,128]{1,0:T(8,128)(2,1)S(1)} %shard_map.55._.refs_1_), channel_id=1, source_target_pairs={{2,4},{3,5},{4,2},{5,3},{10,12},{11,13},{12,10},{13,11},{18,20},{1... | collective-permute-start | bytes 2752520 | tf_op jit(solution)/shard_map/ppermute | solution.py:86
  73.9 31.3 %collective-permute-start.17 = (bf16[1792,128]{1,0:T(8,128)(2,1)S(1)}, bf16[1792,128]{1,0:T(8,128)(2,1)S(1)}, u32[]{:S(2)}, u32[]{:S(2)}) collective-permute-start(bf16[1792,128]{1,0:T(8,128)(2,1)S(1)} %shard_map.58._.refs_1_), channel_id=1, source_target_pairs={{0,2},{1,3},{2,0},{3,1},{4,6},{5,7},{6,4},{7,5},{8,10},{9,11},{10,... | collective-permute-start | bytes 1376264 | tf_op jit(solution)/shard_map/ppermute | solution.py:86
  81.2 23.0 %collective-permute-start.16 = (bf16[128,2048]{1,0:T(8,128)(2,1)S(1)}, bf16[128,2048]{1,0:T(8,128)(2,1)S(1)}, u32[]{:S(2)}, u32[]{:S(2)}) collective-permute-start(bf16[128,2048]{1,0:T(8,128)(2,1)S(1)} %get-tuple-element.63), channel_id=1, source_target_pairs={{0,1},{1,0},{2,3},{3,2},{4,5},{5,4},{6,7},{7,6},{8,9},{9,8},{10,11... | collective-permute-start | bytes 1572872 | tf_op jit(solution)/shard_map/ppermute | solution.py:86
  89.5 23.8 %collective-permute-start.18 = (bf16[1792,128]{1,0:T(8,128)(2,1)S(1)}, bf16[1792,128]{1,0:T(8,128)(2,1)S(1)}, u32[]{:S(2)}, u32[]{:S(2)}) collective-permute-start(bf16[1792,128]{1,0:T(8,128)(2,1)S(1)} %shard_map.67._.refs_1_), channel_id=1, source_target_pairs={{0,4},{1,5},{2,6},{3,7},{4,0},{5,1},{6,2},{7,3},{8,12},{9,13},{10,... | collective-permute-start | bytes 1376264 | tf_op jit(solution)/shard_map/ppermute | solution.py:86
  93.1 24.4 %collective-permute-start.19 = (bf16[1792,128]{1,0:T(8,128)(2,1)S(1)}, bf16[1792,128]{1,0:T(8,128)(2,1)S(1)}, u32[]{:S(2)}, u32[]{:S(2)}) collective-permute-start(bf16[1792,128]{1,0:T(8,128)(2,1)S(1)} %shard_map.57._.refs_1_), channel_id=1, source_target_pairs={{0,1},{1,0},{2,3},{3,2},{4,5},{5,4},{6,7},{7,6},{8,9},{9,8},{10,11... | collective-permute-start | bytes 1376264 | tf_op jit(solution)/shard_map/ppermute | solution.py:86
  95.1 23.2 %collective-permute-start.20 = (bf16[1792,128]{1,0:T(8,128)(2,1)S(1)}, bf16[1792,128]{1,0:T(8,128)(2,1)S(1)}, u32[]{:S(2)}, u32[]{:S(2)}) collective-permute-start(bf16[1792,128]{1,0:T(8,128)(2,1)S(1)} %get-tuple-element.67), channel_id=1, source_target_pairs={{2,0},{3,1},{4,6},{5,7},{10,8},{11,9},{12,14},{13,15},{18,16},{19,... | collective-permute-start | bytes 1376264 | tf_op jit(solution)/shard_map/ppermute | solution.py:86
  104.2 33.4 %collective-permute-start.23 = (bf16[3584,128]{1,0:T(8,128)(2,1)S(1)}, bf16[3584,128]{1,0:T(8,128)(2,1)S(1)}, u32[]{:S(2)}, u32[]{:S(2)}) collective-permute-start(bf16[3584,128]{1,0:T(8,128)(2,1)S(1)} %shard_map.65._.refs_1_), channel_id=1, source_target_pairs={{2,4},{3,5},{4,2},{5,3},{10,12},{11,13},{12,10},{13,11},{18,20},{1... | collective-permute-start | bytes 2752520 | tf_op jit(solution)/shard_map/ppermute | solution.py:86
  105.2 50.3 %collective-permute-start.27 = (bf16[1792,128]{1,0:T(8,128)(2,1)S(1)}, bf16[1792,128]{1,0:T(8,128)(2,1)S(1)}, u32[]{:S(2)}, u32[]{:S(2)}) collective-permute-start(bf16[1792,128]{1,0:T(8,128)(2,1)S(1)} %shard_map.66._.refs_1_), channel_id=1, source_target_pairs={{0,1},{1,0},{2,3},{3,2},{4,5},{5,4},{6,7},{7,6},{8,9},{9,8},{10,11... | collective-permute-start | bytes 1376264 | tf_op jit(solution)/shard_map/ppermute | solution.py:86
  113.3 19.0 %collective-permute-start.21 = (bf16[128,2048]{1,0:T(8,128)(2,1)S(1)}, bf16[128,2048]{1,0:T(8,128)(2,1)S(1)}, u32[]{:S(2)}, u32[]{:S(2)}) collective-permute-start(bf16[128,2048]{1,0:T(8,128)(2,1)S(1)} %get-tuple-element.68), channel_id=1, source_target_pairs={{0,1},{1,0},{2,3},{3,2},{4,5},{5,4},{6,7},{7,6},{8,9},{9,8},{10,11... | collective-permute-start | bytes 1572872 | tf_op jit(solution)/shard_map/ppermute | solution.py:86
  118.3 19.8 %collective-permute-start.24 = (bf16[128,2048]{1,0:T(8,128)(2,1)S(1)}, bf16[128,2048]{1,0:T(8,128)(2,1)S(1)}, u32[]{:S(2)}, u32[]{:S(2)}) collective-permute-start(bf16[128,2048]{1,0:T(8,128)(2,1)S(1)} %get-tuple-element.73), channel_id=1, source_target_pairs={{0,2},{1,3},{2,0},{3,1},{4,6},{5,7},{6,4},{7,5},{8,10},{9,11},{10,... | collective-permute-start | bytes 1572872 | tf_op jit(solution)/shard_map/ppermute | solution.py:86
  134.0 26.5 %collective-permute-start.29 = (bf16[1792,128]{1,0:T(8,128)(2,1)S(1)}, bf16[1792,128]{1,0:T(8,128)(2,1)S(1)}, u32[]{:S(2)}, u32[]{:S(2)}) collective-permute-start(bf16[1792,128]{1,0:T(8,128)(2,1)S(1)} %shard_map.73._.refs_1_), channel_id=1, source_target_pairs={{0,4},{1,5},{2,6},{3,7},{4,0},{5,1},{6,2},{7,3},{8,12},{9,13},{10,... | collective-permute-start | bytes 1376264 | tf_op jit(solution)/shard_map/ppermute | solution.py:86
  137.6 17.9 %collective-permute-start.26 = (bf16[128,1024]{1,0:T(8,128)(2,1)S(1)}, bf16[128,1024]{1,0:T(8,128)(2,1)S(1)}, u32[]{:S(2)}, u32[]{:S(2)}) collective-permute-start(bf16[128,1024]{1,0:T(8,128)(2,1)S(1)} %get-tuple-element.76), channel_id=1, source_target_pairs={{0,2},{1,3},{2,0},{3,1},{4,6},{5,7},{6,4},{7,5},{8,10},{9,11},{10,... | collective-permute-start | bytes 786440 | tf_op jit(solution)/shard_map/ppermute | solution.py:86
  138.1 37.8 %collective-permute-start.30 = (bf16[1792,128]{1,0:T(8,128)(2,1)S(1)}, bf16[1792,128]{1,0:T(8,128)(2,1)S(1)}, u32[]{:S(2)}, u32[]{:S(2)}) collective-permute-start(bf16[1792,128]{1,0:T(8,128)(2,1)S(1)} %get-tuple-element.81), channel_id=1, source_target_pairs={{2,0},{3,1},{4,6},{5,7},{10,8},{11,9},{12,14},{13,15},{18,16},{19,... | collective-permute-start | bytes 1376264 | tf_op jit(solution)/shard_map/ppermute | solution.py:86
  158.3 20.9 %collective-permute-start.31 = (bf16[128,2048]{1,0:T(8,128)(2,1)S(1)}, bf16[128,2048]{1,0:T(8,128)(2,1)S(1)}, u32[]{:S(2)}, u32[]{:S(2)}) collective-permute-start(bf16[128,2048]{1,0:T(8,128)(2,1)S(1)} %get-tuple-element.83), channel_id=1, source_target_pairs={{0,1},{1,0},{2,3},{3,2},{4,5},{5,4},{6,7},{7,6},{8,9},{9,8},{10,11... | collective-permute-start | bytes 1572872 | tf_op jit(solution)/shard_map/ppermute | solution.py:86
  158.9 20.4 %collective-permute-start.32 = (bf16[128,2048]{1,0:T(8,128)(2,1)S(1)}, bf16[128,2048]{1,0:T(8,128)(2,1)S(1)}, u32[]{:S(2)}, u32[]{:S(2)}) collective-permute-start(bf16[128,2048]{1,0:T(8,128)(2,1)S(1)} %get-tuple-element.85), channel_id=1, source_target_pairs={{0,1},{1,0},{2,3},{3,2},{4,5},{5,4},{6,7},{7,6},{8,9},{9,8},{10,11... | collective-permute-start | bytes 1572872 | tf_op jit(solution)/shard_map/ppermute | solution.py:86
  160.4 20.5 %collective-permute-start.33 = (bf16[1792,128]{1,0:T(8,128)(2,1)S(1)}, bf16[1792,128]{1,0:T(8,128)(2,1)S(1)}, u32[]{:S(2)}, u32[]{:S(2)}) collective-permute-start(bf16[1792,128]{1,0:T(8,128)(2,1)S(1)} %shard_map.68._.refs_1_), channel_id=1, source_target_pairs={{0,4},{1,5},{2,6},{3,7},{4,0},{5,1},{6,2},{7,3},{8,12},{9,13},{10,... | collective-permute-start | bytes 1376264 | tf_op jit(solution)/shard_map/ppermute | solution.py:86
  160.6 23.8 %collective-permute-start.34 = (bf16[1792,128]{1,0:T(8,128)(2,1)S(1)}, bf16[1792,128]{1,0:T(8,128)(2,1)S(1)}, u32[]{:S(2)}, u32[]{:S(2)}) collective-permute-start(bf16[1792,128]{1,0:T(8,128)(2,1)S(1)} %shard_map.83._.refs_1_), channel_id=1, source_target_pairs={{0,2},{1,3},{2,0},{3,1},{4,6},{5,7},{6,4},{7,5},{8,10},{9,11},{10,... | collective-permute-start | bytes 1376264 | tf_op jit(solution)/shard_map/ppermute | solution.py:86
  187.4 17.9 %collective-permute-start.39 = (bf16[128,2048]{1,0:T(8,128)(2,1)S(1)}, bf16[128,2048]{1,0:T(8,128)(2,1)S(1)}, u32[]{:S(2)}, u32[]{:S(2)}) collective-permute-start(bf16[128,2048]{1,0:T(8,128)(2,1)S(1)} %get-tuple-element.96), channel_id=1, source_target_pairs={{0,1},{1,0},{2,3},{3,2},{4,5},{5,4},{6,7},{7,6},{8,9},{9,8},{10,11... | collective-permute-start | bytes 1572872 | tf_op jit(solution)/shard_map/ppermute | solution.py:86
  193.1 19.6 %collective-permute-start.42 = (bf16[128,512]{1,0:T(8,128)(2,1)S(1)}, bf16[128,512]{1,0:T(8,128)(2,1)S(1)}, u32[]{:S(2)}, u32[]{:S(2)}) collective-permute-start(bf16[128,512]{1,0:T(8,128)(2,1)S(1)} %get-tuple-element.101), channel_id=1, source_target_pairs={{0,4},{1,5},{2,6},{3,7},{4,0},{5,1},{6,2},{7,3},{8,12},{9,13},{10,... | collective-permute-start | bytes 393224 | tf_op jit(solution)/shard_map/ppermute | solution.py:86
  193.3 19.6 %collective-permute-start.43 = (bf16[128,2048]{1,0:T(8,128)(2,1)S(1)}, bf16[128,2048]{1,0:T(8,128)(2,1)S(1)}, u32[]{:S(2)}, u32[]{:S(2)}) collective-permute-start(bf16[128,2048]{1,0:T(8,128)(2,1)S(1)} %get-tuple-element.102), channel_id=1, source_target_pairs={{0,1},{1,0},{2,3},{3,2},{4,5},{5,4},{6,7},{7,6},{8,9},{9,8},{10,11... | collective-permute-start | bytes 1572872 | tf_op jit(solution)/shard_map/ppermute | solution.py:86
  205.3 20.7 %collective-permute-start.45 = (bf16[128,512]{1,0:T(8,128)(2,1)S(1)}, bf16[128,512]{1,0:T(8,128)(2,1)S(1)}, u32[]{:S(2)}, u32[]{:S(2)}) collective-permute-start(bf16[128,512]{1,0:T(8,128)(2,1)S(1)} %get-tuple-element.106), channel_id=1, source_target_pairs={{0,4},{1,5},{2,6},{3,7},{4,0},{5,1},{6,2},{7,3},{8,12},{9,13},{10,... | collective-permute-start | bytes 393224 | tf_op jit(solution)/shard_map/ppermute | solution.py:86
  (28 other events, 407.7 us)

commit v4 on v3

--- a/solution.py
+++ b/solution.py
@@ -10,25 +10,25 @@
 
 SIZES = (1, 1, 1, 1, 1, 1, 1, 1)
 EXCHANGE = (
-    (100, 101, 102, 0), (1, 0, 2), (0, 100, 101, 102), (0, 1, 2), (0, 2, 1), (100, 101, 102, 0), (2, 0, 1), (0, 1, 2),
+    (0, 100, 101, 102), (0, 1, 2), (100, 101, 102, 0), (1, 0, 2), (2, 0, 1), (0, 100, 101, 102), (2, 0, 1), (0, 1, 2),
 )
 REDUCE = (
-    (0, 1, 2), (0, 1, 2), (0, 1, 2), (1, 0, 2), (0, 1, 2), (0, 2, 1), (0, 1, 2), (0, 1, 2),
+    (0, 1, 2), (0, 1, 2), (0, 1, 2), (0, 1, 2), (0, 1, 2), (0, 2, 1), (0, 1, 2), (1, 0, 2),
 )
 EVENTS = (
-    5, 7, 6, 2, 0, 5, 6, 7, 2, 0, 1, 4, 6, 3, 7, 5, 1, 3, 7, 2, 5, 3, 1, 0,
-    7, 6, 3, 4, 0, 6, 7, 2, 3, 0, 6, 5, 3, 4, 2, 5, 0, 1, 4, 2, 6, 0, 5, 4,
-    2, 3, 7, 1, 4, 0, 4, 1, 2, 5, 1,
+    4, 2, 0, 3, 5, 6, 7, 0, 4, 2, 7, 5, 6, 3, 4, 0, 6, 7, 1, 2, 3, 1, 6, 4,
+    2, 6, 0, 3, 1, 2, 5, 3, 7, 2, 6, 3, 0, 5, 7, 0, 5, 4, 7, 2, 3, 1, 5, 0,
+    7, 2, 1, 6, 4, 5, 1, 0, 4, 5, 1,
 )
 COSTS = (
-    1, 1, 1, 1, 1, 1048421339, 1, 1,
-    1, 1, 1048421339, 2096842679, 1, 1, 1048421339, 1,
-    1, 1, 1, 2096842679, 1048421339, 4193685358, 1, 1,
-    1048421339, 1, 2096842679, 1, 4193685358, 1048421339, 4193685358, 1048421339,
-    1048421339, 1048421339, 1048421339, 1, 1, 1, 1, 1048421339,
-    1, 1, 1, 1, 1048421339, 1048421339, 2096842679, 1,
-    1048421339, 2096842679, 1, 1, 1, 1048421339, 1048421339, 1,
-    1048421339, 1, 1,
+    4193685358, 1, 1, 1, 4193685358, 1048421339, 1, 4193685358,
+    1, 1048421339, 1, 1, 1, 8387370716, 1048421339, 1,
+    4193685358, 1048421339, 2096842679, 8387370716, 2096842679, 8387370716, 1, 2096842679,
+    4193685358, 2096842679, 1, 1, 2096842679, 8387370716, 4193685358, 8387370716,
+    4193685358, 1, 1, 2096842679, 1048421339, 1, 1, 1,
+    2096842679, 1048421339, 1048421339, 1, 1, 4193685358, 4193685358, 8387370716,
+    1, 8387370716, 1, 8387370716, 4193685358, 1, 1, 2096842679,
+    1, 1, 1,
 )
 VMEM = 16 * 1024 * 1024
 
@@ -111,38 +111,15 @@
 
 def activate(after, cost, gate, up, first, step):
     units = gate.shape[0]
-    blocks = 2
-    rows = units // blocks
-
-    def kernel(gate_ref, up_ref, out_ref, gates, ups, arrived):
-        copies = [
-            [
-                pltpu.make_async_copy(
-                    ref.at[pl.ds(block * rows, rows), pl.ds(first, step)],
-                    held.at[block],
-                    arrived.at[which, block],
-                )
-                for which, (ref, held) in enumerate(((gate_ref, gates), (up_ref, ups)))
-            ]
-            for block in range(blocks)
-        ]
-        for pair in copies:
-            for copy in pair:
-                copy.start()
-        for block, pair in enumerate(copies):
-            for copy in pair:
-                copy.wait()
-            g = gates[block].astype(jnp.float32)
-            u = ups[block].astype(jnp.float32)
-            out_ref[pl.ds(block * rows, rows), :] = (
-                0.5 * g * (1.0 + jnp.tanh(0.5 * g)) * u
-            ).astype(jnp.bfloat16)
-
-    held = pltpu.VMEM((blocks, rows, step), jnp.bfloat16)
-    return call(
-        kernel, after, cost, (gate, up), [AWAY, AWAY], [(units, step)],
-        [held, held, pltpu.SemaphoreType.DMA((2, blocks))],
-    )[0]
+    gate, up = gate[:, first : first + step], up[:, first : first + step]
+    after = gate if after is None else after
+
+    def kernel(gate_ref, up_ref, out_ref):
+        for rows in rows_of(units):
+            g, u = wide(gate_ref.at[rows]), wide(up_ref.at[rows])
+            out_ref[rows] = (0.5 * g * (1.0 + jnp.tanh(0.5 * g)) * u).astype(jnp.bfloat16)
+
+    return call(kernel, after, cost, (gate, up), [HELD, HELD], [(units, step)])[0]
 
 
 def bit_of(level):
@@ -249,13 +226,31 @@
     )
 
 
-def add(after, cost, taken, kept):
+def add(after, cost, taken, kept, whole, first, tokens):
     step, rows = kept.shape
 
-    def kernel(taken_ref, kept_ref, out_ref):
-        out_ref[...] = (wide(taken_ref) + wide(kept_ref)).astype(jnp.bfloat16).T
-
-    return call(kernel, after, cost, (taken, kept), [HELD, HELD], [(rows, step)])[0]
+    def kernel(_, taken_ref, kept_ref, *refs):
+        whole_ref, token_ref, block, done = refs[-4:]
+        block[...] = (wide(taken_ref) + wide(kept_ref)).astype(jnp.bfloat16).T
+        token_ref[...] = jnp.zeros_like(token_ref)
+        copy = pltpu.make_async_copy(block, whole_ref.at[:, pl.ds(first, step)], done)
+        copy.start()
+        copy.wait()
+
+    more = () if whole is None else (whole,)
+    return pl.pallas_call(
+        kernel,
+        out_shape=[
+            jax.ShapeDtypeStruct((rows, tokens), jnp.bfloat16),
+            jax.ShapeDtypeStruct((16, 128), jnp.bfloat16),
+        ],
+        in_specs=[pl.BlockSpec(memory_space=pl.ANY), HELD, HELD, *[AWAY for _ in more]],
+        out_specs=[AWAY, HELD],
+        scratch_shapes=[pltpu.VMEM((rows, step), jnp.bfloat16), pltpu.SemaphoreType.DMA(())],
+        input_output_aliases={3: 0} if more else {},
+        compiler_params=pltpu.CompilerParams(vmem_limit_bytes=VMEM),
+        cost_estimate=pl.CostEstimate(flops=cost, bytes_accessed=1, transcendentals=0),
+    )(after, taken, kept, *more)
 
 
 def add_split(after, cost, taken, kept):
@@ -291,8 +286,7 @@
     sizes, exchanges, reductions, turns = plan(levels)
     stages = [0] * len(sizes)
     state = [None] * len(sizes)
-    outs = [None] * len(sizes)
-    last = gate
+    whole = last = None
     for chunk, cost in turns:
         stage = stages[chunk]
         stages[chunk] += 1
@@ -301,6 +295,8 @@
             step = tokens // sum(sizes)
             first = sum(sizes[:chunk])
             last = activate(last, cost, gate, up, first * step, sizes[chunk] * step)
+            if stages.count(0) == len(sizes) - 1:
+                gate, up, last = lax.optimization_barrier((gate, up, last))
             state[chunk] = (exchange(last, steps[0]), last)
             continue
         partner, own = state[chunk]
@@ -322,8 +318,9 @@
             given, last = add_split(last, cost, partner, own)
             state[chunk] = (exchange(given, reduction[stage - len(steps)]), last)
         else:
-            outs[chunk] = last = add(last, cost, partner, own)
-    return jnp.concatenate(outs, axis=1)
+            first = sum(sizes[:chunk]) * (tokens // sum(sizes))
+            whole, last = add(last, cost, partner, own, whole, first, tokens)
+    return whole
 
 
 def solution(mesh):

time: 239 us -> 229 us (0.958)
  waiting for transfers between devices: 136 us -> 124 us
  Pallas kernels: 31.7 us -> 35.1 us
    ppermute x51, waiting for transfers between devices: 136 us -> 124 us  [exchange(): return lax.ppermute(value, 'tensor', pairs)]
    pallas_call x0 -> x8, Pallas kernels: none -> 6.62 us  [add(): pl.pallas_call(kernel, out_shape=[jax.ShapeDtypeStruct((rows, tokens), jn...]
    unnamed x25 -> x14, local copies, waits for them, and re-layouts: 5.34 us -> 0.04 us
    slice x0 -> x3, local copies, waits for them, and re-layouts: none -> 3.66 us  [activate(): gate, up = (gate[:, first:first + step], up[:, first:first + step])]
    pallas_call x59 -> x51, Pallas kernels: 31.7 us -> 28.5 us  [call(): pl.pallas_call(run, out_shape=[jax.ShapeDtypeStruct(shape, jnp.bfloat16)...]
  transfers between devices with their start and end apart: 51 -> 51, of which waited for: 23 -> 29; matrix products, arithmetic and copies ran while one was open for 0% -> 1% of each run, Pallas kernels for 13% -> 15%
where the time goes in v4:
time: 229 us
  waiting for transfers between devices  124 us (54%)
  starting transfers between devices  65.3 us (29%)
  Pallas kernels  35.1 us (15%)
  local copies, waits for them, and re-layouts  3.71 us (2%)
    ppermute x51, waiting for transfers between devices, exchange(): return lax.ppermute(value, 'tensor', pairs)  124 us
    ppermute x51, starting transfers between devices, exchange(): return lax.ppermute(value, 'tensor', pairs)  65.3 us
    pallas_call x51, Pallas kernels, call(): pl.pallas_call(run, out_shape=[jax.ShapeDtypeStruct(shape, jnp.bfloat16)...  28.5 us
    pallas_call x8, Pallas kernels, add(): pl.pallas_call(kernel, out_shape=[jax.ShapeDtypeStruct((rows, tokens), jn...  6.62 us
  transfers between devices with their start and end apart: 51, of which 29 were waited for; matrix products, arithmetic and copies ran while one was open for 1% of the time, Pallas kernels for 15%

profile of v4, /device:TPU:0, one launch (start us, length us, event | category | flops | bytes accessed | tf_op | source)
XLA Modules:
  0.0 228.6 jit_solution(12543486770728614787)
XLA Ops:
  2.4 4.1 %collective-permute-start.1 = (bf16[1792,128]{1,0:T(8,128)(2,1)S(1)}, bf16[1792,128]{1,0:T(8,128)(2,1)S(1)}, u32[]{:S(2)}, u32[]{:S(2)}) collective-permute-start(bf16[1792,128]{1,0:T(8,128)(2,1)S(1)} %shard_map.46._.refs_1_), channel_id=1, source_target_pairs={{0,4},{1,5},{2,6},{3,7},{4,0},{5,1},{6,2},{7,3},{8,12},{9,13},{10,... | collective-permute-start | bytes 1376264 | tf_op jit(solution)/shard_map/ppermute | solution.py:86
  8.3 3.8 %collective-permute-start.2 = (bf16[1792,128]{1,0:T(8,128)(2,1)S(1)}, bf16[1792,128]{1,0:T(8,128)(2,1)S(1)}, u32[]{:S(2)}, u32[]{:S(2)}) collective-permute-start(bf16[1792,128]{1,0:T(8,128)(2,1)S(1)} %shard_map.47._.refs_1_), channel_id=1, source_target_pairs={{0,2},{1,3},{6,4},{7,5},{8,10},{9,11},{14,12},{15,13},{16,18},{17,... | collective-permute-start | bytes 1376264 | tf_op jit(solution)/shard_map/ppermute | solution.py:86
  15.8 10.0 %collective-permute-done.refs_0_ = bf16[1792,128]{1,0:T(8,128)(2,1)S(1)} collective-permute-done((bf16[1792,128]{1,0:T(8,128)(2,1)S(1)}, bf16[1792,128]{1,0:T(8,128)(2,1)S(1)}, u32[]{:S(2)}, u32[]{:S(2)}) %collective-permute-start) | collective-permute-done | bytes 458784 | tf_op jit(solution)/shard_map/ppermute | solution.py:86
  25.8 2.7 %collective-permute-done.1.refs_0_ = bf16[1792,128]{1,0:T(8,128)(2,1)S(1)} collective-permute-done((bf16[1792,128]{1,0:T(8,128)(2,1)S(1)}, bf16[1792,128]{1,0:T(8,128)(2,1)S(1)}, u32[]{:S(2)}, u32[]{:S(2)}) %collective-permute-start.1) | collective-permute-done | bytes 458784 | tf_op jit(solution)/shard_map/ppermute | solution.py:86
  31.2 14.2 %collective-permute-done.3.refs_0_ = bf16[1792,128]{1,0:T(8,128)(2,1)S(1)} collective-permute-done((bf16[1792,128]{1,0:T(8,128)(2,1)S(1)}, bf16[1792,128]{1,0:T(8,128)(2,1)S(1)}, u32[]{:S(2)}, u32[]{:S(2)}) %collective-permute-start.3) | collective-permute-done | bytes 458784 | tf_op jit(solution)/shard_map/ppermute | solution.py:86
  49.8 5.5 %collective-permute-done.7.refs_0_ = bf16[1792,128]{1,0:T(8,128)(2,1)S(1)} collective-permute-done((bf16[1792,128]{1,0:T(8,128)(2,1)S(1)}, bf16[1792,128]{1,0:T(8,128)(2,1)S(1)}, u32[]{:S(2)}, u32[]{:S(2)}) %collective-permute-start.7) | collective-permute-done | bytes 458784 | tf_op jit(solution)/shard_map/ppermute | solution.py:86
  60.4 4.7 %collective-permute-done.9.refs_0_ = bf16[1792,128]{1,0:T(8,128)(2,1)S(1)} collective-permute-done((bf16[1792,128]{1,0:T(8,128)(2,1)S(1)}, bf16[1792,128]{1,0:T(8,128)(2,1)S(1)}, u32[]{:S(2)}, u32[]{:S(2)}) %collective-permute-start.9) | collective-permute-done | bytes 458784 | tf_op jit(solution)/shard_map/ppermute | solution.py:86
  72.3 2.6 %collective-permute-done.12.refs_0_ = bf16[1792,128]{1,0:T(8,128)(2,1)S(1)} collective-permute-done((bf16[1792,128]{1,0:T(8,128)(2,1)S(1)}, bf16[1792,128]{1,0:T(8,128)(2,1)S(1)}, u32[]{:S(2)}, u32[]{:S(2)}) %collective-permute-start.12) | collective-permute-done | bytes 458784 | tf_op jit(solution)/shard_map/ppermute | solution.py:86
  76.6 6.7 %collective-permute-done.13.refs_0_ = bf16[1792,128]{1,0:T(8,128)(2,1)S(1)} collective-permute-done((bf16[1792,128]{1,0:T(8,128)(2,1)S(1)}, bf16[1792,128]{1,0:T(8,128)(2,1)S(1)}, u32[]{:S(2)}, u32[]{:S(2)}) %collective-permute-start.13) | collective-permute-done | bytes 458784 | tf_op jit(solution)/shard_map/ppermute | solution.py:86
  84.1 3.1 %collective-permute-done.14.refs_0_ = bf16[1792,128]{1,0:T(8,128)(2,1)S(1)} collective-permute-done((bf16[1792,128]{1,0:T(8,128)(2,1)S(1)}, bf16[1792,128]{1,0:T(8,128)(2,1)S(1)}, u32[]{:S(2)}, u32[]{:S(2)}) %collective-permute-start.14) | collective-permute-done | bytes 458784 | tf_op jit(solution)/shard_map/ppermute | solution.py:86
  89.7 2.7 %shard_map.68 = (bf16[128,2048]{1,0:T(8,128)(2,1)S(1)}, bf16[128,2048]{1,0:T(8,128)(2,1)S(1)}) custom-call(bf16[1792,128]{1,0:T(8,128)(2,1)S(1)} %shard_map.67._.refs_1_, bf16[1792,128]{1,0:T(8,128)(2,1)S(1)} %collective-permute-done.14.refs_0_, bf16[1792,128]{1,0:T(8,128)(2,1)S(1)} %shard_map.62._.refs_1_, bf16[448,448]{1,0:T(8,128)(2,1)S(1)} %copy-done, ...), custom_call_target="tpu_custom_call" | custom-call | flops 1 | bytes 1 | tf_op jit(solution)/shard_map/pallas_call | solution.py:97
  94.0 2.7 %shard_map.69 = (bf16[128,2048]{1,0:T(8,128)(2,1)S(1)}, bf16[128,2048]{1,0:T(8,128)(2,1)S(1)}) custom-call(bf16[128,2048]{1,0:T(8,128)(2,1)S(1)} %get-tuple-element.81._.refs_1_, bf16[1792,128]{1,0:T(8,128)(2,1)S(1)} %collective-permute-done.15.refs_0_, bf16[1792,128]{1,0:T(8,128)(2,1)S(1)} %shard_map.60._.refs_1_, bf16[448,448]{1,0:T(8,128)(2,1)S(1)} %copy-done, ...), custom_call_target="tpu_custom_call" | custom-call | flops 2096842624 | bytes 1 | tf_op jit(solution)/shard_map/pallas_call | solution.py:97
  97.4 9.6 %collective-permute-done.17.refs_0_ = bf16[128,2048]{1,0:T(8,128)(2,1)S(1)} collective-permute-done((bf16[128,2048]{1,0:T(8,128)(2,1)S(1)}, bf16[128,2048]{1,0:T(8,128)(2,1)S(1)}, u32[]{:S(2)}, u32[]{:S(2)}) %collective-permute-start.17) | collective-permute-done | bytes 524320 | tf_op jit(solution)/shard_map/ppermute | solution.py:86
  109.8 4.7 %collective-permute-done.19.refs_0_ = bf16[1792,128]{1,0:T(8,128)(2,1)S(1)} collective-permute-done((bf16[1792,128]{1,0:T(8,128)(2,1)S(1)}, bf16[1792,128]{1,0:T(8,128)(2,1)S(1)}, u32[]{:S(2)}, u32[]{:S(2)}) %collective-permute-start.19) | collective-permute-done | bytes 458784 | tf_op jit(solution)/shard_map/ppermute | solution.py:86
  114.5 2.7 %shard_map.73 = (bf16[128,2048]{1,0:T(8,128)(2,1)S(1)}, bf16[128,2048]{1,0:T(8,128)(2,1)S(1)}) custom-call(bf16[1792,128]{1,0:T(8,128)(2,1)S(1)} %get-tuple-element.86._.refs_1_, bf16[1792,128]{1,0:T(8,128)(2,1)S(1)} %collective-permute-done.19.refs_0_, bf16[1792,128]{1,0:T(8,128)(2,1)S(1)} %shard_map.66._.refs_1_, bf16[448,448]{1,0:T(8,128)(2,1)S(1)} %copy-done, ...), custom_call_target="tpu_custom_call" | custom-call | flops 1 | bytes 1 | tf_op jit(solution)/shard_map/pallas_call | solution.py:97
  120.5 2.7 %shard_map.75 = (bf16[128,2048]{1,0:T(8,128)(2,1)S(1)}, bf16[128,2048]{1,0:T(8,128)(2,1)S(1)}) custom-call(bf16[1792,128]{1,0:T(8,128)(2,1)S(1)} %shard_map.74._.refs_1_, bf16[1792,128]{1,0:T(8,128)(2,1)S(1)} %collective-permute-done.21.refs_0_, bf16[1792,128]{1,0:T(8,128)(2,1)S(1)} %shard_map.70._.refs_1_, bf16[448,448]{1,0:T(8,128)(2,1)S(1)} %copy-done, ...), custom_call_target="tpu_custom_call" | custom-call | flops 8387370496 | bytes 1 | tf_op jit(solution)/shard_map/pallas_call | solution.py:97
  124.0 5.5 %collective-permute-done.23.refs_0_ = bf16[128,2048]{1,0:T(8,128)(2,1)S(1)} collective-permute-done((bf16[128,2048]{1,0:T(8,128)(2,1)S(1)}, bf16[128,2048]{1,0:T(8,128)(2,1)S(1)}, u32[]{:S(2)}, u32[]{:S(2)}) %collective-permute-start.23) | collective-permute-done | bytes 524320 | tf_op jit(solution)/shard_map/ppermute | solution.py:86
  134.0 2.7 %shard_map.78 = (bf16[128,2048]{1,0:T(8,128)(2,1)S(1)}, bf16[128,2048]{1,0:T(8,128)(2,1)S(1)}) custom-call(bf16[128,1024]{1,0:T(8,128)(2,1)S(1)} %get-tuple-element.90._.refs_1_, bf16[1792,128]{1,0:T(8,128)(2,1)S(1)} %collective-permute-done.24.refs_0_, bf16[1792,128]{1,0:T(8,128)(2,1)S(1)} %shard_map.63._.refs_1_, bf16[448,448]{1,0:T(8,128)(2,1)S(1)} %copy-done, ...), custom_call_target="tpu_custom_call" | custom-call | flops 4193685248 | bytes 1 | tf_op jit(solution)/shard_map/pallas_call | solution.py:97
  137.7 8.8 %collective-permute-done.27.refs_0_ = bf16[128,1024]{1,0:T(8,128)(2,1)S(1)} collective-permute-done((bf16[128,1024]{1,0:T(8,128)(2,1)S(1)}, bf16[128,1024]{1,0:T(8,128)(2,1)S(1)}, u32[]{:S(2)}, u32[]{:S(2)}) %collective-permute-start.27) | collective-permute-done | bytes 262176 | tf_op jit(solution)/shard_map/ppermute | solution.py:86
  146.6 2.7 %shard_map.82 = (bf16[128,2048]{1,0:T(8,128)(2,1)S(1)}, bf16[128,2048]{1,0:T(8,128)(2,1)S(1)}) custom-call(bf16[128,512]{1,0:T(8,128)(2,1)S(1)} %get-tuple-element.97._.kept_ref, bf16[1792,128]{1,0:T(8,128)(2,1)S(1)} %collective-permute-done.28.refs_0_, bf16[1792,128]{1,0:T(8,128)(2,1)S(1)} %get-tuple-element.86._.refs_1_, bf16[448,448]{1,0:T(8,128)(2,1)S(1)} %copy-done, ...), custom_call_target="tpu_custom_call" | custom-call | flops 1048421312 | bytes 1 | tf_op jit(solution)/shard_map/pallas_call | solution.py:97
  153.4 6.9 %collective-permute-start.37 = (bf16[1792,128]{1,0:T(8,128)(2,1)S(1)}, bf16[1792,128]{1,0:T(8,128)(2,1)S(1)}, u32[]{:S(2)}, u32[]{:S(2)}) collective-permute-start(bf16[1792,128]{1,0:T(8,128)(2,1)S(1)} %shard_map.74._.refs_1_), channel_id=1, source_target_pairs={{0,4},{1,5},{2,6},{3,7},{4,0},{5,1},{6,2},{7,3},{8,12},{9,13},{10,... | collective-permute-start | bytes 1376264 | tf_op jit(solution)/shard_map/ppermute | solution.py:86
  160.3 5.6 %collective-permute-done.30.refs_0_ = bf16[128,2048]{1,0:T(8,128)(2,1)S(1)} collective-permute-done((bf16[128,2048]{1,0:T(8,128)(2,1)S(1)}, bf16[128,2048]{1,0:T(8,128)(2,1)S(1)}, u32[]{:S(2)}, u32[]{:S(2)}) %collective-permute-start.30) | collective-permute-done | bytes 524320 | tf_op jit(solution)/shard_map/ppermute | solution.py:86
  166.0 3.0 %collective-permute-start.36 = (bf16[128,512]{1,0:T(8,128)(2,1)S(1)}, bf16[128,512]{1,0:T(8,128)(2,1)S(1)}, u32[]{:S(2)}, u32[]{:S(2)}) collective-permute-start(bf16[128,512]{1,0:T(8,128)(2,1)S(1)} %get-tuple-element.113), channel_id=1, source_target_pairs={{0,4},{1,5},{2,6},{3,7},{4,0},{5,1},{6,2},{7,3},{8,12},{9,13},{10,... | collective-permute-start | bytes 393224 | tf_op jit(solution)/shard_map/ppermute | solution.py:86
  169.1 10.9 %collective-permute-done.32.refs_0_ = bf16[1792,128]{1,0:T(8,128)(2,1)S(1)} collective-permute-done((bf16[1792,128]{1,0:T(8,128)(2,1)S(1)}, bf16[1792,128]{1,0:T(8,128)(2,1)S(1)}, u32[]{:S(2)}, u32[]{:S(2)}) %collective-permute-start.32) | collective-permute-done | bytes 458784 | tf_op jit(solution)/shard_map/ppermute | solution.py:86
  181.0 2.7 %shard_map.86 = (bf16[128,2048]{1,0:T(8,128)(2,1)S(1)}, bf16[128,2048]{1,0:T(8,128)(2,1)S(1)}) custom-call(bf16[128,1024]{1,0:T(8,128)(2,1)S(1)} %get-tuple-element.104._.refs_1_, bf16[1792,128]{1,0:T(8,128)(2,1)S(1)} %collective-permute-done.32.refs_0_, bf16[1792,128]{1,0:T(8,128)(2,1)S(1)} %get-tuple-element.100._.refs_1_, bf16[448,448]{1,0:T(8,128)(2,1)S(1)} %copy-done, ...), custom_call_target="tpu_custom_call" | custom-call | flops 2096842624 | bytes 1 | tf_op jit(solution)/shard_map/pallas_call | solution.py:97
  190.4 2.6 %collective-permute-start.41 = (bf16[128,512]{1,0:T(8,128)(2,1)S(1)}, bf16[128,512]{1,0:T(8,128)(2,1)S(1)}, u32[]{:S(2)}, u32[]{:S(2)}) collective-permute-start(bf16[128,512]{1,0:T(8,128)(2,1)S(1)} %get-tuple-element.123), channel_id=1, source_target_pairs={{0,4},{1,5},{2,6},{3,7},{4,0},{5,1},{6,2},{7,3},{8,12},{9,13},{10,... | collective-permute-start | bytes 393224 | tf_op jit(solution)/shard_map/ppermute | solution.py:86
  192.9 2.7 %shard_map.91 = (bf16[128,2048]{1,0:T(8,128)(2,1)S(1)}, bf16[128,2048]{1,0:T(8,128)(2,1)S(1)}) custom-call(bf16[16,128]{1,0:T(8,128)(2,1)S(1)} %get-tuple-element.114._, bf16[1792,128]{1,0:T(8,128)(2,1)S(1)} %collective-permute-done.37.refs_0_, bf16[1792,128]{1,0:T(8,128)(2,1)S(1)} %shard_map.74._.refs_1_, bf16[448,448]{1,0:T(8,128)(2,1)S(1)} %copy-done, ...), custom_call_target="tpu_custom_call" | custom-call | flops 4193685248 | bytes 1 | tf_op jit(solution)/shard_map/pallas_call | solution.py:97
  195.6 2.8 %collective-permute-done.38.refs_0_ = bf16[128,2048]{1,0:T(8,128)(2,1)S(1)} collective-permute-done((bf16[128,2048]{1,0:T(8,128)(2,1)S(1)}, bf16[128,2048]{1,0:T(8,128)(2,1)S(1)}, u32[]{:S(2)}, u32[]{:S(2)}) %collective-permute-start.38) | collective-permute-done | bytes 524320 | tf_op jit(solution)/shard_map/ppermute | solution.py:86
  199.8 2.6 %collective-permute-done.40.taken_ref = bf16[128,512]{1,0:T(8,128)(2,1)S(1)} collective-permute-done((bf16[128,512]{1,0:T(8,128)(2,1)S(1)}, bf16[128,512]{1,0:T(8,128)(2,1)S(1)}, u32[]{:S(2)}, u32[]{:S(2)}) %collective-permute-start.40) | collective-permute-done | bytes 131104 | tf_op jit(solution)/shard_map/ppermute | solution.py:86
  203.2 2.7 %collective-permute-done.41.taken_ref = bf16[128,512]{1,0:T(8,128)(2,1)S(1)} collective-permute-done((bf16[128,512]{1,0:T(8,128)(2,1)S(1)}, bf16[128,512]{1,0:T(8,128)(2,1)S(1)}, u32[]{:S(2)}, u32[]{:S(2)}) %collective-permute-start.41) | collective-permute-done | bytes 131104 | tf_op jit(solution)/shard_map/ppermute | solution.py:86
  210.6 3.1 %collective-permute-done.44.refs_0_ = bf16[128,1024]{1,0:T(8,128)(2,1)S(1)} collective-permute-done((bf16[128,1024]{1,0:T(8,128)(2,1)S(1)}, bf16[128,1024]{1,0:T(8,128)(2,1)S(1)}, u32[]{:S(2)}, u32[]{:S(2)}) %collective-permute-start.44) | collective-permute-done | bytes 262176 | tf_op jit(solution)/shard_map/ppermute | solution.py:86
  215.9 4.7 %collective-permute-done.46.refs_0_ = bf16[128,1024]{1,0:T(8,128)(2,1)S(1)} collective-permute-done((bf16[128,1024]{1,0:T(8,128)(2,1)S(1)}, bf16[128,1024]{1,0:T(8,128)(2,1)S(1)}, u32[]{:S(2)}, u32[]{:S(2)}) %collective-permute-start.46) | collective-permute-done | bytes 262176 | tf_op jit(solution)/shard_map/ppermute | solution.py:86
  (147 shorter events, 75.3 us)
Async XLA Ops:
  2.4 26.1 %collective-permute-start.1 = (bf16[1792,128]{1,0:T(8,128)(2,1)S(1)}, bf16[1792,128]{1,0:T(8,128)(2,1)S(1)}, u32[]{:S(2)}, u32[]{:S(2)}) collective-permute-start(bf16[1792,128]{1,0:T(8,128)(2,1)S(1)} %shard_map.46._.refs_1_), channel_id=1, source_target_pairs={{0,4},{1,5},{2,6},{3,7},{4,0},{5,1},{6,2},{7,3},{8,12},{9,13},{10,... | collective-permute-start | bytes 1376264 | tf_op jit(solution)/shard_map/ppermute | solution.py:86
  8.3 22.6 %collective-permute-start.2 = (bf16[1792,128]{1,0:T(8,128)(2,1)S(1)}, bf16[1792,128]{1,0:T(8,128)(2,1)S(1)}, u32[]{:S(2)}, u32[]{:S(2)}) collective-permute-start(bf16[1792,128]{1,0:T(8,128)(2,1)S(1)} %shard_map.47._.refs_1_), channel_id=1, source_target_pairs={{0,2},{1,3},{6,4},{7,5},{8,10},{9,11},{14,12},{15,13},{16,18},{17,... | collective-permute-start | bytes 1376264 | tf_op jit(solution)/shard_map/ppermute | solution.py:86
  14.3 32.6 %collective-permute-start.4 = (bf16[1792,128]{1,0:T(8,128)(2,1)S(1)}, bf16[1792,128]{1,0:T(8,128)(2,1)S(1)}, u32[]{:S(2)}, u32[]{:S(2)}) collective-permute-start(bf16[1792,128]{1,0:T(8,128)(2,1)S(1)} %shard_map.50._.refs_1_), channel_id=1, source_target_pairs={{0,1},{1,0},{2,3},{3,2},{4,5},{5,4},{6,7},{7,6},{8,9},{9,8},{10,11... | collective-permute-start | bytes 1376264 | tf_op jit(solution)/shard_map/ppermute | solution.py:86
  15.1 32.0 %collective-permute-start.5 = (bf16[1792,128]{1,0:T(8,128)(2,1)S(1)}, bf16[1792,128]{1,0:T(8,128)(2,1)S(1)}, u32[]{:S(2)}, u32[]{:S(2)}) collective-permute-start(bf16[1792,128]{1,0:T(8,128)(2,1)S(1)} %shard_map.51._.refs_1_), channel_id=1, source_target_pairs={{0,4},{1,5},{2,6},{3,7},{4,0},{5,1},{6,2},{7,3},{8,12},{9,13},{10,... | collective-permute-start | bytes 1376264 | tf_op jit(solution)/shard_map/ppermute | solution.py:86
  25.8 22.3 %collective-permute-start.6 = (bf16[1792,128]{1,0:T(8,128)(2,1)S(1)}, bf16[1792,128]{1,0:T(8,128)(2,1)S(1)}, u32[]{:S(2)}, u32[]{:S(2)}) collective-permute-start(bf16[1792,128]{1,0:T(8,128)(2,1)S(1)} %shard_map.49._.refs_1_), channel_id=1, source_target_pairs={{0,2},{1,3},{2,0},{3,1},{4,6},{5,7},{6,4},{7,5},{8,10},{9,11},{10,... | collective-permute-start | bytes 1376264 | tf_op jit(solution)/shard_map/ppermute | solution.py:86
  28.5 17.0 %collective-permute-start.3 = (bf16[1792,128]{1,0:T(8,128)(2,1)S(1)}, bf16[1792,128]{1,0:T(8,128)(2,1)S(1)}, u32[]{:S(2)}, u32[]{:S(2)}) collective-permute-start(bf16[1792,128]{1,0:T(8,128)(2,1)S(1)} %shard_map.52._.refs_1_), channel_id=1, source_target_pairs={{0,1},{1,0},{2,3},{3,2},{4,5},{5,4},{6,7},{7,6},{8,9},{9,8},{10,11... | collective-permute-start | bytes 1376264 | tf_op jit(solution)/shard_map/ppermute | solution.py:86
  30.9 24.4 %collective-permute-start.7 = (bf16[1792,128]{1,0:T(8,128)(2,1)S(1)}, bf16[1792,128]{1,0:T(8,128)(2,1)S(1)}, u32[]{:S(2)}, u32[]{:S(2)}) collective-permute-start(bf16[1792,128]{1,0:T(8,128)(2,1)S(1)} %shard_map.54._.refs_1_), channel_id=1, source_target_pairs={{0,1},{1,0},{2,3},{3,2},{4,5},{5,4},{6,7},{7,6},{8,9},{9,8},{10,11... | collective-permute-start | bytes 1376264 | tf_op jit(solution)/shard_map/ppermute | solution.py:86
  46.9 20.6 %collective-permute-start.10 = (bf16[1792,128]{1,0:T(8,128)(2,1)S(1)}, bf16[1792,128]{1,0:T(8,128)(2,1)S(1)}, u32[]{:S(2)}, u32[]{:S(2)}) collective-permute-start(bf16[1792,128]{1,0:T(8,128)(2,1)S(1)} %shard_map.56._.refs_1_), channel_id=1, source_target_pairs={{0,2},{1,3},{2,0},{3,1},{4,6},{5,7},{6,4},{7,5},{8,10},{9,11},{10,... | collective-permute-start | bytes 1376264 | tf_op jit(solution)/shard_map/ppermute | solution.py:86
  47.2 23.2 %collective-permute-start.11 = (bf16[3584,128]{1,0:T(8,128)(2,1)S(1)}, bf16[3584,128]{1,0:T(8,128)(2,1)S(1)}, u32[]{:S(2)}, u32[]{:S(2)}) collective-permute-start(bf16[3584,128]{1,0:T(8,128)(2,1)S(1)} %shard_map.55._.refs_1_), channel_id=1, source_target_pairs={{2,4},{3,5},{4,2},{5,3},{10,12},{11,13},{12,10},{13,11},{18,20},{1... | collective-permute-start | bytes 2752520 | tf_op jit(solution)/shard_map/ppermute | solution.py:86
  48.1 17.1 %collective-permute-start.9 = (bf16[1792,128]{1,0:T(8,128)(2,1)S(1)}, bf16[1792,128]{1,0:T(8,128)(2,1)S(1)}, u32[]{:S(2)}, u32[]{:S(2)}) collective-permute-start(bf16[1792,128]{1,0:T(8,128)(2,1)S(1)} %shard_map.58._.refs_1_), channel_id=1, source_target_pairs={{0,1},{1,0},{2,3},{3,2},{4,5},{5,4},{6,7},{7,6},{8,9},{9,8},{10,11... | collective-permute-start | bytes 1376264 | tf_op jit(solution)/shard_map/ppermute | solution.py:86
  55.3 19.7 %collective-permute-start.12 = (bf16[1792,128]{1,0:T(8,128)(2,1)S(1)}, bf16[1792,128]{1,0:T(8,128)(2,1)S(1)}, u32[]{:S(2)}, u32[]{:S(2)}) collective-permute-start(bf16[1792,128]{1,0:T(8,128)(2,1)S(1)} %shard_map.59._.refs_1_), channel_id=1, source_target_pairs={{0,1},{1,0},{2,3},{3,2},{4,5},{5,4},{6,7},{7,6},{8,9},{9,8},{10,11... | collective-permute-start | bytes 1376264 | tf_op jit(solution)/shard_map/ppermute | solution.py:86
  57.7 34.7 %collective-permute-start.15 = (bf16[1792,128]{1,0:T(8,128)(2,1)S(1)}, bf16[1792,128]{1,0:T(8,128)(2,1)S(1)}, u32[]{:S(2)}, u32[]{:S(2)}) collective-permute-start(bf16[1792,128]{1,0:T(8,128)(2,1)S(1)} %shard_map.60._.refs_1_), channel_id=1, source_target_pairs={{0,2},{1,3},{2,0},{3,1},{4,6},{5,7},{6,4},{7,5},{8,10},{9,11},{10,... | collective-permute-start | bytes 1376264 | tf_op jit(solution)/shard_map/ppermute | solution.py:86
  65.1 44.2 %collective-permute-start.18 = (bf16[3584,128]{1,0:T(8,128)(2,1)S(1)}, bf16[3584,128]{1,0:T(8,128)(2,1)S(1)}, u32[]{:S(2)}, u32[]{:S(2)}) collective-permute-start(bf16[3584,128]{1,0:T(8,128)(2,1)S(1)} %shard_map.61._.refs_1_), channel_id=1, source_target_pairs={{2,4},{3,5},{4,2},{5,3},{10,12},{11,13},{12,10},{13,11},{18,20},{1... | collective-permute-start | bytes 2752520 | tf_op jit(solution)/shard_map/ppermute | solution.py:86
  67.5 19.7 %collective-permute-start.14 = (bf16[1792,128]{1,0:T(8,128)(2,1)S(1)}, bf16[1792,128]{1,0:T(8,128)(2,1)S(1)}, u32[]{:S(2)}, u32[]{:S(2)}) collective-permute-start(bf16[1792,128]{1,0:T(8,128)(2,1)S(1)} %shard_map.62._.refs_1_), channel_id=1, source_target_pairs={{0,2},{1,3},{2,0},{3,1},{4,6},{5,7},{6,4},{7,5},{8,10},{9,11},{10,... | collective-permute-start | bytes 1376264 | tf_op jit(solution)/shard_map/ppermute | solution.py:86
  74.9 21.7 %collective-permute-start.16 = (bf16[1792,128]{1,0:T(8,128)(2,1)S(1)}, bf16[1792,128]{1,0:T(8,128)(2,1)S(1)}, u32[]{:S(2)}, u32[]{:S(2)}) collective-permute-start(bf16[1792,128]{1,0:T(8,128)(2,1)S(1)} %get-tuple-element.83), channel_id=1, source_target_pairs={{2,0},{3,1},{4,6},{5,7},{10,8},{11,9},{12,14},{13,15},{18,16},{19,... | collective-permute-start | bytes 1376264 | tf_op jit(solution)/shard_map/ppermute | solution.py:86
  83.3 31.2 %collective-permute-start.19 = (bf16[1792,128]{1,0:T(8,128)(2,1)S(1)}, bf16[1792,128]{1,0:T(8,128)(2,1)S(1)}, u32[]{:S(2)}, u32[]{:S(2)}) collective-permute-start(bf16[1792,128]{1,0:T(8,128)(2,1)S(1)} %shard_map.66._.refs_1_), channel_id=1, source_target_pairs={{0,4},{1,5},{2,6},{3,7},{4,0},{5,1},{6,2},{7,3},{8,12},{9,13},{10,... | collective-permute-start | bytes 1376264 | tf_op jit(solution)/shard_map/ppermute | solution.py:86
  87.2 31.6 %collective-permute-start.20 = (bf16[1792,128]{1,0:T(8,128)(2,1)S(1)}, bf16[1792,128]{1,0:T(8,128)(2,1)S(1)}, u32[]{:S(2)}, u32[]{:S(2)}) collective-permute-start(bf16[1792,128]{1,0:T(8,128)(2,1)S(1)} %shard_map.67._.refs_1_), channel_id=1, source_target_pairs={{0,2},{1,3},{2,0},{3,1},{4,6},{5,7},{6,4},{7,5},{8,10},{9,11},{10,... | collective-permute-start | bytes 1376264 | tf_op jit(solution)/shard_map/ppermute | solution.py:86
  96.8 22.1 %collective-permute-start.21 = (bf16[1792,128]{1,0:T(8,128)(2,1)S(1)}, bf16[1792,128]{1,0:T(8,128)(2,1)S(1)}, u32[]{:S(2)}, u32[]{:S(2)}) collective-permute-start(bf16[1792,128]{1,0:T(8,128)(2,1)S(1)} %shard_map.70._.refs_1_), channel_id=1, source_target_pairs={{0,1},{1,0},{2,3},{3,2},{4,5},{5,4},{6,7},{7,6},{8,9},{9,8},{10,11... | collective-permute-start | bytes 1376264 | tf_op jit(solution)/shard_map/ppermute | solution.py:86
  107.0 16.2 %collective-permute-start.22 = (bf16[1792,128]{1,0:T(8,128)(2,1)S(1)}, bf16[1792,128]{1,0:T(8,128)(2,1)S(1)}, u32[]{:S(2)}, u32[]{:S(2)}) collective-permute-start(bf16[1792,128]{1,0:T(8,128)(2,1)S(1)} %shard_map.57._.refs_1_), channel_id=1, source_target_pairs={{0,2},{1,3},{6,4},{7,5},{8,10},{9,11},{14,12},{15,13},{16,18},{17,... | collective-permute-start | bytes 1376264 | tf_op jit(solution)/shard_map/ppermute | solution.py:86
  109.4 23.3 %collective-permute-start.24 = (bf16[1792,128]{1,0:T(8,128)(2,1)S(1)}, bf16[1792,128]{1,0:T(8,128)(2,1)S(1)}, u32[]{:S(2)}, u32[]{:S(2)}) collective-permute-start(bf16[1792,128]{1,0:T(8,128)(2,1)S(1)} %shard_map.63._.refs_1_), channel_id=1, source_target_pairs={{0,4},{1,5},{2,6},{3,7},{4,0},{5,1},{6,2},{7,3},{8,12},{9,13},{10,... | collective-permute-start | bytes 1376264 | tf_op jit(solution)/shard_map/ppermute | solution.py:86
  118.8 18.9 %collective-permute-start.26 = (bf16[128,1024]{1,0:T(8,128)(2,1)S(1)}, bf16[128,1024]{1,0:T(8,128)(2,1)S(1)}, u32[]{:S(2)}, u32[]{:S(2)}) collective-permute-start(bf16[128,1024]{1,0:T(8,128)(2,1)S(1)} %get-tuple-element.94), channel_id=1, source_target_pairs={{0,2},{1,3},{2,0},{3,1},{4,6},{5,7},{6,4},{7,5},{8,10},{9,11},{10,... | collective-permute-start | bytes 786440 | tf_op jit(solution)/shard_map/ppermute | solution.py:86
  118.9 27.7 %collective-permute-start.28 = (bf16[1792,128]{1,0:T(8,128)(2,1)S(1)}, bf16[1792,128]{1,0:T(8,128)(2,1)S(1)}, u32[]{:S(2)}, u32[]{:S(2)}) collective-permute-start(bf16[1792,128]{1,0:T(8,128)(2,1)S(1)} %get-tuple-element.98), channel_id=1, source_target_pairs={{2,0},{3,1},{4,6},{5,7},{10,8},{11,9},{12,14},{13,15},{18,16},{19,... | collective-permute-start | bytes 1376264 | tf_op jit(solution)/shard_map/ppermute | solution.py:86
  129.5 20.8 %collective-permute-start.29 = (bf16[3584,128]{1,0:T(8,128)(2,1)S(1)}, bf16[3584,128]{1,0:T(8,128)(2,1)S(1)}, u32[]{:S(2)}, u32[]{:S(2)}) collective-permute-start(bf16[3584,128]{1,0:T(8,128)(2,1)S(1)} %shard_map.76._.refs_1_), channel_id=1, source_target_pairs={{2,4},{3,5},{4,2},{5,3},{10,12},{11,13},{12,10},{13,11},{18,20},{1... | collective-permute-start | bytes 2752520 | tf_op jit(solution)/shard_map/ppermute | solution.py:86
  136.7 29.1 %collective-permute-start.30 = (bf16[128,2048]{1,0:T(8,128)(2,1)S(1)}, bf16[128,2048]{1,0:T(8,128)(2,1)S(1)}, u32[]{:S(2)}, u32[]{:S(2)}) collective-permute-start(bf16[128,2048]{1,0:T(8,128)(2,1)S(1)} %get-tuple-element.101), channel_id=1, source_target_pairs={{0,2},{1,3},{2,0},{3,1},{4,6},{5,7},{6,4},{7,5},{8,10},{9,11},{10,... | collective-permute-start | bytes 1572872 | tf_op jit(solution)/shard_map/ppermute | solution.py:86
  149.3 16.7 %collective-permute-start.31 = (bf16[128,2048]{1,0:T(8,128)(2,1)S(1)}, bf16[128,2048]{1,0:T(8,128)(2,1)S(1)}, u32[]{:S(2)}, u32[]{:S(2)}) collective-permute-start(bf16[128,2048]{1,0:T(8,128)(2,1)S(1)} %get-tuple-element.103), channel_id=1, source_target_pairs={{0,1},{1,0},{2,3},{3,2},{4,5},{5,4},{6,7},{7,6},{8,9},{9,8},{10,11... | collective-permute-start | bytes 1572872 | tf_op jit(solution)/shard_map/ppermute | solution.py:86
  150.7 29.3 %collective-permute-start.32 = (bf16[1792,128]{1,0:T(8,128)(2,1)S(1)}, bf16[1792,128]{1,0:T(8,128)(2,1)S(1)}, u32[]{:S(2)}, u32[]{:S(2)}) collective-permute-start(bf16[1792,128]{1,0:T(8,128)(2,1)S(1)} %get-tuple-element.105), channel_id=1, source_target_pairs={{2,0},{3,1},{4,6},{5,7},{10,8},{11,9},{12,14},{13,15},{18,16},{19,... | collective-permute-start | bytes 1376264 | tf_op jit(solution)/shard_map/ppermute | solution.py:86
  152.2 31.5 %collective-permute-start.33 = (bf16[128,2048]{1,0:T(8,128)(2,1)S(1)}, bf16[128,2048]{1,0:T(8,128)(2,1)S(1)}, u32[]{:S(2)}, u32[]{:S(2)}) collective-permute-start(bf16[128,2048]{1,0:T(8,128)(2,1)S(1)} %get-tuple-element.107), channel_id=1, source_target_pairs={{0,1},{1,0},{2,3},{3,2},{4,5},{5,4},{6,7},{7,6},{8,9},{9,8},{10,11... | collective-permute-start | bytes 1572872 | tf_op jit(solution)/shard_map/ppermute | solution.py:86
  153.4 37.0 %collective-permute-start.37 = (bf16[1792,128]{1,0:T(8,128)(2,1)S(1)}, bf16[1792,128]{1,0:T(8,128)(2,1)S(1)}, u32[]{:S(2)}, u32[]{:S(2)}) collective-permute-start(bf16[1792,128]{1,0:T(8,128)(2,1)S(1)} %shard_map.74._.refs_1_), channel_id=1, source_target_pairs={{0,4},{1,5},{2,6},{3,7},{4,0},{5,1},{6,2},{7,3},{8,12},{9,13},{10,... | collective-permute-start | bytes 1376264 | tf_op jit(solution)/shard_map/ppermute | solution.py:86
  165.9 20.6 %collective-permute-start.35 = (bf16[128,1024]{1,0:T(8,128)(2,1)S(1)}, bf16[128,1024]{1,0:T(8,128)(2,1)S(1)}, u32[]{:S(2)}, u32[]{:S(2)}) collective-permute-start(bf16[128,1024]{1,0:T(8,128)(2,1)S(1)} %get-tuple-element.111), channel_id=1, source_target_pairs={{0,2},{1,3},{2,0},{3,1},{4,6},{5,7},{6,4},{7,5},{8,10},{9,11},{10,... | collective-permute-start | bytes 786440 | tf_op jit(solution)/shard_map/ppermute | solution.py:86
  166.0 23.1 %collective-permute-start.36 = (bf16[128,512]{1,0:T(8,128)(2,1)S(1)}, bf16[128,512]{1,0:T(8,128)(2,1)S(1)}, u32[]{:S(2)}, u32[]{:S(2)}) collective-permute-start(bf16[128,512]{1,0:T(8,128)(2,1)S(1)} %get-tuple-element.113), channel_id=1, source_target_pairs={{0,4},{1,5},{2,6},{3,7},{4,0},{5,1},{6,2},{7,3},{8,12},{9,13},{10,... | collective-permute-start | bytes 393224 | tf_op jit(solution)/shard_map/ppermute | solution.py:86
  186.4 23.5 %collective-permute-start.43 = (bf16[128,512]{1,0:T(8,128)(2,1)S(1)}, bf16[128,512]{1,0:T(8,128)(2,1)S(1)}, u32[]{:S(2)}, u32[]{:S(2)}) collective-permute-start(bf16[128,512]{1,0:T(8,128)(2,1)S(1)} %get-tuple-element.128), channel_id=1, source_target_pairs={{0,4},{1,5},{2,6},{3,7},{4,0},{5,1},{6,2},{7,3},{8,12},{9,13},{10,... | collective-permute-start | bytes 393224 | tf_op jit(solution)/shard_map/ppermute | solution.py:86
  190.4 15.5 %collective-permute-start.41 = (bf16[128,512]{1,0:T(8,128)(2,1)S(1)}, bf16[128,512]{1,0:T(8,128)(2,1)S(1)}, u32[]{:S(2)}, u32[]{:S(2)}) collective-permute-start(bf16[128,512]{1,0:T(8,128)(2,1)S(1)} %get-tuple-element.123), channel_id=1, source_target_pairs={{0,4},{1,5},{2,6},{3,7},{4,0},{5,1},{6,2},{7,3},{8,12},{9,13},{10,... | collective-permute-start | bytes 393224 | tf_op jit(solution)/shard_map/ppermute | solution.py:86
  (26 other events, 305.0 us)

commit v5 on v4

--- a/solution.py
+++ b/solution.py
@@ -112,7 +112,6 @@
 def activate(after, cost, gate, up, first, step):
     units = gate.shape[0]
     gate, up = gate[:, first : first + step], up[:, first : first + step]
-    after = gate if after is None else after
 
     def kernel(gate_ref, up_ref, out_ref):
         for rows in rows_of(units):
@@ -294,7 +293,12 @@
         if stage == 0:
             step = tokens // sum(sizes)
             first = sum(sizes[:chunk])
-            last = activate(last, cost, gate, up, first * step, sizes[chunk] * step)
+            if last is None:
+                part = slice(first * step, (first + sizes[chunk]) * step)
+                g, u = gate[:, part].astype(jnp.float32), up[:, part].astype(jnp.float32)
+                last = (0.5 * g * (1.0 + jnp.tanh(0.5 * g)) * u).astype(jnp.bfloat16)
+            else:
+                last = activate(last, cost, gate, up, first * step, sizes[chunk] * step)
             if stages.count(0) == len(sizes) - 1:
                 gate, up, last = lax.optimization_barrier((gate, up, last))
             state[chunk] = (exchange(last, steps[0]), last)

time: 229 us -> 230 us (level)
  starting transfers between devices: 65.3 us -> 60.8 us
  waiting for transfers between devices: 124 us -> 128 us
    ppermute x51, starting transfers between devices: 65.3 us -> 60.8 us  [exchange(): return lax.ppermute(value, 'tensor', pairs)]
    ppermute x51, waiting for transfers between devices: 124 us -> 128 us  [exchange(): return lax.ppermute(value, 'tensor', pairs)]
    pallas_call x51 -> x50, Pallas kernels: 28.5 us -> 28.3 us  [call(): pl.pallas_call(run, out_shape=[jax.ShapeDtypeStruct(shape, jnp.bfloat16)...]
  transfers between devices with their start and end apart: 51 -> 51, of which waited for: 29 -> 27; matrix products, arithmetic and copies ran while one was open for 1% -> 2% of each run, Pallas kernels for 15% -> 15%
where the time goes in v5:
time: 230 us; the launch traced here: 229 us
  waiting for transfers between devices  128 us (56%)
  starting transfers between devices  60.8 us (26%)
  Pallas kernels  34.9 us (15%)
  local copies, waits for them, and re-layouts  3.61 us (2%)
    ppermute x51, waiting for transfers between devices, exchange(): return lax.ppermute(value, 'tensor', pairs)  128 us
    ppermute x51, starting transfers between devices, exchange(): return lax.ppermute(value, 'tensor', pairs)  60.8 us
    pallas_call x50, Pallas kernels, call(): pl.pallas_call(run, out_shape=[jax.ShapeDtypeStruct(shape, jnp.bfloat16)...  28.3 us
    pallas_call x8, Pallas kernels, add(): pl.pallas_call(kernel, out_shape=[jax.ShapeDtypeStruct((rows, tokens), jn...  6.62 us
  transfers between devices with their start and end apart: 51, of which 27 were waited for; matrix products, arithmetic and copies ran while one was open for 2% of the time, Pallas kernels for 15%

profile of v5, /device:TPU:0, one launch (start us, length us, event | category | flops | bytes accessed | tf_op | source)
XLA Modules:
  0.0 229.3 jit_solution(5397316046791555458)
XLA Ops:
  1.4 4.1 %collective-permute-start.1 = (bf16[1792,128]{1,0:T(8,128)(2,1)S(1)}, bf16[1792,128]{1,0:T(8,128)(2,1)S(1)}, u32[]{:S(2)}, u32[]{:S(2)}) collective-permute-start(bf16[1792,128]{1,0:T(8,128)(2,1)S(1)} %multiply_convert_fusion._.refs_1_), channel_id=1, source_target_pairs={{0,4},{1,5},{2,6},{3,7},{4,0},{5,1},{6,2},{7,3},{8,12},{9,13},{10,... | collective-permute-start | bytes 1376264 | tf_op jit(solution)/shard_map/ppermute | solution.py:86
  5.5 3.6 %fusion = (bf16[1792,128]{1,0:T(8,128)(2,1)S(1)}, bf16[1792,128]{1,0:T(8,128)(2,1)S(1)}, bf16[1792,128]{1,0:T(8,128)(2,1)S(1)}, bf16[1792,128]{1,0:T(8,128)(2,1)...) fusion(bf16[1792,1024]{1,0:T(8,128)(2,1)} %bitcast.14, ...), kind=kLoop, calls=%fused_computation.1 | loop fusion | bytes 12845056 | tf_op jit(solution)/shard_map/slice | solution.py:114
  9.3 3.5 %collective-permute-start.2 = (bf16[1792,128]{1,0:T(8,128)(2,1)S(1)}, bf16[1792,128]{1,0:T(8,128)(2,1)S(1)}, u32[]{:S(2)}, u32[]{:S(2)}) collective-permute-start(bf16[1792,128]{1,0:T(8,128)(2,1)S(1)} %shard_map.46._.refs_1_), channel_id=1, source_target_pairs={{0,2},{1,3},{6,4},{7,5},{8,10},{9,11},{14,12},{15,13},{16,18},{17,... | collective-permute-start | bytes 1376264 | tf_op jit(solution)/shard_map/ppermute | solution.py:86
  16.3 10.4 %collective-permute-done.refs_0_ = bf16[1792,128]{1,0:T(8,128)(2,1)S(1)} collective-permute-done((bf16[1792,128]{1,0:T(8,128)(2,1)S(1)}, bf16[1792,128]{1,0:T(8,128)(2,1)S(1)}, u32[]{:S(2)}, u32[]{:S(2)}) %collective-permute-start) | collective-permute-done | bytes 458784 | tf_op jit(solution)/shard_map/ppermute | solution.py:86
  30.3 16.0 %collective-permute-done.3.refs_0_ = bf16[1792,128]{1,0:T(8,128)(2,1)S(1)} collective-permute-done((bf16[1792,128]{1,0:T(8,128)(2,1)S(1)}, bf16[1792,128]{1,0:T(8,128)(2,1)S(1)}, u32[]{:S(2)}, u32[]{:S(2)}) %collective-permute-start.3) | collective-permute-done | bytes 458784 | tf_op jit(solution)/shard_map/ppermute | solution.py:86
  50.6 5.5 %collective-permute-done.7.refs_0_ = bf16[1792,128]{1,0:T(8,128)(2,1)S(1)} collective-permute-done((bf16[1792,128]{1,0:T(8,128)(2,1)S(1)}, bf16[1792,128]{1,0:T(8,128)(2,1)S(1)}, u32[]{:S(2)}, u32[]{:S(2)}) %collective-permute-start.7) | collective-permute-done | bytes 458784 | tf_op jit(solution)/shard_map/ppermute | solution.py:86
  58.5 2.5 %collective-permute-start.15 = (bf16[1792,128]{1,0:T(8,128)(2,1)S(1)}, bf16[1792,128]{1,0:T(8,128)(2,1)S(1)}, u32[]{:S(2)}, u32[]{:S(2)}) collective-permute-start(bf16[1792,128]{1,0:T(8,128)(2,1)S(1)} %shard_map.59._.refs_1_), channel_id=1, source_target_pairs={{0,2},{1,3},{2,0},{3,1},{4,6},{5,7},{6,4},{7,5},{8,10},{9,11},{10,... | collective-permute-start | bytes 1376264 | tf_op jit(solution)/shard_map/ppermute | solution.py:86
  61.2 4.7 %collective-permute-done.9.refs_0_ = bf16[1792,128]{1,0:T(8,128)(2,1)S(1)} collective-permute-done((bf16[1792,128]{1,0:T(8,128)(2,1)S(1)}, bf16[1792,128]{1,0:T(8,128)(2,1)S(1)}, u32[]{:S(2)}, u32[]{:S(2)}) %collective-permute-start.9) | collective-permute-done | bytes 458784 | tf_op jit(solution)/shard_map/ppermute | solution.py:86
  68.4 2.5 %collective-permute-start.14 = (bf16[1792,128]{1,0:T(8,128)(2,1)S(1)}, bf16[1792,128]{1,0:T(8,128)(2,1)S(1)}, u32[]{:S(2)}, u32[]{:S(2)}) collective-permute-start(bf16[1792,128]{1,0:T(8,128)(2,1)S(1)} %shard_map.61._.refs_1_), channel_id=1, source_target_pairs={{0,2},{1,3},{2,0},{3,1},{4,6},{5,7},{6,4},{7,5},{8,10},{9,11},{10,... | collective-permute-start | bytes 1376264 | tf_op jit(solution)/shard_map/ppermute | solution.py:86
  73.2 2.6 %collective-permute-done.12.refs_0_ = bf16[1792,128]{1,0:T(8,128)(2,1)S(1)} collective-permute-done((bf16[1792,128]{1,0:T(8,128)(2,1)S(1)}, bf16[1792,128]{1,0:T(8,128)(2,1)S(1)}, u32[]{:S(2)}, u32[]{:S(2)}) %collective-permute-start.12) | collective-permute-done | bytes 458784 | tf_op jit(solution)/shard_map/ppermute | solution.py:86
  77.5 6.4 %collective-permute-done.13.refs_0_ = bf16[1792,128]{1,0:T(8,128)(2,1)S(1)} collective-permute-done((bf16[1792,128]{1,0:T(8,128)(2,1)S(1)}, bf16[1792,128]{1,0:T(8,128)(2,1)S(1)}, u32[]{:S(2)}, u32[]{:S(2)}) %collective-permute-start.13) | collective-permute-done | bytes 458784 | tf_op jit(solution)/shard_map/ppermute | solution.py:86
  85.7 2.5 %collective-permute-start.20 = (bf16[1792,128]{1,0:T(8,128)(2,1)S(1)}, bf16[1792,128]{1,0:T(8,128)(2,1)S(1)}, u32[]{:S(2)}, u32[]{:S(2)}) collective-permute-start(bf16[1792,128]{1,0:T(8,128)(2,1)S(1)} %shard_map.66._.refs_1_), channel_id=1, source_target_pairs={{0,2},{1,3},{2,0},{3,1},{4,6},{5,7},{6,4},{7,5},{8,10},{9,11},{10,... | collective-permute-start | bytes 1376264 | tf_op jit(solution)/shard_map/ppermute | solution.py:86
  88.3 2.7 %shard_map.67 = (bf16[128,2048]{1,0:T(8,128)(2,1)S(1)}, bf16[128,2048]{1,0:T(8,128)(2,1)S(1)}) custom-call(bf16[1792,128]{1,0:T(8,128)(2,1)S(1)} %shard_map.66._.refs_1_, bf16[1792,128]{1,0:T(8,128)(2,1)S(1)} %collective-permute-done.14.refs_0_, bf16[1792,128]{1,0:T(8,128)(2,1)S(1)} %shard_map.61._.refs_1_, bf16[448,448]{1,0:T(8,128)(2,1)S(1)} %copy-done, ...), custom_call_target="tpu_custom_call" | custom-call | flops 1 | bytes 1 | tf_op jit(solution)/shard_map/pallas_call | solution.py:97
  92.5 2.7 %shard_map.68 = (bf16[128,2048]{1,0:T(8,128)(2,1)S(1)}, bf16[128,2048]{1,0:T(8,128)(2,1)S(1)}) custom-call(bf16[128,2048]{1,0:T(8,128)(2,1)S(1)} %get-tuple-element.81._.refs_1_, bf16[1792,128]{1,0:T(8,128)(2,1)S(1)} %collective-permute-done.15.refs_0_, bf16[1792,128]{1,0:T(8,128)(2,1)S(1)} %shard_map.59._.refs_1_, bf16[448,448]{1,0:T(8,128)(2,1)S(1)} %copy-done, ...), custom_call_target="tpu_custom_call" | custom-call | flops 2096842624 | bytes 1 | tf_op jit(solution)/shard_map/pallas_call | solution.py:97
  96.0 8.5 %collective-permute-done.17.refs_0_ = bf16[128,2048]{1,0:T(8,128)(2,1)S(1)} collective-permute-done((bf16[128,2048]{1,0:T(8,128)(2,1)S(1)}, bf16[128,2048]{1,0:T(8,128)(2,1)S(1)}, u32[]{:S(2)}, u32[]{:S(2)}) %collective-permute-start.17) | collective-permute-done | bytes 524320 | tf_op jit(solution)/shard_map/ppermute | solution.py:86
  104.5 3.2 %collective-permute-start.22 = (bf16[1792,128]{1,0:T(8,128)(2,1)S(1)}, bf16[1792,128]{1,0:T(8,128)(2,1)S(1)}, u32[]{:S(2)}, u32[]{:S(2)}) collective-permute-start(bf16[1792,128]{1,0:T(8,128)(2,1)S(1)} %shard_map.56._.refs_1_), channel_id=1, source_target_pairs={{0,2},{1,3},{6,4},{7,5},{8,10},{9,11},{14,12},{15,13},{16,18},{17,... | collective-permute-start | bytes 1376264 | tf_op jit(solution)/shard_map/ppermute | solution.py:86
  108.5 8.9 %collective-permute-done.19.refs_0_ = bf16[1792,128]{1,0:T(8,128)(2,1)S(1)} collective-permute-done((bf16[1792,128]{1,0:T(8,128)(2,1)S(1)}, bf16[1792,128]{1,0:T(8,128)(2,1)S(1)}, u32[]{:S(2)}, u32[]{:S(2)}) %collective-permute-start.19) | collective-permute-done | bytes 458784 | tf_op jit(solution)/shard_map/ppermute | solution.py:86
  117.4 2.7 %shard_map.72 = (bf16[128,2048]{1,0:T(8,128)(2,1)S(1)}, bf16[128,2048]{1,0:T(8,128)(2,1)S(1)}) custom-call(bf16[1792,128]{1,0:T(8,128)(2,1)S(1)} %get-tuple-element.86._.refs_1_, bf16[1792,128]{1,0:T(8,128)(2,1)S(1)} %collective-permute-done.19.refs_0_, bf16[1792,128]{1,0:T(8,128)(2,1)S(1)} %shard_map.65._.refs_1_, bf16[448,448]{1,0:T(8,128)(2,1)S(1)} %copy-done, ...), custom_call_target="tpu_custom_call" | custom-call | flops 1 | bytes 1 | tf_op jit(solution)/shard_map/pallas_call | solution.py:97
  123.3 2.7 %shard_map.74 = (bf16[128,2048]{1,0:T(8,128)(2,1)S(1)}, bf16[128,2048]{1,0:T(8,128)(2,1)S(1)}) custom-call(bf16[1792,128]{1,0:T(8,128)(2,1)S(1)} %shard_map.73._.refs_1_, bf16[1792,128]{1,0:T(8,128)(2,1)S(1)} %collective-permute-done.21.refs_0_, bf16[1792,128]{1,0:T(8,128)(2,1)S(1)} %shard_map.69._.refs_1_, bf16[448,448]{1,0:T(8,128)(2,1)S(1)} %copy-done, ...), custom_call_target="tpu_custom_call" | custom-call | flops 8387370496 | bytes 1 | tf_op jit(solution)/shard_map/pallas_call | solution.py:97
  126.9 2.5 %collective-permute-done.23.refs_0_ = bf16[128,2048]{1,0:T(8,128)(2,1)S(1)} collective-permute-done((bf16[128,2048]{1,0:T(8,128)(2,1)S(1)}, bf16[128,2048]{1,0:T(8,128)(2,1)S(1)}, u32[]{:S(2)}, u32[]{:S(2)}) %collective-permute-start.23) | collective-permute-done | bytes 524320 | tf_op jit(solution)/shard_map/ppermute | solution.py:86
  132.6 2.7 %shard_map.77 = (bf16[128,2048]{1,0:T(8,128)(2,1)S(1)}, bf16[128,2048]{1,0:T(8,128)(2,1)S(1)}) custom-call(bf16[128,1024]{1,0:T(8,128)(2,1)S(1)} %get-tuple-element.90._.refs_1_, bf16[1792,128]{1,0:T(8,128)(2,1)S(1)} %collective-permute-done.24.refs_0_, bf16[1792,128]{1,0:T(8,128)(2,1)S(1)} %shard_map.62._.refs_1_, bf16[448,448]{1,0:T(8,128)(2,1)S(1)} %copy-done, ...), custom_call_target="tpu_custom_call" | custom-call | flops 4193685248 | bytes 1 | tf_op jit(solution)/shard_map/pallas_call | solution.py:97
  135.3 2.6 %collective-permute-start.30 = (bf16[128,2048]{1,0:T(8,128)(2,1)S(1)}, bf16[128,2048]{1,0:T(8,128)(2,1)S(1)}, u32[]{:S(2)}, u32[]{:S(2)}) collective-permute-start(bf16[128,2048]{1,0:T(8,128)(2,1)S(1)} %get-tuple-element.101), channel_id=1, source_target_pairs={{0,2},{1,3},{2,0},{3,1},{4,6},{5,7},{6,4},{7,5},{8,10},{9,11},{10,... | collective-permute-start | bytes 1572872 | tf_op jit(solution)/shard_map/ppermute | solution.py:86
  138.2 10.1 %collective-permute-done.27.refs_0_ = bf16[128,1024]{1,0:T(8,128)(2,1)S(1)} collective-permute-done((bf16[128,1024]{1,0:T(8,128)(2,1)S(1)}, bf16[128,1024]{1,0:T(8,128)(2,1)S(1)}, u32[]{:S(2)}, u32[]{:S(2)}) %collective-permute-start.27) | collective-permute-done | bytes 262176 | tf_op jit(solution)/shard_map/ppermute | solution.py:86
  148.4 2.7 %shard_map.81 = (bf16[128,2048]{1,0:T(8,128)(2,1)S(1)}, bf16[128,2048]{1,0:T(8,128)(2,1)S(1)}) custom-call(bf16[128,512]{1,0:T(8,128)(2,1)S(1)} %get-tuple-element.97._.kept_ref, bf16[1792,128]{1,0:T(8,128)(2,1)S(1)} %collective-permute-done.28.refs_0_, bf16[1792,128]{1,0:T(8,128)(2,1)S(1)} %get-tuple-element.86._.refs_1_, bf16[448,448]{1,0:T(8,128)(2,1)S(1)} %copy-done, ...), custom_call_target="tpu_custom_call" | custom-call | flops 1048421312 | bytes 1 | tf_op jit(solution)/shard_map/pallas_call | solution.py:97
  155.2 3.3 %collective-permute-start.37 = (bf16[1792,128]{1,0:T(8,128)(2,1)S(1)}, bf16[1792,128]{1,0:T(8,128)(2,1)S(1)}, u32[]{:S(2)}, u32[]{:S(2)}) collective-permute-start(bf16[1792,128]{1,0:T(8,128)(2,1)S(1)} %shard_map.73._.refs_1_), channel_id=1, source_target_pairs={{0,4},{1,5},{2,6},{3,7},{4,0},{5,1},{6,2},{7,3},{8,12},{9,13},{10,... | collective-permute-start | bytes 1376264 | tf_op jit(solution)/shard_map/ppermute | solution.py:86
  158.5 9.3 %collective-permute-done.30.refs_0_ = bf16[128,2048]{1,0:T(8,128)(2,1)S(1)} collective-permute-done((bf16[128,2048]{1,0:T(8,128)(2,1)S(1)}, bf16[128,2048]{1,0:T(8,128)(2,1)S(1)}, u32[]{:S(2)}, u32[]{:S(2)}) %collective-permute-start.30) | collective-permute-done | bytes 524320 | tf_op jit(solution)/shard_map/ppermute | solution.py:86
  168.2 14.4 %collective-permute-done.32.refs_0_ = bf16[1792,128]{1,0:T(8,128)(2,1)S(1)} collective-permute-done((bf16[1792,128]{1,0:T(8,128)(2,1)S(1)}, bf16[1792,128]{1,0:T(8,128)(2,1)S(1)}, u32[]{:S(2)}, u32[]{:S(2)}) %collective-permute-start.32) | collective-permute-done | bytes 458784 | tf_op jit(solution)/shard_map/ppermute | solution.py:86
  183.0 2.7 %shard_map.85 = (bf16[128,2048]{1,0:T(8,128)(2,1)S(1)}, bf16[128,2048]{1,0:T(8,128)(2,1)S(1)}) custom-call(bf16[128,1024]{1,0:T(8,128)(2,1)S(1)} %get-tuple-element.104._.refs_1_, bf16[1792,128]{1,0:T(8,128)(2,1)S(1)} %collective-permute-done.32.refs_0_, bf16[1792,128]{1,0:T(8,128)(2,1)S(1)} %get-tuple-element.100._.refs_1_, bf16[448,448]{1,0:T(8,128)(2,1)S(1)} %copy-done, ...), custom_call_target="tpu_custom_call" | custom-call | flops 2096842624 | bytes 1 | tf_op jit(solution)/shard_map/pallas_call | solution.py:97
  187.4 3.3 %collective-permute-done.34.refs_0_ = bf16[128,1024]{1,0:T(8,128)(2,1)S(1)} collective-permute-done((bf16[128,1024]{1,0:T(8,128)(2,1)S(1)}, bf16[128,1024]{1,0:T(8,128)(2,1)S(1)}, u32[]{:S(2)}, u32[]{:S(2)}) %collective-permute-start.34) | collective-permute-done | bytes 262176 | tf_op jit(solution)/shard_map/ppermute | solution.py:86
  196.3 2.7 %shard_map.90 = (bf16[128,2048]{1,0:T(8,128)(2,1)S(1)}, bf16[128,2048]{1,0:T(8,128)(2,1)S(1)}) custom-call(bf16[16,128]{1,0:T(8,128)(2,1)S(1)} %get-tuple-element.114._, bf16[1792,128]{1,0:T(8,128)(2,1)S(1)} %collective-permute-done.37.refs_0_, bf16[1792,128]{1,0:T(8,128)(2,1)S(1)} %shard_map.73._.refs_1_, bf16[448,448]{1,0:T(8,128)(2,1)S(1)} %copy-done, ...), custom_call_target="tpu_custom_call" | custom-call | flops 4193685248 | bytes 1 | tf_op jit(solution)/shard_map/pallas_call | solution.py:97
  200.3 6.3 %collective-permute-done.39.refs_0_ = bf16[128,1024]{1,0:T(8,128)(2,1)S(1)} collective-permute-done((bf16[128,1024]{1,0:T(8,128)(2,1)S(1)}, bf16[128,1024]{1,0:T(8,128)(2,1)S(1)}, u32[]{:S(2)}, u32[]{:S(2)}) %collective-permute-start.39) | collective-permute-done | bytes 262176 | tf_op jit(solution)/shard_map/ppermute | solution.py:86
  215.5 3.3 %collective-permute-done.45.refs_0_ = bf16[128,1024]{1,0:T(8,128)(2,1)S(1)} collective-permute-done((bf16[128,1024]{1,0:T(8,128)(2,1)S(1)}, bf16[128,1024]{1,0:T(8,128)(2,1)S(1)}, u32[]{:S(2)}, u32[]{:S(2)}) %collective-permute-start.45) | collective-permute-done | bytes 262176 | tf_op jit(solution)/shard_map/ppermute | solution.py:86
  (141 shorter events, 66.9 us)
Async XLA Ops:
  1.4 26.1 %collective-permute-start.1 = (bf16[1792,128]{1,0:T(8,128)(2,1)S(1)}, bf16[1792,128]{1,0:T(8,128)(2,1)S(1)}, u32[]{:S(2)}, u32[]{:S(2)}) collective-permute-start(bf16[1792,128]{1,0:T(8,128)(2,1)S(1)} %multiply_convert_fusion._.refs_1_), channel_id=1, source_target_pairs={{0,4},{1,5},{2,6},{3,7},{4,0},{5,1},{6,2},{7,3},{8,12},{9,13},{10,... | collective-permute-start | bytes 1376264 | tf_op jit(solution)/shard_map/ppermute | solution.py:86
  9.3 20.6 %collective-permute-start.2 = (bf16[1792,128]{1,0:T(8,128)(2,1)S(1)}, bf16[1792,128]{1,0:T(8,128)(2,1)S(1)}, u32[]{:S(2)}, u32[]{:S(2)}) collective-permute-start(bf16[1792,128]{1,0:T(8,128)(2,1)S(1)} %shard_map.46._.refs_1_), channel_id=1, source_target_pairs={{0,2},{1,3},{6,4},{7,5},{8,10},{9,11},{14,12},{15,13},{16,18},{17,... | collective-permute-start | bytes 1376264 | tf_op jit(solution)/shard_map/ppermute | solution.py:86
  15.1 32.6 %collective-permute-start.4 = (bf16[1792,128]{1,0:T(8,128)(2,1)S(1)}, bf16[1792,128]{1,0:T(8,128)(2,1)S(1)}, u32[]{:S(2)}, u32[]{:S(2)}) collective-permute-start(bf16[1792,128]{1,0:T(8,128)(2,1)S(1)} %shard_map.49._.refs_1_), channel_id=1, source_target_pairs={{0,1},{1,0},{2,3},{3,2},{4,5},{5,4},{6,7},{7,6},{8,9},{9,8},{10,11... | collective-permute-start | bytes 1376264 | tf_op jit(solution)/shard_map/ppermute | solution.py:86
  15.9 32.0 %collective-permute-start.5 = (bf16[1792,128]{1,0:T(8,128)(2,1)S(1)}, bf16[1792,128]{1,0:T(8,128)(2,1)S(1)}, u32[]{:S(2)}, u32[]{:S(2)}) collective-permute-start(bf16[1792,128]{1,0:T(8,128)(2,1)S(1)} %shard_map.50._.refs_1_), channel_id=1, source_target_pairs={{0,4},{1,5},{2,6},{3,7},{4,0},{5,1},{6,2},{7,3},{8,12},{9,13},{10,... | collective-permute-start | bytes 1376264 | tf_op jit(solution)/shard_map/ppermute | solution.py:86
  26.6 22.3 %collective-permute-start.6 = (bf16[1792,128]{1,0:T(8,128)(2,1)S(1)}, bf16[1792,128]{1,0:T(8,128)(2,1)S(1)}, u32[]{:S(2)}, u32[]{:S(2)}) collective-permute-start(bf16[1792,128]{1,0:T(8,128)(2,1)S(1)} %shard_map.48._.refs_1_), channel_id=1, source_target_pairs={{0,2},{1,3},{2,0},{3,1},{4,6},{5,7},{6,4},{7,5},{8,10},{9,11},{10,... | collective-permute-start | bytes 1376264 | tf_op jit(solution)/shard_map/ppermute | solution.py:86
  27.5 18.8 %collective-permute-start.3 = (bf16[1792,128]{1,0:T(8,128)(2,1)S(1)}, bf16[1792,128]{1,0:T(8,128)(2,1)S(1)}, u32[]{:S(2)}, u32[]{:S(2)}) collective-permute-start(bf16[1792,128]{1,0:T(8,128)(2,1)S(1)} %shard_map.51._.refs_1_), channel_id=1, source_target_pairs={{0,1},{1,0},{2,3},{3,2},{4,5},{5,4},{6,7},{7,6},{8,9},{9,8},{10,11... | collective-permute-start | bytes 1376264 | tf_op jit(solution)/shard_map/ppermute | solution.py:86
  30.0 26.2 %collective-permute-start.7 = (bf16[1792,128]{1,0:T(8,128)(2,1)S(1)}, bf16[1792,128]{1,0:T(8,128)(2,1)S(1)}, u32[]{:S(2)}, u32[]{:S(2)}) collective-permute-start(bf16[1792,128]{1,0:T(8,128)(2,1)S(1)} %shard_map.53._.refs_1_), channel_id=1, source_target_pairs={{0,1},{1,0},{2,3},{3,2},{4,5},{5,4},{6,7},{7,6},{8,9},{9,8},{10,11... | collective-permute-start | bytes 1376264 | tf_op jit(solution)/shard_map/ppermute | solution.py:86
  47.8 20.6 %collective-permute-start.10 = (bf16[1792,128]{1,0:T(8,128)(2,1)S(1)}, bf16[1792,128]{1,0:T(8,128)(2,1)S(1)}, u32[]{:S(2)}, u32[]{:S(2)}) collective-permute-start(bf16[1792,128]{1,0:T(8,128)(2,1)S(1)} %shard_map.55._.refs_1_), channel_id=1, source_target_pairs={{0,2},{1,3},{2,0},{3,1},{4,6},{5,7},{6,4},{7,5},{8,10},{9,11},{10,... | collective-permute-start | bytes 1376264 | tf_op jit(solution)/shard_map/ppermute | solution.py:86
  48.0 23.2 %collective-permute-start.11 = (bf16[3584,128]{1,0:T(8,128)(2,1)S(1)}, bf16[3584,128]{1,0:T(8,128)(2,1)S(1)}, u32[]{:S(2)}, u32[]{:S(2)}) collective-permute-start(bf16[3584,128]{1,0:T(8,128)(2,1)S(1)} %shard_map.54._.refs_1_), channel_id=1, source_target_pairs={{2,4},{3,5},{4,2},{5,3},{10,12},{11,13},{12,10},{13,11},{18,20},{1... | collective-permute-start | bytes 2752520 | tf_op jit(solution)/shard_map/ppermute | solution.py:86
  48.9 17.1 %collective-permute-start.9 = (bf16[1792,128]{1,0:T(8,128)(2,1)S(1)}, bf16[1792,128]{1,0:T(8,128)(2,1)S(1)}, u32[]{:S(2)}, u32[]{:S(2)}) collective-permute-start(bf16[1792,128]{1,0:T(8,128)(2,1)S(1)} %shard_map.57._.refs_1_), channel_id=1, source_target_pairs={{0,1},{1,0},{2,3},{3,2},{4,5},{5,4},{6,7},{7,6},{8,9},{9,8},{10,11... | collective-permute-start | bytes 1376264 | tf_op jit(solution)/shard_map/ppermute | solution.py:86
  56.1 19.7 %collective-permute-start.12 = (bf16[1792,128]{1,0:T(8,128)(2,1)S(1)}, bf16[1792,128]{1,0:T(8,128)(2,1)S(1)}, u32[]{:S(2)}, u32[]{:S(2)}) collective-permute-start(bf16[1792,128]{1,0:T(8,128)(2,1)S(1)} %shard_map.58._.refs_1_), channel_id=1, source_target_pairs={{0,1},{1,0},{2,3},{3,2},{4,5},{5,4},{6,7},{7,6},{8,9},{9,8},{10,11... | collective-permute-start | bytes 1376264 | tf_op jit(solution)/shard_map/ppermute | solution.py:86
  58.5 32.4 %collective-permute-start.15 = (bf16[1792,128]{1,0:T(8,128)(2,1)S(1)}, bf16[1792,128]{1,0:T(8,128)(2,1)S(1)}, u32[]{:S(2)}, u32[]{:S(2)}) collective-permute-start(bf16[1792,128]{1,0:T(8,128)(2,1)S(1)} %shard_map.59._.refs_1_), channel_id=1, source_target_pairs={{0,2},{1,3},{2,0},{3,1},{4,6},{5,7},{6,4},{7,5},{8,10},{9,11},{10,... | collective-permute-start | bytes 1376264 | tf_op jit(solution)/shard_map/ppermute | solution.py:86
  65.9 41.8 %collective-permute-start.18 = (bf16[3584,128]{1,0:T(8,128)(2,1)S(1)}, bf16[3584,128]{1,0:T(8,128)(2,1)S(1)}, u32[]{:S(2)}, u32[]{:S(2)}) collective-permute-start(bf16[3584,128]{1,0:T(8,128)(2,1)S(1)} %shard_map.60._.refs_1_), channel_id=1, source_target_pairs={{2,4},{3,5},{4,2},{5,3},{10,12},{11,13},{12,10},{13,11},{18,20},{1... | collective-permute-start | bytes 2752520 | tf_op jit(solution)/shard_map/ppermute | solution.py:86
  68.4 17.4 %collective-permute-start.14 = (bf16[1792,128]{1,0:T(8,128)(2,1)S(1)}, bf16[1792,128]{1,0:T(8,128)(2,1)S(1)}, u32[]{:S(2)}, u32[]{:S(2)}) collective-permute-start(bf16[1792,128]{1,0:T(8,128)(2,1)S(1)} %shard_map.61._.refs_1_), channel_id=1, source_target_pairs={{0,2},{1,3},{2,0},{3,1},{4,6},{5,7},{6,4},{7,5},{8,10},{9,11},{10,... | collective-permute-start | bytes 1376264 | tf_op jit(solution)/shard_map/ppermute | solution.py:86
  75.8 19.5 %collective-permute-start.16 = (bf16[1792,128]{1,0:T(8,128)(2,1)S(1)}, bf16[1792,128]{1,0:T(8,128)(2,1)S(1)}, u32[]{:S(2)}, u32[]{:S(2)}) collective-permute-start(bf16[1792,128]{1,0:T(8,128)(2,1)S(1)} %get-tuple-element.83), channel_id=1, source_target_pairs={{2,0},{3,1},{4,6},{5,7},{10,8},{11,9},{12,14},{13,15},{18,16},{19,... | collective-permute-start | bytes 1376264 | tf_op jit(solution)/shard_map/ppermute | solution.py:86
  83.8 33.5 %collective-permute-start.19 = (bf16[1792,128]{1,0:T(8,128)(2,1)S(1)}, bf16[1792,128]{1,0:T(8,128)(2,1)S(1)}, u32[]{:S(2)}, u32[]{:S(2)}) collective-permute-start(bf16[1792,128]{1,0:T(8,128)(2,1)S(1)} %shard_map.65._.refs_1_), channel_id=1, source_target_pairs={{0,4},{1,5},{2,6},{3,7},{4,0},{5,1},{6,2},{7,3},{8,12},{9,13},{10,... | collective-permute-start | bytes 1376264 | tf_op jit(solution)/shard_map/ppermute | solution.py:86
  85.7 35.9 %collective-permute-start.20 = (bf16[1792,128]{1,0:T(8,128)(2,1)S(1)}, bf16[1792,128]{1,0:T(8,128)(2,1)S(1)}, u32[]{:S(2)}, u32[]{:S(2)}) collective-permute-start(bf16[1792,128]{1,0:T(8,128)(2,1)S(1)} %shard_map.66._.refs_1_), channel_id=1, source_target_pairs={{0,2},{1,3},{2,0},{3,1},{4,6},{5,7},{6,4},{7,5},{8,10},{9,11},{10,... | collective-permute-start | bytes 1376264 | tf_op jit(solution)/shard_map/ppermute | solution.py:86
  95.4 26.4 %collective-permute-start.21 = (bf16[1792,128]{1,0:T(8,128)(2,1)S(1)}, bf16[1792,128]{1,0:T(8,128)(2,1)S(1)}, u32[]{:S(2)}, u32[]{:S(2)}) collective-permute-start(bf16[1792,128]{1,0:T(8,128)(2,1)S(1)} %shard_map.69._.refs_1_), channel_id=1, source_target_pairs={{0,1},{1,0},{2,3},{3,2},{4,5},{5,4},{6,7},{7,6},{8,9},{9,8},{10,11... | collective-permute-start | bytes 1376264 | tf_op jit(solution)/shard_map/ppermute | solution.py:86
  104.5 21.6 %collective-permute-start.22 = (bf16[1792,128]{1,0:T(8,128)(2,1)S(1)}, bf16[1792,128]{1,0:T(8,128)(2,1)S(1)}, u32[]{:S(2)}, u32[]{:S(2)}) collective-permute-start(bf16[1792,128]{1,0:T(8,128)(2,1)S(1)} %shard_map.56._.refs_1_), channel_id=1, source_target_pairs={{0,2},{1,3},{6,4},{7,5},{8,10},{9,11},{14,12},{15,13},{16,18},{17,... | collective-permute-start | bytes 1376264 | tf_op jit(solution)/shard_map/ppermute | solution.py:86
  107.8 24.8 %collective-permute-start.24 = (bf16[1792,128]{1,0:T(8,128)(2,1)S(1)}, bf16[1792,128]{1,0:T(8,128)(2,1)S(1)}, u32[]{:S(2)}, u32[]{:S(2)}) collective-permute-start(bf16[1792,128]{1,0:T(8,128)(2,1)S(1)} %shard_map.62._.refs_1_), channel_id=1, source_target_pairs={{0,4},{1,5},{2,6},{3,7},{4,0},{5,1},{6,2},{7,3},{8,12},{9,13},{10,... | collective-permute-start | bytes 1376264 | tf_op jit(solution)/shard_map/ppermute | solution.py:86
  121.6 16.4 %collective-permute-start.26 = (bf16[128,1024]{1,0:T(8,128)(2,1)S(1)}, bf16[128,1024]{1,0:T(8,128)(2,1)S(1)}, u32[]{:S(2)}, u32[]{:S(2)}) collective-permute-start(bf16[128,1024]{1,0:T(8,128)(2,1)S(1)} %get-tuple-element.94), channel_id=1, source_target_pairs={{0,2},{1,3},{2,0},{3,1},{4,6},{5,7},{6,4},{7,5},{8,10},{9,11},{10,... | collective-permute-start | bytes 786440 | tf_op jit(solution)/shard_map/ppermute | solution.py:86
  121.8 26.6 %collective-permute-start.28 = (bf16[1792,128]{1,0:T(8,128)(2,1)S(1)}, bf16[1792,128]{1,0:T(8,128)(2,1)S(1)}, u32[]{:S(2)}, u32[]{:S(2)}) collective-permute-start(bf16[1792,128]{1,0:T(8,128)(2,1)S(1)} %get-tuple-element.98), channel_id=1, source_target_pairs={{2,0},{3,1},{4,6},{5,7},{10,8},{11,9},{12,14},{13,15},{18,16},{19,... | collective-permute-start | bytes 1376264 | tf_op jit(solution)/shard_map/ppermute | solution.py:86
  129.3 21.8 %collective-permute-start.29 = (bf16[3584,128]{1,0:T(8,128)(2,1)S(1)}, bf16[3584,128]{1,0:T(8,128)(2,1)S(1)}, u32[]{:S(2)}, u32[]{:S(2)}) collective-permute-start(bf16[3584,128]{1,0:T(8,128)(2,1)S(1)} %shard_map.75._.refs_1_), channel_id=1, source_target_pairs={{2,4},{3,5},{4,2},{5,3},{10,12},{11,13},{12,10},{13,11},{18,20},{1... | collective-permute-start | bytes 2752520 | tf_op jit(solution)/shard_map/ppermute | solution.py:86
  132.6 15.7 %collective-permute-start.27 = (bf16[128,1024]{1,0:T(8,128)(2,1)S(1)}, bf16[128,1024]{1,0:T(8,128)(2,1)S(1)}, u32[]{:S(2)}, u32[]{:S(2)}) collective-permute-start(bf16[128,1024]{1,0:T(8,128)(2,1)S(1)} %get-tuple-element.96), channel_id=1, source_target_pairs={{0,2},{1,3},{2,0},{3,1},{4,6},{5,7},{6,4},{7,5},{8,10},{9,11},{10,... | collective-permute-start | bytes 786440 | tf_op jit(solution)/shard_map/ppermute | solution.py:86
  135.3 32.5 %collective-permute-start.30 = (bf16[128,2048]{1,0:T(8,128)(2,1)S(1)}, bf16[128,2048]{1,0:T(8,128)(2,1)S(1)}, u32[]{:S(2)}, u32[]{:S(2)}) collective-permute-start(bf16[128,2048]{1,0:T(8,128)(2,1)S(1)} %get-tuple-element.101), channel_id=1, source_target_pairs={{0,2},{1,3},{2,0},{3,1},{4,6},{5,7},{6,4},{7,5},{8,10},{9,11},{10,... | collective-permute-start | bytes 1572872 | tf_op jit(solution)/shard_map/ppermute | solution.py:86
  151.1 16.9 %collective-permute-start.31 = (bf16[128,2048]{1,0:T(8,128)(2,1)S(1)}, bf16[128,2048]{1,0:T(8,128)(2,1)S(1)}, u32[]{:S(2)}, u32[]{:S(2)}) collective-permute-start(bf16[128,2048]{1,0:T(8,128)(2,1)S(1)} %get-tuple-element.103), channel_id=1, source_target_pairs={{0,1},{1,0},{2,3},{3,2},{4,5},{5,4},{6,7},{7,6},{8,9},{9,8},{10,11... | collective-permute-start | bytes 1572872 | tf_op jit(solution)/shard_map/ppermute | solution.py:86
  151.6 31.0 %collective-permute-start.32 = (bf16[1792,128]{1,0:T(8,128)(2,1)S(1)}, bf16[1792,128]{1,0:T(8,128)(2,1)S(1)}, u32[]{:S(2)}, u32[]{:S(2)}) collective-permute-start(bf16[1792,128]{1,0:T(8,128)(2,1)S(1)} %get-tuple-element.105), channel_id=1, source_target_pairs={{2,0},{3,1},{4,6},{5,7},{10,8},{11,9},{12,14},{13,15},{18,16},{19,... | collective-permute-start | bytes 1376264 | tf_op jit(solution)/shard_map/ppermute | solution.py:86
  153.1 32.6 %collective-permute-start.33 = (bf16[128,2048]{1,0:T(8,128)(2,1)S(1)}, bf16[128,2048]{1,0:T(8,128)(2,1)S(1)}, u32[]{:S(2)}, u32[]{:S(2)}) collective-permute-start(bf16[128,2048]{1,0:T(8,128)(2,1)S(1)} %get-tuple-element.107), channel_id=1, source_target_pairs={{0,1},{1,0},{2,3},{3,2},{4,5},{5,4},{6,7},{7,6},{8,9},{9,8},{10,11... | collective-permute-start | bytes 1572872 | tf_op jit(solution)/shard_map/ppermute | solution.py:86
  155.2 40.1 %collective-permute-start.37 = (bf16[1792,128]{1,0:T(8,128)(2,1)S(1)}, bf16[1792,128]{1,0:T(8,128)(2,1)S(1)}, u32[]{:S(2)}, u32[]{:S(2)}) collective-permute-start(bf16[1792,128]{1,0:T(8,128)(2,1)S(1)} %shard_map.73._.refs_1_), channel_id=1, source_target_pairs={{0,4},{1,5},{2,6},{3,7},{4,0},{5,1},{6,2},{7,3},{8,12},{9,13},{10,... | collective-permute-start | bytes 1376264 | tf_op jit(solution)/shard_map/ppermute | solution.py:86
  167.8 23.0 %collective-permute-start.35 = (bf16[128,1024]{1,0:T(8,128)(2,1)S(1)}, bf16[128,1024]{1,0:T(8,128)(2,1)S(1)}, u32[]{:S(2)}, u32[]{:S(2)}) collective-permute-start(bf16[128,1024]{1,0:T(8,128)(2,1)S(1)} %get-tuple-element.111), channel_id=1, source_target_pairs={{0,2},{1,3},{2,0},{3,1},{4,6},{5,7},{6,4},{7,5},{8,10},{9,11},{10,... | collective-permute-start | bytes 786440 | tf_op jit(solution)/shard_map/ppermute | solution.py:86
  167.9 24.5 %collective-permute-start.36 = (bf16[128,512]{1,0:T(8,128)(2,1)S(1)}, bf16[128,512]{1,0:T(8,128)(2,1)S(1)}, u32[]{:S(2)}, u32[]{:S(2)}) collective-permute-start(bf16[128,512]{1,0:T(8,128)(2,1)S(1)} %get-tuple-element.113), channel_id=1, source_target_pairs={{0,4},{1,5},{2,6},{3,7},{4,0},{5,1},{6,2},{7,3},{8,12},{9,13},{10,... | collective-permute-start | bytes 393224 | tf_op jit(solution)/shard_map/ppermute | solution.py:86
  190.8 22.6 %collective-permute-start.43 = (bf16[128,512]{1,0:T(8,128)(2,1)S(1)}, bf16[128,512]{1,0:T(8,128)(2,1)S(1)}, u32[]{:S(2)}, u32[]{:S(2)}) collective-permute-start(bf16[128,512]{1,0:T(8,128)(2,1)S(1)} %get-tuple-element.128), channel_id=1, source_target_pairs={{0,4},{1,5},{2,6},{3,7},{4,0},{5,1},{6,2},{7,3},{8,12},{9,13},{10,... | collective-permute-start | bytes 393224 | tf_op jit(solution)/shard_map/ppermute | solution.py:86
  (24 other events, 268.1 us)
